TPU v7x, 32 devices: a whole 2x2x4 slice. The times are simulated.
32 devices in a mesh: src: 2 (over y), tp: 8 (over z, x), row: 2 (over core).
Axes of the slice: x: 2, y: 2, z: 4, core: 2. Of those that a mesh axis runs over, the one named last changes fastest.
Arguments:
- tokens: bfloat16 [2, 256, 8192], P('src', 'tp', 'row'), may hold values from -6 to 6
- coefficients: float32 [2, 2], replicated, may hold values from -2 to 2
- gate_weights: bfloat16 [2, 8192, 4096], P('src', 'row', 'tp'), may hold values from -0.0625 to 0.0625
- up_weights: bfloat16 [2, 8192, 4096], P('src', 'row', 'tp'), may hold values from -0.0625 to 0.0625
Outputs:
- hidden: bfloat16 [2, 256, 4096], P('src', 'row', 'tp')
All inputs are finite; a program needn't handle non-finite values.
Results may differ from a plain program's by a relative error of at most 0.0013.
Values may be sent and summed in bfloat16 or wider, within the bound.
No kernel may reach another device: no remote copies, remote signals or barrier semaphores. Data moves between devices by JAX's collectives and lax.ppermute only.
A program may use at most 64 MiB of HBM per device.

v0:
```python
import jax
import jax.numpy as jnp
from jax import lax
from jax.sharding import PartitionSpec as P


def shards(tokens, coefficients, gate_weights, up_weights):
    local_rows = tokens.shape[1]
    half_width = tokens.shape[2]
    candidates = coefficients.shape[0]
    sources = coefficients.shape[1]
    per_candidate = local_rows * lax.axis_size("tp")
    out_rows = per_candidate // lax.axis_size("row")
    own_source = lax.axis_index("src")
    picked = (jnp.arange(sources, dtype=jnp.int32) == own_source).astype(jnp.float32)
    own_factors = jnp.sum(coefficients * picked[None, :], axis=1)
    gate_local = gate_weights[0]
    up_local = up_weights[0]
    hidden_width = gate_local.shape[1]
    flat_tokens = tokens.reshape(local_rows, half_width)
    row_block = lax.all_gather(flat_tokens, ("src", "tp"), axis=0, tiled=True)
    row_count = row_block.shape[0]
    owner_ids = jnp.arange(row_count, dtype=jnp.int32) // per_candidate
    one_hot = (owner_ids[:, None] == jnp.arange(candidates, dtype=jnp.int32)[None, :]).astype(
        jnp.float32
    )
    factor = jnp.sum(one_hot * own_factors[None, :], axis=1)[:, None]
    gate_part = jnp.dot(row_block, gate_local, preferred_element_type=jnp.float32)
    up_part = jnp.dot(row_block, up_local, preferred_element_type=jnp.float32)
    collected = jnp.concatenate((gate_part, up_part), axis=1) * factor
    summed = lax.psum_scatter(collected, ("src", "row"), scatter_dimension=0, tiled=True)
    hidden = (jax.nn.silu(summed[:, :hidden_width]) * summed[:, hidden_width:]).astype(jnp.bfloat16)
    return hidden.reshape(1, out_rows, hidden_width)


def solution(mesh):
    return jax.shard_map(
        shards,
        mesh=mesh,
        in_specs=(P("src", "tp", "row"), P(), P("src", "row", "tp"), P("src", "row", "tp")),
        out_specs=P("src", "row", "tp"),
        check_vma=False,
    )
```

profile of v0, /device:TPU:0, one launch (start us, length us, event | category | flops | bytes accessed | tf_op | source)
XLA Modules:
  0.0 137.7 jit_solution(3341342688443781198)
XLA Ops:
  6.5 0.0 all-gather.3.cloned.1.call-start
  6.5 0.7 all-gather.3.cloned.1.call-update
  7.3 0.0 reduce-scatter.2.cloned.1.call-start
  7.3 0.8 multiply_reduce_fusion
  8.1 0.1 fusion.8
  8.2 80.6 %all-gather.3.cloned.1.call-done = bf16[1,512,4096]{2,1,0:T(8,128)(2,1)} async-done(((bf16[1,32,4096]{2,1,0:T(8,128)(2,1)}), bf16[1,512,4096]{2,1,0:T(8,128)(2,1)}) %all-gather.3.cloned.1.call-update) | async-done | bytes 4194320 | tf_op jit(solution)/shard_map/all_gather | solution.py:21
  88.8 0.0 copy-start
  88.8 0.0 copy-start.1
  88.8 6.0 %fusion = f32[512,512]{0,1:T(8,128)S(1)} fusion(bf16[1,4096,512]{2,1,0:T(8,128)(2,1)} %param.7, bf16[1,512,4096]{2,1,0:T(8,128)(2,1)} %all-gather.3.cloned.1.call-done), kind=kOutput, calls=%fused_computation | convolution fusion | flops 2147483648 | bytes 9437184 | tf_op jit(solution)/shard_map/dot_general | solution.py:29
  94.8 0.0 copy-done
  94.8 0.0 copy-done.1
  94.8 2.4 %fusion.2 = f32[512,512]{0,1:T(8,128)S(1)} fusion(bf16[1,4096,512]{2,1,0:T(8,128)(2,1)S(1)} %copy-done, bf16[1,512,4096]{2,1,0:T(8,128)(2,1)S(1)} %copy-done.1), kind=kOutput, calls=%fused_computation.2 | convolution fusion | flops 2147483648 | bytes 9437184 | tf_op jit(solution)/shard_map/dot_general | solution.py:28
  97.2 1.6 %maximum_multiply_fusion = f32[512,1024]{0,1:T(8,128)} fusion(f32[512,512]{0,1:T(8,128)S(1)} %fusion, f32[512,512]{0,1:T(8,128)S(1)} %fusion.2, f32[512]{0:T(512)S(1)} %fusion.8), kind=kLoop, calls=%fused_computation.6 | loop fusion | flops 1048576 | bytes 4196352 | tf_op jit(solution)/shard_map/mul | solution.py:30
  98.8 0.0 reduce-scatter.2.cloned.1.call-update
  98.8 30.2 %reduce-scatter.2.cloned.1.call-done = f32[128,1024]{0,1:T(8,128)} async-done(((f32[512,1024]{0,1:T(8,128)}), f32[128,1024]{0,1:T(8,128)}) %reduce-scatter.2.cloned.1.call-update) | async-done | bytes 524304 | tf_op jit(solution)/shard_map/reduce_scatter | solution.py:31
  129.0 1.1 fusion.7
  130.1 0.8 copy.6
  (2 shorter events, 0.0 us)
Async XLA Ops:
  6.5 82.3 %all-gather.3.cloned.1.call-start = ((), (), s32[]{:S(2)}) async-start(), calls=%async_computation.2 | async-start | bytes 4456448 | tf_op jit(solution)/shard_map/all_gather | solution.py:21
  7.3 121.7 %reduce-scatter.2.cloned.1.call-start = ((), (), s32[]{:S(2)}) async-start(), calls=%async_computation.1 | async-start | bytes 2621440 | tf_op jit(solution)/shard_map/reduce_scatter | solution.py:31
  88.8 6.0 %copy-start = (bf16[1,4096,512]{2,1,0:T(8,128)(2,1)S(1)}, bf16[1,4096,512]{2,1,0:T(8,128)(2,1)}, u32[]{:S(2)}) copy-start(bf16[1,4096,512]{2,1,0:T(8,128)(2,1)} %param.6) | copy-start | bytes 12582916
  88.8 6.0 %copy-start.1 = (bf16[1,512,4096]{2,1,0:T(8,128)(2,1)S(1)}, bf16[1,512,4096]{2,1,0:T(8,128)(2,1)}, u32[]{:S(2)}) copy-start(bf16[1,512,4096]{2,1,0:T(8,128)(2,1)} %all-gather.3.cloned.1.call-done) | copy-start | bytes 12582916
Sparse Core Ops, SparseCore 0:
  10.2 78.5 all-gather.2
  98.9 30.0 reduce-scatter.1
where the time goes:
time: 138 us
  waiting for transfers between devices  112 us (81%)
  between operations  13.5 us (10%)
  matrix products  8.33 us (6%)
  other arithmetic  3.59 us (3%)
    all_gather x1, waiting for transfers between devices, shards(): row_block = lax.all_gather(flat_tokens, ('src', 'tp'), axis=0, tiled=True)  80.6 us
    reduce_scatter x1, waiting for transfers between devices, shards(): lax.psum_scatter(collected, ('src', 'row'), scatter_dimension=0, tiled=True)  30.2 us
    dot_general x1, matrix products, shards(): up_part = jnp.dot(row_block, up_local, preferred_element_type=jnp.float32)  5.97 us
  transfers between devices with their start and end apart: 2, of which 2 were waited for; matrix products, arithmetic and copies ran while one was open for 1% of the time, Pallas kernels for 0%

commit v1 on v0

--- a/solution.py
+++ b/solution.py
@@ -1,10 +1,14 @@
 import jax
 import jax.numpy as jnp
 from jax import lax
+from jax.experimental import pallas as pl
+from jax.experimental.pallas import tpu as pltpu
 from jax.sharding import PartitionSpec as P
 
+AXES = ("src", "tp", "row")
 
-def shards(tokens, coefficients, gate_weights, up_weights):
+
+def gathered(tokens, coefficients, gate_weights, up_weights):
     local_rows = tokens.shape[1]
     half_width = tokens.shape[2]
     candidates = coefficients.shape[0]
@@ -19,8 +23,7 @@
     hidden_width = gate_local.shape[1]
     flat_tokens = tokens.reshape(local_rows, half_width)
     row_block = lax.all_gather(flat_tokens, ("src", "tp"), axis=0, tiled=True)
-    row_count = row_block.shape[0]
-    owner_ids = jnp.arange(row_count, dtype=jnp.int32) // per_candidate
+    owner_ids = jnp.arange(row_block.shape[0], dtype=jnp.int32) // per_candidate
     one_hot = (owner_ids[:, None] == jnp.arange(candidates, dtype=jnp.int32)[None, :]).astype(
         jnp.float32
     )
@@ -33,9 +36,131 @@
     return hidden.reshape(1, out_rows, hidden_width)
 
 
+def products(blocks, factors, gate_weights, up_weights):
+    count = len(blocks)
+    rows, depth = blocks[0].shape
+    width = gate_weights.shape[2]
+    step = min(depth, 1024)
+
+    def kernel(*refs):
+        scale, block_refs = refs[0], refs[1 : count + 1]
+        gate, up, out = refs[count + 1 :]
+        lhs = jnp.concatenate([ref[...] for ref in block_refs], axis=0)
+        first = pl.program_id(0) == 0
+        last = pl.program_id(0) == pl.num_programs(0) - 1
+        for start, weights in ((0, gate), (width, up)):
+            part = jnp.dot(lhs, weights[0], preferred_element_type=jnp.float32)
+            columns = slice(start, start + width)
+
+            @pl.when(first)
+            def _():
+                out[:, columns] = part
+
+            @pl.when(jnp.logical_not(first))
+            def _():
+                out[:, columns] += part
+
+        @pl.when(last)
+        def _():
+            for i in range(count):
+                span = slice(i * rows, (i + 1) * rows)
+                out[span, :] = out[span, :] * scale[i]
+
+    return pl.pallas_call(
+        kernel,
+        grid=(depth // step,),
+        out_shape=jax.ShapeDtypeStruct((count * rows, 2 * width), jnp.float32),
+        in_specs=[pl.BlockSpec(memory_space=pltpu.SMEM)]
+        + [pl.BlockSpec((rows, step), lambda k: (0, k))] * count
+        + [pl.BlockSpec((1, step, width), lambda k: (0, k, 0))] * 2,
+        out_specs=pl.BlockSpec((count * rows, 2 * width), lambda k: (0, 0)),
+        compiler_params=pltpu.CompilerParams(vmem_limit_bytes=24 * 2**20),
+        cost_estimate=pl.CostEstimate(
+            flops=4 * count * rows * depth * width,
+            bytes_accessed=4 * depth * width + 2 * count * rows * depth,
+            transcendentals=0,
+        ),
+    )(jnp.stack(factors), *blocks, gate_weights, up_weights)
+
+
+def paired(mesh):
+    tp = mesh.shape["tp"]
+    levels = tp // 2
+    half = levels // 2
+
+    def place(src, z, x, row):
+        return (src * tp + z * 2 + x) * 2 + row
+
+    every = [(s, z, x, r) for s in range(2) for z in range(levels) for x in range(2) for r in range(2)]
+
+    def swap(array, src=0, z=0, x=0):
+        pairs = [(place(*at), place(at[0] ^ src, at[1] ^ z, at[2] ^ x, at[3])) for at in every]
+        return lax.ppermute(array, AXES, pairs)
+
+    def to_owner(array, far):
+        pairs = [
+            (place(s, z, x, r), place(s, z, x, r ^ 1)) for s, z, x, r in every if (r == z // half) == far
+        ]
+        return lax.ppermute(array, AXES, pairs)
+
+    def owner_src(array, far):
+        pairs = [
+            (place(s, z, x, r), place(s ^ 1, z, x, r)) for s, z, x, r in every if (r == z // half) != far
+        ]
+        return lax.ppermute(array, AXES, pairs)
+
+    def shards(tokens, coefficients, gate_weights, up_weights):
+        rows = tokens.shape[1]
+        own_src, own_tp, own_row = (lax.axis_index(name) for name in AXES)
+        picked = jnp.where(own_src == 0, coefficients[:, 0], coefficients[:, 1])
+        own_factor = jnp.where(own_src == 0, picked[0], picked[1])
+        other_factor = jnp.where(own_src == 0, picked[1], picked[0])
+
+        b0 = tokens[0]
+        z1 = swap(b0, z=1)
+        x0 = swap(b0, x=1)
+        y0 = swap(b0, src=1)
+        z2 = swap(b0, z=2)
+        z3 = swap(b0, z=3)
+        y1, x1 = swap(z1, src=1), swap(z1, x=1)
+        d0 = swap(y0, x=1)
+        d1 = swap(d0, z=1)
+        y2, x2 = swap(z2, src=1), swap(z2, x=1)
+        d2 = swap(d0, z=2)
+        y3, x3 = swap(z3, src=1), swap(z3, x=1)
+        d3 = swap(d2, z=1)
+
+        own4 = [own_factor] * 4
+        other4 = [other_factor] * 4
+        near = products(
+            [y0, d0, y1, d1, b0, x0, z1, x1], other4 + own4, gate_weights, up_weights
+        )
+        near = near + to_owner(near, False)
+        split = 4 * rows
+        near_other = owner_src(near[:split], False)
+        far_other = products([y2, d2, y3, d3], other4, gate_weights, up_weights)
+        far_other = far_other + to_owner(far_other, True)
+        far_other = owner_src(far_other, True)
+        far_own = products([z2, x2, z3, x3], own4, gate_weights, up_weights)
+        far_sum = far_own + to_owner(far_own, True) + far_other
+        near_sum = near[split:] + near_other
+
+        keeps_near = own_row == own_tp // 2 // half
+        total = jnp.where(keeps_near, near_sum, far_sum)
+        width = gate_weights.shape[2]
+        hidden = (jax.nn.silu(total[:, :width]) * total[:, width:]).astype(jnp.bfloat16)
+        hidden = hidden.reshape(2, 2, rows, width)
+        hidden = jnp.where(own_tp % 2 == 0, hidden, hidden[:, ::-1])
+        hidden = jnp.where(own_tp // 2 % 2 == 0, hidden, hidden[::-1])
+        return hidden.reshape(1, 4 * rows, width)
+
+    return shards
+
+
 def solution(mesh):
+    fits = mesh.shape["src"] == 2 and mesh.shape["tp"] == 8 and mesh.shape["row"] == 2
     return jax.shard_map(
-        shards,
+        paired(mesh) if fits else gathered,
         mesh=mesh,
         in_specs=(P("src", "tp", "row"), P(), P("src", "row", "tp"), P("src", "row", "tp")),
         out_specs=P("src", "row", "tp"),

time: 138 us -> 97.9 us (0.71)
  waiting for transfers between devices: 112 us -> 42.2 us
  starting transfers between devices: 0.04 us -> 31.5 us
  Pallas kernels: 0 us -> 11.6 us
  between operations: 13.5 us -> 2.88 us
  matrix products: 8.33 us -> 0 us
  local copies, waits for them, and re-layouts: 0.78 us -> 6.06 us
    all_gather x1 -> x0, waiting for transfers between devices: 80.6 us -> none  [shards(): row_block = lax.all_gather(flat_tokens, ('src', 'tp'), axis=0, tiled=True)]
    ppermute x0 -> x20, waiting for transfers between devices: none -> 42.2 us  [the longest x15 32.7 us: swap(): return lax.ppermute(array, AXES, pairs)]
    ppermute x0 -> x20, starting transfers between devices: none -> 31.5 us  [the longest x15 22.4 us: swap(): return lax.ppermute(array, AXES, pairs)]
    reduce_scatter x1 -> x0, waiting for transfers between devices: 30.2 us -> none  [shards(): lax.psum_scatter(collected, ('src', 'row'), scatter_dimension=0, tiled=True)]
    pallas_call x0 -> x3, Pallas kernels: none -> 11.6 us  [products(): pl.pallas_call(kernel, grid=(depth // step,), out_shape=jax.ShapeDtypeStr...]
    dot_general x2 -> x0, matrix products: 8.33 us -> none  [the longest x1 5.97 us: shards(): up_part = jnp.dot(row_block, up_local, preferred_element_type=jnp.float32)]
    unnamed x4 -> x10, local copies, waits for them, and re-layouts: 0.01 us -> 5.33 us
    select_n x1 -> x4, other arithmetic: 0.01 us -> 2.95 us  [the longest x1 1.41 us: shards(): total = jnp.where(keeps_near, near_sum, far_sum)]
  transfers between devices with their start and end apart: 2 -> 20, of which waited for: 2 -> 9; matrix products, arithmetic and copies ran while one was open for 1% -> 2% of each run, Pallas kernels for 0% -> 12%
where the time goes in v1:
time: 97.9 us; the launch traced here: 97.5 us
  waiting for transfers between devices  42.2 us (43%)
  starting transfers between devices  31.5 us (32%)
  Pallas kernels  11.6 us (12%)
  local copies, waits for them, and re-layouts  6.06 us (6%)
  other arithmetic  3.24 us (3%)
  between operations  2.88 us (3%)
    ppermute x15, waiting for transfers between devices, swap(): return lax.ppermute(array, AXES, pairs)  32.7 us
    ppermute x15, starting transfers between devices, swap(): return lax.ppermute(array, AXES, pairs)  22.4 us
    pallas_call x3, Pallas kernels, products(): pl.pallas_call(kernel, grid=(depth // step,), out_shape=jax.ShapeDtypeStr...  11.6 us
    ppermute x2, waiting for transfers between devices, owner_src(): return lax.ppermute(array, AXES, pairs)  9.49 us
    unnamed x10, local copies, waits for them, and re-layouts  5.33 us
    ppermute x3, starting transfers between devices, to_owner(): return lax.ppermute(array, AXES, pairs)  4.66 us
    ppermute x2, starting transfers between devices, owner_src(): return lax.ppermute(array, AXES, pairs)  4.46 us
  transfers between devices with their start and end apart: 20, of which 9 were waited for; matrix products, arithmetic and copies ran while one was open for 2% of the time, Pallas kernels for 12%

profile of v1, /device:TPU:0, one launch (start us, length us, event | category | flops | bytes accessed | tf_op | source)
XLA Modules:
  0.0 97.5 jit_solution(6733669865468608954)
XLA Ops:
  0.0 3.0 %collective-permute-start = (bf16[32,4096]{1,0:T(8,128)(2,1)}, bf16[32,4096]{1,0:T(8,128)(2,1)S(1)}, u32[]{:S(2)}, u32[]{:S(2)}) collective-permute-start(bf16[32,4096]{1,0:T(8,128)(2,1)} %bitcast.7), channel_id=1, source_target_pairs={{0,16},{1,17},{2,18},{3,19},{4,20},{5,21},{6,22},{7,23},{8,24},{9,... | collective-permute-start | bytes 786440 | tf_op jit(solution)/shard_map/ppermute | solution.py:98
  3.0 1.6 %collective-permute-start.2 = (bf16[32,4096]{1,0:T(8,128)(2,1)}, bf16[32,4096]{1,0:T(8,128)(2,1)S(1)}, u32[]{:S(2)}, u32[]{:S(2)}) collective-permute-start(bf16[32,4096]{1,0:T(8,128)(2,1)} %bitcast.8), channel_id=1, source_target_pairs={{0,4},{1,5},{2,6},{3,7},{4,0},{5,1},{6,2},{7,3},{8,12},{9,13},{10,... | collective-permute-start | bytes 786440 | tf_op jit(solution)/shard_map/ppermute | solution.py:98
  4.5 4.9 %collective-permute-done.refs_1_ = bf16[32,4096]{1,0:T(8,128)(2,1)S(1)} collective-permute-done((bf16[32,4096]{1,0:T(8,128)(2,1)}, bf16[32,4096]{1,0:T(8,128)(2,1)S(1)}, u32[]{:S(2)}, u32[]{:S(2)}) %collective-permute-start) | collective-permute-done | bytes 262176 | tf_op jit(solution)/shard_map/ppermute | solution.py:98
  9.5 1.7 %collective-permute-start.1 = (bf16[32,4096]{1,0:T(8,128)(2,1)S(1)}, bf16[32,4096]{1,0:T(8,128)(2,1)S(1)}, u32[]{:S(2)}, u32[]{:S(2)}) collective-permute-start(bf16[32,4096]{1,0:T(8,128)(2,1)S(1)} %collective-permute-done.refs_1_), channel_id=1, source_target_pairs={{0,2},{1,3},{2,0},{3,1},{4,6},{5,7},{6,4},{7,5},{8,10},{9,11},{10,... | collective-permute-start | bytes 786440 | tf_op jit(solution)/shard_map/ppermute | solution.py:98
  11.2 0.3 collective-permute-start.5
  11.5 2.8 %collective-permute-start.9 = (bf16[32,4096]{1,0:T(8,128)(2,1)}, bf16[32,4096]{1,0:T(8,128)(2,1)S(1)}, u32[]{:S(2)}, u32[]{:S(2)}) collective-permute-start(bf16[32,4096]{1,0:T(8,128)(2,1)} %bitcast.10), channel_id=1, source_target_pairs={{0,8},{1,9},{2,10},{3,11},{4,12},{5,13},{6,14},{7,15},{8,0},{9,1},... | collective-permute-start | bytes 786440 | tf_op jit(solution)/shard_map/ppermute | solution.py:98
  14.3 0.0 collective-permute-done.2.refs_7_
  14.3 1.5 %collective-permute-start.3 = (bf16[32,4096]{1,0:T(8,128)(2,1)S(1)}, bf16[32,4096]{1,0:T(8,128)(2,1)S(1)}, u32[]{:S(2)}, u32[]{:S(2)}) collective-permute-start(bf16[32,4096]{1,0:T(8,128)(2,1)S(1)} %collective-permute-done.2.refs_7_), channel_id=1, source_target_pairs={{0,16},{1,17},{2,18},{3,19},{4,20},{5,21},{6,22},{7,23},{8,24},{9,... | collective-permute-start | bytes 786440 | tf_op jit(solution)/shard_map/ppermute | solution.py:98
  15.8 1.5 %collective-permute-start.6 = (bf16[32,4096]{1,0:T(8,128)(2,1)S(1)}, bf16[32,4096]{1,0:T(8,128)(2,1)S(1)}, u32[]{:S(2)}, u32[]{:S(2)}) collective-permute-start(bf16[32,4096]{1,0:T(8,128)(2,1)S(1)} %collective-permute-done.2.refs_7_), channel_id=1, source_target_pairs={{0,2},{1,3},{2,0},{3,1},{4,6},{5,7},{6,4},{7,5},{8,10},{9,11},{10,... | collective-permute-start | bytes 786440 | tf_op jit(solution)/shard_map/ppermute | solution.py:98
  17.3 1.4 %collective-permute-done.1.refs_2_ = bf16[32,4096]{1,0:T(8,128)(2,1)S(1)} collective-permute-done((bf16[32,4096]{1,0:T(8,128)(2,1)S(1)}, bf16[32,4096]{1,0:T(8,128)(2,1)S(1)}, u32[]{:S(2)}, u32[]{:S(2)}) %collective-permute-start.1) | collective-permute-done | bytes 262176 | tf_op jit(solution)/shard_map/ppermute | solution.py:98
  18.7 1.8 %collective-permute-start.4 = (bf16[32,4096]{1,0:T(8,128)(2,1)S(1)}, bf16[32,4096]{1,0:T(8,128)(2,1)S(1)}, u32[]{:S(2)}, u32[]{:S(2)}) collective-permute-start(bf16[32,4096]{1,0:T(8,128)(2,1)S(1)} %collective-permute-done.1.refs_2_), channel_id=1, source_target_pairs={{0,4},{1,5},{2,6},{3,7},{4,0},{5,1},{6,2},{7,3},{8,12},{9,13},{10,... | collective-permute-start | bytes 786440 | tf_op jit(solution)/shard_map/ppermute | solution.py:98
  20.5 0.8 slice_select_fusion
  21.4 0.6 fusion.2
  24.6 0.1 stack.12.refs_0_
  24.7 3.4 %collective-permute-start.11 = (bf16[32,4096]{1,0:T(8,128)(2,1)}, bf16[32,4096]{1,0:T(8,128)(2,1)S(1)}, u32[]{:S(2)}, u32[]{:S(2)}) collective-permute-start(bf16[32,4096]{1,0:T(8,128)(2,1)} %bitcast.11), channel_id=1, source_target_pairs={{0,12},{1,13},{2,14},{3,15},{4,8},{5,9},{6,10},{7,11},{8,4},{9,5},... | collective-permute-start | bytes 786440 | tf_op jit(solution)/shard_map/ppermute | solution.py:98
  28.2 0.0 collective-permute-done.3.refs_3_
  28.2 0.0 collective-permute-start.15
  28.2 0.0 collective-permute-done.6.refs_8_
  28.2 3.2 %collective-permute-done.4.refs_4_ = bf16[32,4096]{1,0:T(8,128)(2,1)S(1)} collective-permute-done((bf16[32,4096]{1,0:T(8,128)(2,1)S(1)}, bf16[32,4096]{1,0:T(8,128)(2,1)S(1)}, u32[]{:S(2)}, u32[]{:S(2)}) %collective-permute-start.4) | collective-permute-done | bytes 262176 | tf_op jit(solution)/shard_map/ppermute | solution.py:98
  31.4 2.2 %copy-done = bf16[1,4096,512]{2,1,0:T(8,128)(2,1)S(1)} copy-done((bf16[1,4096,512]{2,1,0:T(8,128)(2,1)S(1)}, bf16[1,4096,512]{2,1,0:T(8,128)(2,1)}, u32[]{:S(2)}) %copy-start) | copy-done | bytes 4194328
  33.6 2.2 %copy-done.2 = bf16[1,4096,512]{2,1,0:T(8,128)(2,1)S(1)} copy-done((bf16[1,4096,512]{2,1,0:T(8,128)(2,1)S(1)}, bf16[1,4096,512]{2,1,0:T(8,128)(2,1)}, u32[]{:S(2)}) %copy-start.2) | copy-done | bytes 4194328
  35.8 0.9 copy-done.4
  36.7 4.8 %shard_map.46 = f32[256,1024]{1,0:T(8,128)S(1)} custom-call(f32[8]{0:T(128)S(1)} %stack.12.refs_0_, bf16[32,4096]{1,0:T(8,128)(2,1)S(1)} %collective-permute-done.refs_1_, bf16[32,4096]{1,0:T(8,128)(2,1)S(1)} %collective-permute-done.1.refs_2_, bf16[32,4096]{1,0:T(8,128)(2,1)S(1)} %collective-permute-done.3.refs_3_, ...), custom_call_target="tpu_custom_call" | custom-call | flops 2147483648 | bytes 10485760 | tf_op jit(solution)/shard_map/pallas_call | solution.py:69
  41.5 1.3 %collective-permute-start.7 = (f32[256,1024]{1,0:T(8,128)S(1)}, f32[256,1024]{1,0:T(8,128)S(1)}, u32[]{:S(2)}, u32[]{:S(2)}) collective-permute-start(f32[256,1024]{1,0:T(8,128)S(1)} %shard_map.46), channel_id=1, source_target_pairs={{1,0},{3,2},{5,4},{7,6},{8,9},{10,11},{12,13},{14,15},{17,16},{19,... | collective-permute-start | bytes 3145736 | tf_op jit(solution)/shard_map/ppermute | solution.py:104
  42.8 0.0 collective-permute-done.9.refs_1_
  42.8 1.1 %collective-permute-start.14 = (bf16[32,4096]{1,0:T(8,128)(2,1)S(1)}, bf16[32,4096]{1,0:T(8,128)(2,1)S(1)}, u32[]{:S(2)}, u32[]{:S(2)}) collective-permute-start(bf16[32,4096]{1,0:T(8,128)(2,1)S(1)} %collective-permute-done.9.refs_1_), channel_id=1, source_target_pairs={{0,16},{1,17},{2,18},{3,19},{4,20},{5,21},{6,22},{7,23},{8,24},{9,... | collective-permute-start | bytes 786440 | tf_op jit(solution)/shard_map/ppermute | solution.py:98
  43.9 0.0 collective-permute-done.11.refs_3_
  43.9 0.9 collective-permute-start.16
  44.9 2.8 %collective-permute-done.15.refs_2_ = bf16[32,4096]{1,0:T(8,128)(2,1)S(1)} collective-permute-done((bf16[32,4096]{1,0:T(8,128)(2,1)S(1)}, bf16[32,4096]{1,0:T(8,128)(2,1)S(1)}, u32[]{:S(2)}, u32[]{:S(2)}) %collective-permute-start.15) | collective-permute-done | bytes 262176 | tf_op jit(solution)/shard_map/ppermute | solution.py:98
  47.7 0.6 collective-permute-start.17
  48.3 3.6 %collective-permute-done.14.refs_1_ = bf16[32,4096]{1,0:T(8,128)(2,1)S(1)} collective-permute-done((bf16[32,4096]{1,0:T(8,128)(2,1)S(1)}, bf16[32,4096]{1,0:T(8,128)(2,1)S(1)}, u32[]{:S(2)}, u32[]{:S(2)}) %collective-permute-start.14) | collective-permute-done | bytes 262176 | tf_op jit(solution)/shard_map/ppermute | solution.py:98
  51.8 5.6 %collective-permute-done.16.refs_3_ = bf16[32,4096]{1,0:T(8,128)(2,1)S(1)} collective-permute-done((bf16[32,4096]{1,0:T(8,128)(2,1)S(1)}, bf16[32,4096]{1,0:T(8,128)(2,1)S(1)}, u32[]{:S(2)}, u32[]{:S(2)}) %collective-permute-start.16) | collective-permute-done | bytes 262176 | tf_op jit(solution)/shard_map/ppermute | solution.py:98
  57.5 3.4 %shard_map.48 = f32[128,1024]{1,0:T(8,128)S(1)} custom-call(f32[4]{0:T(128)S(1)} %stack.14.refs_0_, bf16[32,4096]{1,0:T(8,128)(2,1)S(1)} %collective-permute-done.14.refs_1_, bf16[32,4096]{1,0:T(8,128)(2,1)S(1)} %collective-permute-done.15.refs_2_, bf16[32,4096]{1,0:T(8,128)(2,1)S(1)} %collective-permute-done.16.refs_3_, ...), custom_call_target="tpu_custom_call" | custom-call | flops 1073741824 | bytes 9437184 | tf_op jit(solution)/shard_map/pallas_call | solution.py:69
  60.9 2.0 %collective-permute-start.18 = (f32[128,1024]{1,0:T(8,128)S(1)}, f32[128,1024]{1,0:T(8,128)S(1)}, u32[]{:S(2)}, u32[]{:S(2)}) collective-permute-start(f32[128,1024]{1,0:T(8,128)S(1)} %shard_map.48), channel_id=1, source_target_pairs={{0,1},{2,3},{4,5},{6,7},{9,8},{11,10},{13,12},{15,14},{16,17},{18,... | collective-permute-start | bytes 1572872 | tf_op jit(solution)/shard_map/ppermute | solution.py:104
  63.0 1.1 %collective-permute-start.10 = (bf16[32,4096]{1,0:T(8,128)(2,1)S(1)}, bf16[32,4096]{1,0:T(8,128)(2,1)S(1)}, u32[]{:S(2)}, u32[]{:S(2)}) collective-permute-start(bf16[32,4096]{1,0:T(8,128)(2,1)S(1)} %collective-permute-done.9.refs_1_), channel_id=1, source_target_pairs={{0,2},{1,3},{2,0},{3,1},{4,6},{5,7},{6,4},{7,5},{8,10},{9,11},{10,... | collective-permute-start | bytes 786440 | tf_op jit(solution)/shard_map/ppermute | solution.py:98
  64.1 1.0 collective-permute-start.12
  65.0 7.2 %collective-permute-done.10.refs_2_ = bf16[32,4096]{1,0:T(8,128)(2,1)S(1)} collective-permute-done((bf16[32,4096]{1,0:T(8,128)(2,1)S(1)}, bf16[32,4096]{1,0:T(8,128)(2,1)S(1)}, u32[]{:S(2)}, u32[]{:S(2)}) %collective-permute-start.10) | collective-permute-done | bytes 262176 | tf_op jit(solution)/shard_map/ppermute | solution.py:98
  72.3 3.9 %collective-permute-done.12.refs_4_ = bf16[32,4096]{1,0:T(8,128)(2,1)S(1)} collective-permute-done((bf16[32,4096]{1,0:T(8,128)(2,1)S(1)}, bf16[32,4096]{1,0:T(8,128)(2,1)S(1)}, u32[]{:S(2)}, u32[]{:S(2)}) %collective-permute-start.12) | collective-permute-done | bytes 262176 | tf_op jit(solution)/shard_map/ppermute | solution.py:98
  76.2 3.4 %shard_map.47 = f32[128,1024]{1,0:T(8,128)S(1)} custom-call(f32[4]{0:T(128)S(1)} %stack.13.refs_0_, bf16[32,4096]{1,0:T(8,128)(2,1)S(1)} %collective-permute-done.9.refs_1_, bf16[32,4096]{1,0:T(8,128)(2,1)S(1)} %collective-permute-done.10.refs_2_, bf16[32,4096]{1,0:T(8,128)(2,1)S(1)} %collective-permute-done.11.refs_3_, ...), custom_call_target="tpu_custom_call" | custom-call | flops 1073741824 | bytes 9437184 | tf_op jit(solution)/shard_map/pallas_call | solution.py:69
  79.6 1.3 %collective-permute-start.13 = (f32[128,1024]{1,0:T(8,128)S(1)}, f32[128,1024]{1,0:T(8,128)S(1)}, u32[]{:S(2)}, u32[]{:S(2)}) collective-permute-start(f32[128,1024]{1,0:T(8,128)S(1)} %shard_map.47), channel_id=1, source_target_pairs={{0,1},{2,3},{4,5},{6,7},{9,8},{11,10},{13,12},{15,14},{16,17},{18,... | collective-permute-start | bytes 1572872 | tf_op jit(solution)/shard_map/ppermute | solution.py:104
  81.0 0.1 add.33
  81.0 1.5 %collective-permute-start.19 = (f32[128,1024]{1,0:T(8,128)S(1)}, f32[128,1024]{1,0:T(8,128)}, u32[]{:S(2)}, u32[]{:S(2)}) collective-permute-start(f32[128,1024]{1,0:T(8,128)S(1)} %add.33), channel_id=1, source_target_pairs={{1,17},{3,19},{5,21},{7,23},{8,24},{10,26},{12,28},{14,30},{17,1},... | collective-permute-start | bytes 1572872 | tf_op jit(solution)/shard_map/ppermute | solution.py:110
  82.5 0.1 add.30
  82.7 3.0 %collective-permute-start.8 = (f32[128,1024]{1,0:T(8,128)S(1)}, f32[128,1024]{1,0:T(8,128)}, u32[]{:S(2)}, u32[]{:S(2)}) collective-permute-start(f32[128,1024]{1,0:T(8,128)S(1)} %slice.37), channel_id=1, source_target_pairs={{0,16},{2,18},{4,20},{6,22},{9,25},{11,27},{13,29},{15,31},{16,0},... | collective-permute-start | bytes 1572872 | tf_op jit(solution)/shard_map/ppermute | solution.py:110
  85.8 9.5 %collective-permute-done.8 = f32[128,1024]{1,0:T(8,128)} collective-permute-done((f32[128,1024]{1,0:T(8,128)S(1)}, f32[128,1024]{1,0:T(8,128)}, u32[]{:S(2)}, u32[]{:S(2)}) %collective-permute-start.8) | collective-permute-done | bytes 524320 | tf_op jit(solution)/shard_map/ppermute | solution.py:110
  95.3 1.4 %fusion = f32[128,1024]{1,0:T(8,128)S(1)} fusion(f32[128,1024]{1,0:T(8,128)} %collective-permute-done.8, f32[256,1024]{1,0:T(8,128)S(1)} %add.30, f32[128,1024]{1,0:T(8,128)} %collective-permute-done.19, f32[128,1024]{1,0:T(8,128)S(1)} %shard_map.47, f32[128,1024]{1,0:T(8,128)S(1)} %collective-permute-done.13, pred[]{:T(512)S(6)} %eq.19), kind=kLoop, calls=%fused_computation.1 | loop fusion | flops 524288 | bytes 3145729 | tf_op jit(solution)/shard_map/jit(_where)/select_n | solution.py:149
  96.7 0.1 fusion.1
  96.8 0.7 reverse_select_fusion
  (17 shorter events, 0.1 us)
Async XLA Ops:
  0.0 9.5 %collective-permute-start = (bf16[32,4096]{1,0:T(8,128)(2,1)}, bf16[32,4096]{1,0:T(8,128)(2,1)S(1)}, u32[]{:S(2)}, u32[]{:S(2)}) collective-permute-start(bf16[32,4096]{1,0:T(8,128)(2,1)} %bitcast.7), channel_id=1, source_target_pairs={{0,16},{1,17},{2,18},{3,19},{4,20},{5,21},{6,22},{7,23},{8,24},{9,... | collective-permute-start | bytes 786440 | tf_op jit(solution)/shard_map/ppermute | solution.py:98
  3.0 11.4 %collective-permute-start.2 = (bf16[32,4096]{1,0:T(8,128)(2,1)}, bf16[32,4096]{1,0:T(8,128)(2,1)S(1)}, u32[]{:S(2)}, u32[]{:S(2)}) collective-permute-start(bf16[32,4096]{1,0:T(8,128)(2,1)} %bitcast.8), channel_id=1, source_target_pairs={{0,4},{1,5},{2,6},{3,7},{4,0},{5,1},{6,2},{7,3},{8,12},{9,13},{10,... | collective-permute-start | bytes 786440 | tf_op jit(solution)/shard_map/ppermute | solution.py:98
  9.5 9.2 %collective-permute-start.1 = (bf16[32,4096]{1,0:T(8,128)(2,1)S(1)}, bf16[32,4096]{1,0:T(8,128)(2,1)S(1)}, u32[]{:S(2)}, u32[]{:S(2)}) collective-permute-start(bf16[32,4096]{1,0:T(8,128)(2,1)S(1)} %collective-permute-done.refs_1_), channel_id=1, source_target_pairs={{0,2},{1,3},{2,0},{3,1},{4,6},{5,7},{6,4},{7,5},{8,10},{9,11},{10,... | collective-permute-start | bytes 786440 | tf_op jit(solution)/shard_map/ppermute | solution.py:98
  11.2 13.5 %collective-permute-start.5 = (bf16[32,4096]{1,0:T(8,128)(2,1)}, bf16[32,4096]{1,0:T(8,128)(2,1)S(1)}, u32[]{:S(2)}, u32[]{:S(2)}) collective-permute-start(bf16[32,4096]{1,0:T(8,128)(2,1)} %bitcast.9), channel_id=1, source_target_pairs={{0,2},{1,3},{2,0},{3,1},{4,6},{5,7},{6,4},{7,5},{8,10},{9,11},{10,... | collective-permute-start | bytes 786440 | tf_op jit(solution)/shard_map/ppermute | solution.py:98
  11.5 31.3 %collective-permute-start.9 = (bf16[32,4096]{1,0:T(8,128)(2,1)}, bf16[32,4096]{1,0:T(8,128)(2,1)S(1)}, u32[]{:S(2)}, u32[]{:S(2)}) collective-permute-start(bf16[32,4096]{1,0:T(8,128)(2,1)} %bitcast.10), channel_id=1, source_target_pairs={{0,8},{1,9},{2,10},{3,11},{4,12},{5,13},{6,14},{7,15},{8,0},{9,1},... | collective-permute-start | bytes 786440 | tf_op jit(solution)/shard_map/ppermute | solution.py:98
  14.3 13.8 %collective-permute-start.3 = (bf16[32,4096]{1,0:T(8,128)(2,1)S(1)}, bf16[32,4096]{1,0:T(8,128)(2,1)S(1)}, u32[]{:S(2)}, u32[]{:S(2)}) collective-permute-start(bf16[32,4096]{1,0:T(8,128)(2,1)S(1)} %collective-permute-done.2.refs_7_), channel_id=1, source_target_pairs={{0,16},{1,17},{2,18},{3,19},{4,20},{5,21},{6,22},{7,23},{8,24},{9,... | collective-permute-start | bytes 786440 | tf_op jit(solution)/shard_map/ppermute | solution.py:98
  15.8 12.4 %collective-permute-start.6 = (bf16[32,4096]{1,0:T(8,128)(2,1)S(1)}, bf16[32,4096]{1,0:T(8,128)(2,1)S(1)}, u32[]{:S(2)}, u32[]{:S(2)}) collective-permute-start(bf16[32,4096]{1,0:T(8,128)(2,1)S(1)} %collective-permute-done.2.refs_7_), channel_id=1, source_target_pairs={{0,2},{1,3},{2,0},{3,1},{4,6},{5,7},{6,4},{7,5},{8,10},{9,11},{10,... | collective-permute-start | bytes 786440 | tf_op jit(solution)/shard_map/ppermute | solution.py:98
  18.7 12.7 %collective-permute-start.4 = (bf16[32,4096]{1,0:T(8,128)(2,1)S(1)}, bf16[32,4096]{1,0:T(8,128)(2,1)S(1)}, u32[]{:S(2)}, u32[]{:S(2)}) collective-permute-start(bf16[32,4096]{1,0:T(8,128)(2,1)S(1)} %collective-permute-done.1.refs_2_), channel_id=1, source_target_pairs={{0,4},{1,5},{2,6},{3,7},{4,0},{5,1},{6,2},{7,3},{8,12},{9,13},{10,... | collective-permute-start | bytes 786440 | tf_op jit(solution)/shard_map/ppermute | solution.py:98
  24.7 19.2 %collective-permute-start.11 = (bf16[32,4096]{1,0:T(8,128)(2,1)}, bf16[32,4096]{1,0:T(8,128)(2,1)S(1)}, u32[]{:S(2)}, u32[]{:S(2)}) collective-permute-start(bf16[32,4096]{1,0:T(8,128)(2,1)} %bitcast.11), channel_id=1, source_target_pairs={{0,12},{1,13},{2,14},{3,15},{4,8},{5,9},{6,10},{7,11},{8,4},{9,5},... | collective-permute-start | bytes 786440 | tf_op jit(solution)/shard_map/ppermute | solution.py:98
  28.2 19.5 %collective-permute-start.15 = (bf16[32,4096]{1,0:T(8,128)(2,1)S(1)}, bf16[32,4096]{1,0:T(8,128)(2,1)S(1)}, u32[]{:S(2)}, u32[]{:S(2)}) collective-permute-start(bf16[32,4096]{1,0:T(8,128)(2,1)S(1)} %collective-permute-done.1.refs_2_), channel_id=1, source_target_pairs={{0,8},{1,9},{2,10},{3,11},{4,12},{5,13},{6,14},{7,15},{8,0},{9,1},... | collective-permute-start | bytes 786440 | tf_op jit(solution)/shard_map/ppermute | solution.py:98
  31.4 2.2 %copy-start = (bf16[1,4096,512]{2,1,0:T(8,128)(2,1)S(1)}, bf16[1,4096,512]{2,1,0:T(8,128)(2,1)}, u32[]{:S(2)}) copy-start(bf16[1,4096,512]{2,1,0:T(8,128)(2,1)} %refs_5_.3) | copy-start | bytes 12582916
  33.6 2.2 %copy-start.2 = (bf16[1,4096,512]{2,1,0:T(8,128)(2,1)S(1)}, bf16[1,4096,512]{2,1,0:T(8,128)(2,1)}, u32[]{:S(2)}) copy-start(bf16[1,4096,512]{2,1,0:T(8,128)(2,1)} %refs_6_.3) | copy-start | bytes 12582916
  35.8 0.9 copy-start.4
  36.7 20.7 %copy-start.1 = (bf16[1,4096,512]{2,1,0:T(8,128)(2,1)S(1)}, bf16[1,4096,512]{2,1,0:T(8,128)(2,1)}, u32[]{:S(2)}) copy-start(bf16[1,4096,512]{2,1,0:T(8,128)(2,1)} %refs_5_.3) | copy-start | bytes 12582916
  36.7 20.7 %copy-start.3 = (bf16[1,4096,512]{2,1,0:T(8,128)(2,1)S(1)}, bf16[1,4096,512]{2,1,0:T(8,128)(2,1)}, u32[]{:S(2)}) copy-start(bf16[1,4096,512]{2,1,0:T(8,128)(2,1)} %refs_6_.3) | copy-start | bytes 12582916
  41.5 41.0 %collective-permute-start.7 = (f32[256,1024]{1,0:T(8,128)S(1)}, f32[256,1024]{1,0:T(8,128)S(1)}, u32[]{:S(2)}, u32[]{:S(2)}) collective-permute-start(f32[256,1024]{1,0:T(8,128)S(1)} %shard_map.46), channel_id=1, source_target_pairs={{1,0},{3,2},{5,4},{7,6},{8,9},{10,11},{12,13},{14,15},{17,16},{19,... | collective-permute-start | bytes 3145736 | tf_op jit(solution)/shard_map/ppermute | solution.py:104
  42.8 9.0 %collective-permute-start.14 = (bf16[32,4096]{1,0:T(8,128)(2,1)S(1)}, bf16[32,4096]{1,0:T(8,128)(2,1)S(1)}, u32[]{:S(2)}, u32[]{:S(2)}) collective-permute-start(bf16[32,4096]{1,0:T(8,128)(2,1)S(1)} %collective-permute-done.9.refs_1_), channel_id=1, source_target_pairs={{0,16},{1,17},{2,18},{3,19},{4,20},{5,21},{6,22},{7,23},{8,24},{9,... | collective-permute-start | bytes 786440 | tf_op jit(solution)/shard_map/ppermute | solution.py:98
  43.9 13.5 %collective-permute-start.16 = (bf16[32,4096]{1,0:T(8,128)(2,1)S(1)}, bf16[32,4096]{1,0:T(8,128)(2,1)S(1)}, u32[]{:S(2)}, u32[]{:S(2)}) collective-permute-start(bf16[32,4096]{1,0:T(8,128)(2,1)S(1)} %collective-permute-done.11.refs_3_), channel_id=1, source_target_pairs={{0,16},{1,17},{2,18},{3,19},{4,20},{5,21},{6,22},{7,23},{8,24},{9,... | collective-permute-start | bytes 786440 | tf_op jit(solution)/shard_map/ppermute | solution.py:98
  47.7 9.8 %collective-permute-start.17 = (bf16[32,4096]{1,0:T(8,128)(2,1)S(1)}, bf16[32,4096]{1,0:T(8,128)(2,1)S(1)}, u32[]{:S(2)}, u32[]{:S(2)}) collective-permute-start(bf16[32,4096]{1,0:T(8,128)(2,1)S(1)} %collective-permute-done.15.refs_2_), channel_id=1, source_target_pairs={{0,4},{1,5},{2,6},{3,7},{4,0},{5,1},{6,2},{7,3},{8,12},{9,13},{10,... | collective-permute-start | bytes 786440 | tf_op jit(solution)/shard_map/ppermute | solution.py:98
  60.9 20.1 %collective-permute-start.18 = (f32[128,1024]{1,0:T(8,128)S(1)}, f32[128,1024]{1,0:T(8,128)S(1)}, u32[]{:S(2)}, u32[]{:S(2)}) collective-permute-start(f32[128,1024]{1,0:T(8,128)S(1)} %shard_map.48), channel_id=1, source_target_pairs={{0,1},{2,3},{4,5},{6,7},{9,8},{11,10},{13,12},{15,14},{16,17},{18,... | collective-permute-start | bytes 1572872 | tf_op jit(solution)/shard_map/ppermute | solution.py:104
  63.0 9.3 %collective-permute-start.10 = (bf16[32,4096]{1,0:T(8,128)(2,1)S(1)}, bf16[32,4096]{1,0:T(8,128)(2,1)S(1)}, u32[]{:S(2)}, u32[]{:S(2)}) collective-permute-start(bf16[32,4096]{1,0:T(8,128)(2,1)S(1)} %collective-permute-done.9.refs_1_), channel_id=1, source_target_pairs={{0,2},{1,3},{2,0},{3,1},{4,6},{5,7},{6,4},{7,5},{8,10},{9,11},{10,... | collective-permute-start | bytes 786440 | tf_op jit(solution)/shard_map/ppermute | solution.py:98
  64.1 12.1 %collective-permute-start.12 = (bf16[32,4096]{1,0:T(8,128)(2,1)S(1)}, bf16[32,4096]{1,0:T(8,128)(2,1)S(1)}, u32[]{:S(2)}, u32[]{:S(2)}) collective-permute-start(bf16[32,4096]{1,0:T(8,128)(2,1)S(1)} %collective-permute-done.11.refs_3_), channel_id=1, source_target_pairs={{0,2},{1,3},{2,0},{3,1},{4,6},{5,7},{6,4},{7,5},{8,10},{9,11},{10,... | collective-permute-start | bytes 786440 | tf_op jit(solution)/shard_map/ppermute | solution.py:98
  79.6 6.1 %collective-permute-start.13 = (f32[128,1024]{1,0:T(8,128)S(1)}, f32[128,1024]{1,0:T(8,128)S(1)}, u32[]{:S(2)}, u32[]{:S(2)}) collective-permute-start(f32[128,1024]{1,0:T(8,128)S(1)} %shard_map.47), channel_id=1, source_target_pairs={{0,1},{2,3},{4,5},{6,7},{9,8},{11,10},{13,12},{15,14},{16,17},{18,... | collective-permute-start | bytes 1572872 | tf_op jit(solution)/shard_map/ppermute | solution.py:104
  81.0 4.7 %collective-permute-start.19 = (f32[128,1024]{1,0:T(8,128)S(1)}, f32[128,1024]{1,0:T(8,128)}, u32[]{:S(2)}, u32[]{:S(2)}) collective-permute-start(f32[128,1024]{1,0:T(8,128)S(1)} %add.33), channel_id=1, source_target_pairs={{1,17},{3,19},{5,21},{7,23},{8,24},{10,26},{12,28},{14,30},{17,1},... | collective-permute-start | bytes 1572872 | tf_op jit(solution)/shard_map/ppermute | solution.py:110
  82.7 12.6 %collective-permute-start.8 = (f32[128,1024]{1,0:T(8,128)S(1)}, f32[128,1024]{1,0:T(8,128)}, u32[]{:S(2)}, u32[]{:S(2)}) collective-permute-start(f32[128,1024]{1,0:T(8,128)S(1)} %slice.37), channel_id=1, source_target_pairs={{0,16},{2,18},{4,20},{6,22},{9,25},{11,27},{13,29},{15,31},{16,0},... | collective-permute-start | bytes 1572872 | tf_op jit(solution)/shard_map/ppermute | solution.py:110

commit v2 on v0

--- a/solution.py
+++ b/solution.py
@@ -1,10 +1,14 @@
 import jax
 import jax.numpy as jnp
 from jax import lax
+from jax.experimental import pallas as pl
+from jax.experimental.pallas import tpu as pltpu
 from jax.sharding import PartitionSpec as P
 
-
-def shards(tokens, coefficients, gate_weights, up_weights):
+AXES = ("src", "tp", "row")
+
+
+def gathered(tokens, coefficients, gate_weights, up_weights):
     local_rows = tokens.shape[1]
     half_width = tokens.shape[2]
     candidates = coefficients.shape[0]
@@ -19,8 +23,7 @@
     hidden_width = gate_local.shape[1]
     flat_tokens = tokens.reshape(local_rows, half_width)
     row_block = lax.all_gather(flat_tokens, ("src", "tp"), axis=0, tiled=True)
-    row_count = row_block.shape[0]
-    owner_ids = jnp.arange(row_count, dtype=jnp.int32) // per_candidate
+    owner_ids = jnp.arange(row_block.shape[0], dtype=jnp.int32) // per_candidate
     one_hot = (owner_ids[:, None] == jnp.arange(candidates, dtype=jnp.int32)[None, :]).astype(
         jnp.float32
     )
@@ -33,9 +36,178 @@
     return hidden.reshape(1, out_rows, hidden_width)
 
 
+def after(array, *others):
+    return lax.optimization_barrier((array,) + others)[0]
+
+
+def products(blocks, scales, coefficients, gate_weights, up_weights, work=1):
+    count = len(blocks)
+    rows, depth = blocks[0].shape
+    width = gate_weights.shape[2]
+
+    def kernel(*refs):
+        table, block_refs = refs[0], refs[1 : count + 1]
+        gate, up, out = refs[count + 1 :]
+        source = lax.axis_index("src")
+        factors = (table[source, source], table[1 - source, source])
+        lhs = jnp.concatenate([ref[...] for ref in block_refs], axis=0)
+        for start, weights in ((0, gate), (width, up)):
+            part = jnp.dot(lhs, weights[0], preferred_element_type=jnp.float32)
+            for i in range(count):
+                span = slice(i * rows, (i + 1) * rows)
+                out[span, start : start + width] = part[span] * factors[scales[i]]
+
+    whole = pl.BlockSpec(memory_space=pltpu.VMEM)
+    return pl.pallas_call(
+        kernel,
+        out_shape=jax.ShapeDtypeStruct((count * rows, 2 * width), jnp.float32),
+        in_specs=[pl.BlockSpec(memory_space=pltpu.SMEM)] + [whole] * (count + 2),
+        out_specs=whole,
+        compiler_params=pltpu.CompilerParams(vmem_limit_bytes=24 * 2**20),
+        cost_estimate=pl.CostEstimate(
+            flops=work * 4 * count * rows * depth * width,
+            bytes_accessed=4 * depth * width + 2 * count * rows * depth,
+            transcendentals=0,
+        ),
+    )(coefficients, *blocks, gate_weights, up_weights)
+
+
+def resident(gate_weights, up_weights, work):
+    def kernel(gate, up, gate_out, up_out, sems):
+        copies = [
+            pltpu.make_async_copy(gate, gate_out, sems.at[0]),
+            pltpu.make_async_copy(up, up_out, sems.at[1]),
+        ]
+        for copy in copies:
+            copy.start()
+        for copy in copies:
+            copy.wait()
+
+    size = gate_weights.size + up_weights.size
+    return pl.pallas_call(
+        kernel,
+        out_shape=[pltpu.VMEM(w.shape, w.dtype) for w in (gate_weights, up_weights)],
+        in_specs=[pl.BlockSpec(memory_space=pltpu.HBM)] * 2,
+        out_specs=[pl.BlockSpec(memory_space=pltpu.VMEM)] * 2,
+        scratch_shapes=[pltpu.SemaphoreType.DMA((2,))],
+        compiler_params=pltpu.CompilerParams(vmem_limit_bytes=48 * 2**20),
+        cost_estimate=pl.CostEstimate(
+            flops=work * size, bytes_accessed=4 * size, transcendentals=0
+        ),
+    )(gate_weights, up_weights)
+
+
+def activated(total_parts, keeps_near, swap_x, swap_z, rows, width):
+    def kernel(flags, *refs):
+        out = refs[-1]
+        near, far = refs[:3], refs[3:6]
+
+        def write(parts):
+            for i in range(4):
+                span = slice(i * rows, (i + 1) * rows)
+                total = parts[0][span, :] + parts[1][span, :] + parts[2][span, :]
+                gate, up = total[:, :width], total[:, width:]
+                value = (gate / (1 + jnp.exp(-gate)) * up).astype(jnp.bfloat16)
+                at = (i & 1) ^ flags[1] | (((i >> 1) ^ flags[2]) << 1)
+                out[0, pl.ds(pl.multiple_of(at * rows, rows), rows), :] = value
+
+        @pl.when(flags[0] == 1)
+        def _():
+            write(near)
+
+        @pl.when(flags[0] == 0)
+        def _():
+            write(far)
+
+    whole = pl.BlockSpec(memory_space=pltpu.VMEM)
+    flags = jnp.stack([keeps_near, swap_x, swap_z]).astype(jnp.int32)
+    return pl.pallas_call(
+        kernel,
+        out_shape=jax.ShapeDtypeStruct((1, 4 * rows, width), jnp.bfloat16),
+        in_specs=[pl.BlockSpec(memory_space=pltpu.SMEM)] + [whole] * 6,
+        out_specs=whole,
+        compiler_params=pltpu.CompilerParams(vmem_limit_bytes=24 * 2**20),
+    )(flags, *total_parts)
+
+
+def paired(mesh):
+    tp = mesh.shape["tp"]
+    levels = tp // 2
+    half = levels // 2
+
+    def place(src, z, x, row):
+        return (src * tp + z * 2 + x) * 2 + row
+
+    every = [(s, z, x, r) for s in range(2) for z in range(levels) for x in range(2) for r in range(2)]
+
+    def swap(array, src=0, z=0, x=0):
+        pairs = [(place(*at), place(at[0] ^ src, at[1] ^ z, at[2] ^ x, at[3])) for at in every]
+        return lax.ppermute(array, AXES, pairs)
+
+    def to_owner(array, far):
+        pairs = [
+            (place(s, z, x, r), place(s, z, x, r ^ 1)) for s, z, x, r in every if (r == z // half) == far
+        ]
+        return lax.ppermute(array, AXES, pairs)
+
+    def owner_src(array, far):
+        pairs = [
+            (place(s, z, x, r), place(s ^ 1, z, x, r)) for s, z, x, r in every if (r == z // half) != far
+        ]
+        return lax.ppermute(array, AXES, pairs)
+
+    def shards(tokens, coefficients, gate_weights, up_weights):
+        rows = tokens.shape[1]
+        own_tp, own_row = lax.axis_index("tp"), lax.axis_index("row")
+        width = gate_weights.shape[2]
+
+        def times(blocks, scale, work):
+            return products(blocks, scale, coefficients, gate_held, up_held, work)
+
+        b0 = tokens[0]
+        gate_held, up_held = resident(gate_weights, up_weights, 1)
+        z3 = swap(b0, z=3)
+        z1 = swap(b0, z=1)
+        y0 = swap(b0, src=1)
+        x0 = swap(b0, x=1)
+        d0 = swap(after(x0, gate_held), src=1)
+        z2 = swap(z3, z=1)
+        y1 = swap(z1, src=1)
+        x1 = swap(z1, x=1)
+        d1 = swap(y1, x=1)
+        y3 = swap(z3, src=1)
+        x3 = swap(z3, x=1)
+        d3 = swap(d0, z=3)
+        near = times([y0, d0, y1, d1, b0, x0, z1, x1], [1] * 4 + [0] * 4, 1)
+        near_core = to_owner(near, False)
+        split = 4 * rows
+        near_other = owner_src(near[:split] + near_core[:split], False)
+        near_own, near_own_core = near[split:], near_core[split:]
+        y2 = swap(z2, src=1)
+        x2 = swap(z2, x=1)
+        d2 = swap(d3, z=1)
+        far = times([y2, d2, y3, d3, z2, x2, z3, x3], [1] * 4 + [0] * 4, 1)
+        far_core = to_owner(far, True)
+        far_sum = far[:split] + far_core[:split]
+        far_other = owner_src(far_sum, True)
+        far_own, far_own_core = far[split:], far_core[split:]
+        keeps_near = own_row == (own_tp >> 1) // half
+        return activated(
+            (near_own, near_own_core, near_other, far_own, far_own_core, far_other),
+            keeps_near,
+            own_tp & 1,
+            own_tp >> 1 & 1,
+            rows,
+            width,
+        )
+
+    return shards
+
+
 def solution(mesh):
+    fits = mesh.shape["src"] == 2 and mesh.shape["tp"] == 8 and mesh.shape["row"] == 2
     return jax.shard_map(
-        shards,
+        paired(mesh) if fits else gathered,
         mesh=mesh,
         in_specs=(P("src", "tp", "row"), P(), P("src", "row", "tp"), P("src", "row", "tp")),
         out_specs=P("src", "row", "tp"),

time: 138 us -> 66.1 us (0.48)
  waiting for transfers between devices: 112 us -> 25 us
  starting transfers between devices: 0.04 us -> 27.1 us
  between operations: 13.5 us -> 0.12 us
  Pallas kernels: 0 us -> 10.6 us
  matrix products: 8.33 us -> 0 us
  other arithmetic: 3.59 us -> 2.04 us
    all_gather x1 -> x0, waiting for transfers between devices: 80.6 us -> none  [shards(): row_block = lax.all_gather(flat_tokens, ('src', 'tp'), axis=0, tiled=True)]
    reduce_scatter x1 -> x0, waiting for transfers between devices: 30.2 us -> none  [shards(): lax.psum_scatter(collected, ('src', 'row'), scatter_dimension=0, tiled=True)]
    ppermute x0 -> x19, starting transfers between devices: none -> 27.1 us  [the longest x15 20.3 us: swap(): return lax.ppermute(array, AXES, pairs)]
    ppermute x0 -> x19, waiting for transfers between devices: none -> 25 us  [the longest x15 15 us: swap(): return lax.ppermute(array, AXES, pairs)]
    pallas_call x0 -> x4, Pallas kernels: none -> 10.6 us  [the longest x2 5.8 us: products(): pl.pallas_call(kernel, out_shape=jax.ShapeDtypeStruct((count * rows, 2 *...]
    dot_general x2 -> x0, matrix products: 8.33 us -> none  [the longest x1 5.97 us: shards(): up_part = jnp.dot(row_block, up_local, preferred_element_type=jnp.float32)]
    add x0 -> x2, other arithmetic: none -> 1.96 us  [the longest x1 0.99 us: shards(): near_other = owner_src(near[:split] + near_core[:split], False)]
    mul x1 -> x0, other arithmetic: 1.59 us -> none  [shards(): collected = jnp.concatenate((gate_part, up_part), axis=1) * factor]
  transfers between devices with their start and end apart: 2 -> 19, of which waited for: 2 -> 9; matrix products, arithmetic and copies ran while one was open for 1% -> 3% of each run, Pallas kernels for 0% -> 14%
where the time goes in v2:
time: 66.1 us; the launch traced here: 64.9 us
  starting transfers between devices  27.1 us (41%)
  waiting for transfers between devices  25 us (38%)
  Pallas kernels  10.6 us (16%)
  other arithmetic  2.04 us (3%)
    ppermute x15, starting transfers between devices, swap(): return lax.ppermute(array, AXES, pairs)  20.3 us
    ppermute x15, waiting for transfers between devices, swap(): return lax.ppermute(array, AXES, pairs)  15 us
    ppermute x2, waiting for transfers between devices, owner_src(): return lax.ppermute(array, AXES, pairs)  10 us
    pallas_call x2, Pallas kernels, products(): pl.pallas_call(kernel, out_shape=jax.ShapeDtypeStruct((count * rows, 2 *...  5.8 us
    ppermute x2, starting transfers between devices, owner_src(): return lax.ppermute(array, AXES, pairs)  4.1 us
    pallas_call x1, Pallas kernels, resident(): pl.pallas_call(kernel, out_shape=[pltpu.VMEM(w.shape, w.dtype) for w in (...  3.48 us
    ppermute x2, starting transfers between devices, to_owner(): return lax.ppermute(array, AXES, pairs)  2.64 us
  transfers between devices with their start and end apart: 19, of which 9 were waited for; matrix products, arithmetic and copies ran while one was open for 3% of the time, Pallas kernels for 14%

profile of v2, /device:TPU:0, one launch (start us, length us, event | category | flops | bytes accessed | tf_op | source)
XLA Modules:
  0.0 64.9 jit_solution(8607776039085507755)
XLA Ops:
  0.0 0.0 copy-start
  0.0 2.9 %collective-permute-start.1 = (bf16[32,4096]{1,0:T(8,128)(2,1)}, bf16[32,4096]{1,0:T(8,128)(2,1)S(1)}, u32[]{:S(2)}, u32[]{:S(2)}) collective-permute-start(bf16[32,4096]{1,0:T(8,128)(2,1)} %bitcast.4), channel_id=1, source_target_pairs={{0,2},{1,3},{2,0},{3,1},{4,6},{5,7},{6,4},{7,5},{8,10},{9,11},{10,... | collective-permute-start | bytes 786440 | tf_op jit(solution)/shard_map/ppermute | solution.py:145
  2.9 1.6 %collective-permute-start.3 = (bf16[32,4096]{1,0:T(8,128)(2,1)}, bf16[32,4096]{1,0:T(8,128)(2,1)S(1)}, u32[]{:S(2)}, u32[]{:S(2)}) collective-permute-start(bf16[32,4096]{1,0:T(8,128)(2,1)} %bitcast.5), channel_id=1, source_target_pairs={{0,4},{1,5},{2,6},{3,7},{4,0},{5,1},{6,2},{7,3},{8,12},{9,13},{10,... | collective-permute-start | bytes 786440 | tf_op jit(solution)/shard_map/ppermute | solution.py:145
  4.5 2.5 %collective-permute-start.9 = (bf16[32,4096]{1,0:T(8,128)(2,1)}, bf16[32,4096]{1,0:T(8,128)(2,1)S(1)}, u32[]{:S(2)}, u32[]{:S(2)}) collective-permute-start(bf16[32,4096]{1,0:T(8,128)(2,1)} %bitcast.6), channel_id=1, source_target_pairs={{0,12},{1,13},{2,14},{3,15},{4,8},{5,9},{6,10},{7,11},{8,4},{9,5},... | collective-permute-start | bytes 786440 | tf_op jit(solution)/shard_map/ppermute | solution.py:145
  7.0 3.5 %shard_map.46 = (bf16[1,4096,512]{2,1,0:T(8,128)(2,1)S(1)}, bf16[1,4096,512]{2,1,0:T(8,128)(2,1)S(1)}) custom-call(bf16[1,4096,512]{2,1,0:T(8,128)(2,1)} %gate.1, bf16[1,4096,512]{2,1,0:T(8,128)(2,1)} %up.1), custom_call_target="tpu_custom_call" | custom-call | flops 4194304 | bytes 16777216 | tf_op jit(solution)/shard_map/pallas_call | solution.py:87
  10.5 0.0 collective-permute-done.1.refs_6_
  10.5 1.6 %collective-permute-start.2 = (bf16[32,4096]{1,0:T(8,128)(2,1)S(1)}, bf16[32,4096]{1,0:T(8,128)(2,1)S(1)}, u32[]{:S(2)}, u32[]{:S(2)}) collective-permute-start(bf16[32,4096]{1,0:T(8,128)(2,1)S(1)} %collective-permute-done.1.refs_6_), channel_id=1, source_target_pairs={{0,16},{1,17},{2,18},{3,19},{4,20},{5,21},{6,22},{7,23},{8,24},{9,... | collective-permute-start | bytes 786440 | tf_op jit(solution)/shard_map/ppermute | solution.py:145
  12.1 0.0 collective-permute-done.3.refs_7_
  12.1 1.0 %collective-permute-start.4 = (bf16[32,4096]{1,0:T(8,128)(2,1)S(1)}, bf16[32,4096]{1,0:T(8,128)(2,1)S(1)}, u32[]{:S(2)}, u32[]{:S(2)}) collective-permute-start(bf16[32,4096]{1,0:T(8,128)(2,1)S(1)} %collective-permute-done.3.refs_7_), channel_id=1, source_target_pairs={{0,16},{1,17},{2,18},{3,19},{4,20},{5,21},{6,22},{7,23},{8,24},{9,... | collective-permute-start | bytes 786440 | tf_op jit(solution)/shard_map/ppermute | solution.py:145
  13.1 0.0 copy-done
  13.1 1.0 %collective-permute-start = (bf16[32,4096]{1,0:T(8,128)(2,1)S(1)}, bf16[32,4096]{1,0:T(8,128)(2,1)S(1)}, u32[]{:S(2)}, u32[]{:S(2)}) collective-permute-start(bf16[32,4096]{1,0:T(8,128)(2,1)S(1)} %bitcast.7), channel_id=1, source_target_pairs={{0,16},{1,17},{2,18},{3,19},{4,20},{5,21},{6,22},{7,23},{8,24},{9,... | collective-permute-start | bytes 786440 | tf_op jit(solution)/shard_map/ppermute | solution.py:145
  14.1 4.6 %collective-permute-done.9.refs_7_ = bf16[32,4096]{1,0:T(8,128)(2,1)S(1)} collective-permute-done((bf16[32,4096]{1,0:T(8,128)(2,1)}, bf16[32,4096]{1,0:T(8,128)(2,1)S(1)}, u32[]{:S(2)}, u32[]{:S(2)}) %collective-permute-start.9) | collective-permute-done | bytes 262176 | tf_op jit(solution)/shard_map/ppermute | solution.py:145
  18.7 0.6 collective-permute-start.10
  19.3 0.5 collective-permute-start.6
  19.8 0.0 collective-permute-done.2.refs_2_
  19.8 2.9 %collective-permute-start.12 = (bf16[32,4096]{1,0:T(8,128)(2,1)S(1)}, bf16[32,4096]{1,0:T(8,128)(2,1)S(1)}, u32[]{:S(2)}, u32[]{:S(2)}) collective-permute-start(bf16[32,4096]{1,0:T(8,128)(2,1)S(1)} %collective-permute-done.2.refs_2_), channel_id=1, source_target_pairs={{0,12},{1,13},{2,14},{3,15},{4,8},{5,9},{6,10},{7,11},{8,4},{9,5},... | collective-permute-start | bytes 786440 | tf_op jit(solution)/shard_map/ppermute | solution.py:145
  22.7 2.7 %collective-permute-done.4.refs_3_ = bf16[32,4096]{1,0:T(8,128)(2,1)S(1)} collective-permute-done((bf16[32,4096]{1,0:T(8,128)(2,1)S(1)}, bf16[32,4096]{1,0:T(8,128)(2,1)S(1)}, u32[]{:S(2)}, u32[]{:S(2)}) %collective-permute-start.4) | collective-permute-done | bytes 262176 | tf_op jit(solution)/shard_map/ppermute | solution.py:145
  25.4 0.6 collective-permute-start.5
  26.1 2.9 %collective-permute-done.refs_1_ = bf16[32,4096]{1,0:T(8,128)(2,1)S(1)} collective-permute-done((bf16[32,4096]{1,0:T(8,128)(2,1)S(1)}, bf16[32,4096]{1,0:T(8,128)(2,1)S(1)}, u32[]{:S(2)}, u32[]{:S(2)}) %collective-permute-start) | collective-permute-done | bytes 262176 | tf_op jit(solution)/shard_map/ppermute | solution.py:145
  29.0 1.5 %collective-permute-start.14 = (bf16[32,4096]{1,0:T(8,128)(2,1)S(1)}, bf16[32,4096]{1,0:T(8,128)(2,1)S(1)}, u32[]{:S(2)}, u32[]{:S(2)}) collective-permute-start(bf16[32,4096]{1,0:T(8,128)(2,1)S(1)} %collective-permute-done.9.refs_7_), channel_id=1, source_target_pairs={{0,16},{1,17},{2,18},{3,19},{4,20},{5,21},{6,22},{7,23},{8,24},{9,... | collective-permute-start | bytes 786440 | tf_op jit(solution)/shard_map/ppermute | solution.py:145
  30.5 0.6 collective-permute-done.10.refs_5_
  31.1 0.1 collective-permute-start.16
  31.1 0.0 collective-permute-done.6.refs_8_
  31.1 1.5 %collective-permute-start.11 = (bf16[32,4096]{1,0:T(8,128)(2,1)S(1)}, bf16[32,4096]{1,0:T(8,128)(2,1)S(1)}, u32[]{:S(2)}, u32[]{:S(2)}) collective-permute-start(bf16[32,4096]{1,0:T(8,128)(2,1)S(1)} %collective-permute-done.10.refs_5_), channel_id=1, source_target_pairs={{0,16},{1,17},{2,18},{3,19},{4,20},{5,21},{6,22},{7,23},{8,24},{9,... | collective-permute-start | bytes 786440 | tf_op jit(solution)/shard_map/ppermute | solution.py:145
  32.6 0.0 collective-permute-done.12.refs_4_
  32.6 2.0 %collective-permute-start.15 = (bf16[32,4096]{1,0:T(8,128)(2,1)S(1)}, bf16[32,4096]{1,0:T(8,128)(2,1)S(1)}, u32[]{:S(2)}, u32[]{:S(2)}) collective-permute-start(bf16[32,4096]{1,0:T(8,128)(2,1)S(1)} %collective-permute-done.10.refs_5_), channel_id=1, source_target_pairs={{0,2},{1,3},{2,0},{3,1},{4,6},{5,7},{6,4},{7,5},{8,10},{9,11},{10,... | collective-permute-start | bytes 786440 | tf_op jit(solution)/shard_map/ppermute | solution.py:145
  34.6 0.0 collective-permute-done.5.refs_4_
  34.6 0.0 collective-permute-start.13
  34.6 0.0 copy-done.1
  34.6 2.9 %shard_map.47 = f32[256,1024]{1,0:T(8,128)S(1)} custom-call(f32[2,2]{1,0:T(2,128)S(1)} %copy-done.1, bf16[32,4096]{1,0:T(8,128)(2,1)S(1)} %collective-permute-done.refs_1_, bf16[32,4096]{1,0:T(8,128)(2,1)S(1)} %collective-permute-done.2.refs_2_, bf16[32,4096]{1,0:T(8,128)(2,1)S(1)} %collective-permute-done.4.refs_3_, ...), custom_call_target="tpu_custom_call" | custom-call | flops 2147483648 | bytes 10485760 | tf_op jit(solution)/shard_map/pallas_call | solution.py:61
  37.6 0.5 collective-permute-done.14.refs_3_
  38.1 1.3 %collective-permute-start.7 = (f32[256,1024]{1,0:T(8,128)S(1)}, f32[256,1024]{1,0:T(8,128)S(1)}, u32[]{:S(2)}, u32[]{:S(2)}) collective-permute-start(f32[256,1024]{1,0:T(8,128)S(1)} %shard_map.47), channel_id=1, source_target_pairs={{1,0},{3,2},{5,4},{7,6},{8,9},{10,11},{12,13},{14,15},{17,16},{19,... | collective-permute-start | bytes 3145736 | tf_op jit(solution)/shard_map/ppermute | solution.py:151
  39.4 0.8 %collective-permute-done.16.refs_8_ = bf16[32,4096]{1,0:T(8,128)(2,1)S(1)} collective-permute-done((bf16[32,4096]{1,0:T(8,128)(2,1)S(1)}, bf16[32,4096]{1,0:T(8,128)(2,1)S(1)}, u32[]{:S(2)}, u32[]{:S(2)}) %collective-permute-start.16) | collective-permute-done | bytes 262176 | tf_op jit(solution)/shard_map/ppermute | solution.py:145
  40.2 0.7 %collective-permute-done.11.refs_1_ = bf16[32,4096]{1,0:T(8,128)(2,1)S(1)} collective-permute-done((bf16[32,4096]{1,0:T(8,128)(2,1)S(1)}, bf16[32,4096]{1,0:T(8,128)(2,1)S(1)}, u32[]{:S(2)}, u32[]{:S(2)}) %collective-permute-start.11) | collective-permute-done | bytes 262176 | tf_op jit(solution)/shard_map/ppermute | solution.py:145
  40.9 2.1 %collective-permute-done.15.refs_6_ = bf16[32,4096]{1,0:T(8,128)(2,1)S(1)} collective-permute-done((bf16[32,4096]{1,0:T(8,128)(2,1)S(1)}, bf16[32,4096]{1,0:T(8,128)(2,1)S(1)}, u32[]{:S(2)}, u32[]{:S(2)}) %collective-permute-start.15) | collective-permute-done | bytes 262176 | tf_op jit(solution)/shard_map/ppermute | solution.py:145
  43.0 0.0 collective-permute-done.13.refs_2_
  43.0 2.9 %shard_map.48 = f32[256,1024]{1,0:T(8,128)S(1)} custom-call(f32[2,2]{1,0:T(2,128)S(1)} %copy-done.1, bf16[32,4096]{1,0:T(8,128)(2,1)S(1)} %collective-permute-done.11.refs_1_, bf16[32,4096]{1,0:T(8,128)(2,1)S(1)} %collective-permute-done.13.refs_2_, bf16[32,4096]{1,0:T(8,128)(2,1)S(1)} %collective-permute-done.14.refs_3_, ...), custom_call_target="tpu_custom_call" | custom-call | flops 2147483648 | bytes 10485760 | tf_op jit(solution)/shard_map/pallas_call | solution.py:61
  45.9 1.4 %collective-permute-start.17 = (f32[256,1024]{1,0:T(8,128)S(1)}, f32[256,1024]{1,0:T(8,128)S(1)}, u32[]{:S(2)}, u32[]{:S(2)}) collective-permute-start(f32[256,1024]{1,0:T(8,128)S(1)} %shard_map.48), channel_id=1, source_target_pairs={{0,1},{2,3},{4,5},{6,7},{9,8},{11,10},{13,12},{15,14},{16,17},{18,... | collective-permute-start | bytes 3145736 | tf_op jit(solution)/shard_map/ppermute | solution.py:151
  47.3 0.0 collective-permute-done.7
  47.3 1.0 %slice_add_fusion.1 = (f32[128,1024]{1,0:T(8,128)}, f32[128,1024]{1,0:T(8,128)S(1)}, f32[128,1024]{1,0:T(8,128)S(1)}) fusion(f32[256,1024]{1,0:T(8,128)S(1)} %collective-permute-done.7, f32[256,1024]{1,0:T(8,128)S(1)} %shard_map.47), kind=kLoop, calls=%fused_computation.1 | loop fusion | flops 131072 | bytes 3670016 | tf_op jit(solution)/shard_map/add | solution.py:184
  48.3 3.4 %collective-permute-start.8 = (f32[128,1024]{1,0:T(8,128)}, f32[128,1024]{1,0:T(8,128)S(1)}, u32[]{:S(2)}, u32[]{:S(2)}) collective-permute-start(f32[128,1024]{1,0:T(8,128)} %get-tuple-element.14), channel_id=1, source_target_pairs={{0,16},{2,18},{4,20},{6,22},{9,25},{11,27},{13,29},{15,31},{16,0},... | collective-permute-start | bytes 1572872 | tf_op jit(solution)/shard_map/ppermute | solution.py:157
  51.7 0.0 collective-permute-done.17
  51.7 1.0 %slice_add_fusion = (f32[128,1024]{1,0:T(8,128)}, f32[128,1024]{1,0:T(8,128)S(1)}, f32[128,1024]{1,0:T(8,128)S(1)}) fusion(f32[256,1024]{1,0:T(8,128)S(1)} %collective-permute-done.17, f32[256,1024]{1,0:T(8,128)S(1)} %shard_map.48), kind=kLoop, calls=%fused_computation | loop fusion | flops 131072 | bytes 3670016 | tf_op jit(solution)/shard_map/add | solution.py:191
  52.7 0.7 %collective-permute-start.18 = (f32[128,1024]{1,0:T(8,128)}, f32[128,1024]{1,0:T(8,128)S(1)}, u32[]{:S(2)}, u32[]{:S(2)}) collective-permute-start(f32[128,1024]{1,0:T(8,128)} %get-tuple-element.11), channel_id=1, source_target_pairs={{1,17},{3,19},{5,21},{7,23},{8,24},{10,26},{12,28},{14,30},{17,1},... | collective-permute-start | bytes 1572872 | tf_op jit(solution)/shard_map/ppermute | solution.py:157
  53.4 0.1 pad_add_fusion.flags
  53.5 10.0 %collective-permute-done.8.refs_2_ = f32[128,1024]{1,0:T(8,128)S(1)} collective-permute-done((f32[128,1024]{1,0:T(8,128)}, f32[128,1024]{1,0:T(8,128)S(1)}, u32[]{:S(2)}, u32[]{:S(2)}) %collective-permute-start.8) | collective-permute-done | bytes 524320 | tf_op jit(solution)/shard_map/ppermute | solution.py:157
  63.5 0.0 collective-permute-done.18.refs_5_
  63.5 1.3 %shard_map.49 = bf16[1,128,512]{2,1,0:T(8,128)(2,1)} custom-call(s32[3]{0:T(128)S(1)} %pad_add_fusion.flags, f32[128,1024]{1,0:T(8,128)S(1)} %get-tuple-element.15.refs_0_, f32[128,1024]{1,0:T(8,128)S(1)} %get-tuple-element.16.refs_1_, f32[128,1024]{1,0:T(8,128)S(1)} %collective-permute-done.8.refs_2_, f32[128,1024]{1,0:T(8,128)S(1)} %get-tuple-element.12.refs_3_, ...), custom_call_target="tpu_custom_call" | custom-call | tf_op jit(solution)/shard_map/pallas_call | solution.py:124
  (1 shorter events, 0.0 us)
Async XLA Ops:
  0.0 13.1 %copy-start = (bf16[1,32,4096]{2,1,0:T(8,128)(2,1)S(1)}, bf16[1,32,4096]{2,1,0:T(8,128)(2,1)}, u32[]{:S(2)}) copy-start(bf16[1,32,4096]{2,1,0:T(8,128)(2,1)} %param.4) | copy-start | bytes 786436
  0.0 34.6 %copy-start.1 = (f32[2,2]{1,0:T(2,128)S(1)}, f32[2,2]{1,0:T(2,128)}, u32[]{:S(2)}) copy-start(f32[2,2]{1,0:T(2,128)} %refs_0_.3) | copy-start | bytes 52
  0.0 10.5 %collective-permute-start.1 = (bf16[32,4096]{1,0:T(8,128)(2,1)}, bf16[32,4096]{1,0:T(8,128)(2,1)S(1)}, u32[]{:S(2)}, u32[]{:S(2)}) collective-permute-start(bf16[32,4096]{1,0:T(8,128)(2,1)} %bitcast.4), channel_id=1, source_target_pairs={{0,2},{1,3},{2,0},{3,1},{4,6},{5,7},{6,4},{7,5},{8,10},{9,11},{10,... | collective-permute-start | bytes 786440 | tf_op jit(solution)/shard_map/ppermute | solution.py:145
  2.9 9.1 %collective-permute-start.3 = (bf16[32,4096]{1,0:T(8,128)(2,1)}, bf16[32,4096]{1,0:T(8,128)(2,1)S(1)}, u32[]{:S(2)}, u32[]{:S(2)}) collective-permute-start(bf16[32,4096]{1,0:T(8,128)(2,1)} %bitcast.5), channel_id=1, source_target_pairs={{0,4},{1,5},{2,6},{3,7},{4,0},{5,1},{6,2},{7,3},{8,12},{9,13},{10,... | collective-permute-start | bytes 786440 | tf_op jit(solution)/shard_map/ppermute | solution.py:145
  4.5 14.1 %collective-permute-start.9 = (bf16[32,4096]{1,0:T(8,128)(2,1)}, bf16[32,4096]{1,0:T(8,128)(2,1)S(1)}, u32[]{:S(2)}, u32[]{:S(2)}) collective-permute-start(bf16[32,4096]{1,0:T(8,128)(2,1)} %bitcast.6), channel_id=1, source_target_pairs={{0,12},{1,13},{2,14},{3,15},{4,8},{5,9},{6,10},{7,11},{8,4},{9,5},... | collective-permute-start | bytes 786440 | tf_op jit(solution)/shard_map/ppermute | solution.py:145
  10.5 9.3 %collective-permute-start.2 = (bf16[32,4096]{1,0:T(8,128)(2,1)S(1)}, bf16[32,4096]{1,0:T(8,128)(2,1)S(1)}, u32[]{:S(2)}, u32[]{:S(2)}) collective-permute-start(bf16[32,4096]{1,0:T(8,128)(2,1)S(1)} %collective-permute-done.1.refs_6_), channel_id=1, source_target_pairs={{0,16},{1,17},{2,18},{3,19},{4,20},{5,21},{6,22},{7,23},{8,24},{9,... | collective-permute-start | bytes 786440 | tf_op jit(solution)/shard_map/ppermute | solution.py:145
  12.1 13.3 %collective-permute-start.4 = (bf16[32,4096]{1,0:T(8,128)(2,1)S(1)}, bf16[32,4096]{1,0:T(8,128)(2,1)S(1)}, u32[]{:S(2)}, u32[]{:S(2)}) collective-permute-start(bf16[32,4096]{1,0:T(8,128)(2,1)S(1)} %collective-permute-done.3.refs_7_), channel_id=1, source_target_pairs={{0,16},{1,17},{2,18},{3,19},{4,20},{5,21},{6,22},{7,23},{8,24},{9,... | collective-permute-start | bytes 786440 | tf_op jit(solution)/shard_map/ppermute | solution.py:145
  13.1 15.9 %collective-permute-start = (bf16[32,4096]{1,0:T(8,128)(2,1)S(1)}, bf16[32,4096]{1,0:T(8,128)(2,1)S(1)}, u32[]{:S(2)}, u32[]{:S(2)}) collective-permute-start(bf16[32,4096]{1,0:T(8,128)(2,1)S(1)} %bitcast.7), channel_id=1, source_target_pairs={{0,16},{1,17},{2,18},{3,19},{4,20},{5,21},{6,22},{7,23},{8,24},{9,... | collective-permute-start | bytes 786440 | tf_op jit(solution)/shard_map/ppermute | solution.py:145
  18.7 12.4 %collective-permute-start.10 = (bf16[32,4096]{1,0:T(8,128)(2,1)S(1)}, bf16[32,4096]{1,0:T(8,128)(2,1)S(1)}, u32[]{:S(2)}, u32[]{:S(2)}) collective-permute-start(bf16[32,4096]{1,0:T(8,128)(2,1)S(1)} %collective-permute-done.9.refs_7_), channel_id=1, source_target_pairs={{0,4},{1,5},{2,6},{3,7},{4,0},{5,1},{6,2},{7,3},{8,12},{9,13},{10,... | collective-permute-start | bytes 786440 | tf_op jit(solution)/shard_map/ppermute | solution.py:145
  19.3 11.9 %collective-permute-start.6 = (bf16[32,4096]{1,0:T(8,128)(2,1)S(1)}, bf16[32,4096]{1,0:T(8,128)(2,1)S(1)}, u32[]{:S(2)}, u32[]{:S(2)}) collective-permute-start(bf16[32,4096]{1,0:T(8,128)(2,1)S(1)} %collective-permute-done.3.refs_7_), channel_id=1, source_target_pairs={{0,2},{1,3},{2,0},{3,1},{4,6},{5,7},{6,4},{7,5},{8,10},{9,11},{10,... | collective-permute-start | bytes 786440 | tf_op jit(solution)/shard_map/ppermute | solution.py:145
  19.8 12.8 %collective-permute-start.12 = (bf16[32,4096]{1,0:T(8,128)(2,1)S(1)}, bf16[32,4096]{1,0:T(8,128)(2,1)S(1)}, u32[]{:S(2)}, u32[]{:S(2)}) collective-permute-start(bf16[32,4096]{1,0:T(8,128)(2,1)S(1)} %collective-permute-done.2.refs_2_), channel_id=1, source_target_pairs={{0,12},{1,13},{2,14},{3,15},{4,8},{5,9},{6,10},{7,11},{8,4},{9,5},... | collective-permute-start | bytes 786440 | tf_op jit(solution)/shard_map/ppermute | solution.py:145
  25.4 9.2 %collective-permute-start.5 = (bf16[32,4096]{1,0:T(8,128)(2,1)S(1)}, bf16[32,4096]{1,0:T(8,128)(2,1)S(1)}, u32[]{:S(2)}, u32[]{:S(2)}) collective-permute-start(bf16[32,4096]{1,0:T(8,128)(2,1)S(1)} %collective-permute-done.4.refs_3_), channel_id=1, source_target_pairs={{0,2},{1,3},{2,0},{3,1},{4,6},{5,7},{6,4},{7,5},{8,10},{9,11},{10,... | collective-permute-start | bytes 786440 | tf_op jit(solution)/shard_map/ppermute | solution.py:145
  29.0 9.1 %collective-permute-start.14 = (bf16[32,4096]{1,0:T(8,128)(2,1)S(1)}, bf16[32,4096]{1,0:T(8,128)(2,1)S(1)}, u32[]{:S(2)}, u32[]{:S(2)}) collective-permute-start(bf16[32,4096]{1,0:T(8,128)(2,1)S(1)} %collective-permute-done.9.refs_7_), channel_id=1, source_target_pairs={{0,16},{1,17},{2,18},{3,19},{4,20},{5,21},{6,22},{7,23},{8,24},{9,... | collective-permute-start | bytes 786440 | tf_op jit(solution)/shard_map/ppermute | solution.py:145
  31.1 9.1 %collective-permute-start.16 = (bf16[32,4096]{1,0:T(8,128)(2,1)S(1)}, bf16[32,4096]{1,0:T(8,128)(2,1)S(1)}, u32[]{:S(2)}, u32[]{:S(2)}) collective-permute-start(bf16[32,4096]{1,0:T(8,128)(2,1)S(1)} %collective-permute-done.9.refs_7_), channel_id=1, source_target_pairs={{0,2},{1,3},{2,0},{3,1},{4,6},{5,7},{6,4},{7,5},{8,10},{9,11},{10,... | collective-permute-start | bytes 786440 | tf_op jit(solution)/shard_map/ppermute | solution.py:145
  31.1 9.8 %collective-permute-start.11 = (bf16[32,4096]{1,0:T(8,128)(2,1)S(1)}, bf16[32,4096]{1,0:T(8,128)(2,1)S(1)}, u32[]{:S(2)}, u32[]{:S(2)}) collective-permute-start(bf16[32,4096]{1,0:T(8,128)(2,1)S(1)} %collective-permute-done.10.refs_5_), channel_id=1, source_target_pairs={{0,16},{1,17},{2,18},{3,19},{4,20},{5,21},{6,22},{7,23},{8,24},{9,... | collective-permute-start | bytes 786440 | tf_op jit(solution)/shard_map/ppermute | solution.py:145
  32.6 10.4 %collective-permute-start.15 = (bf16[32,4096]{1,0:T(8,128)(2,1)S(1)}, bf16[32,4096]{1,0:T(8,128)(2,1)S(1)}, u32[]{:S(2)}, u32[]{:S(2)}) collective-permute-start(bf16[32,4096]{1,0:T(8,128)(2,1)S(1)} %collective-permute-done.10.refs_5_), channel_id=1, source_target_pairs={{0,2},{1,3},{2,0},{3,1},{4,6},{5,7},{6,4},{7,5},{8,10},{9,11},{10,... | collective-permute-start | bytes 786440 | tf_op jit(solution)/shard_map/ppermute | solution.py:145
  34.6 8.4 %collective-permute-start.13 = (bf16[32,4096]{1,0:T(8,128)(2,1)S(1)}, bf16[32,4096]{1,0:T(8,128)(2,1)S(1)}, u32[]{:S(2)}, u32[]{:S(2)}) collective-permute-start(bf16[32,4096]{1,0:T(8,128)(2,1)S(1)} %collective-permute-done.12.refs_4_), channel_id=1, source_target_pairs={{0,4},{1,5},{2,6},{3,7},{4,0},{5,1},{6,2},{7,3},{8,12},{9,13},{10,... | collective-permute-start | bytes 786440 | tf_op jit(solution)/shard_map/ppermute | solution.py:145
  38.1 9.2 %collective-permute-start.7 = (f32[256,1024]{1,0:T(8,128)S(1)}, f32[256,1024]{1,0:T(8,128)S(1)}, u32[]{:S(2)}, u32[]{:S(2)}) collective-permute-start(f32[256,1024]{1,0:T(8,128)S(1)} %shard_map.47), channel_id=1, source_target_pairs={{1,0},{3,2},{5,4},{7,6},{8,9},{10,11},{12,13},{14,15},{17,16},{19,... | collective-permute-start | bytes 3145736 | tf_op jit(solution)/shard_map/ppermute | solution.py:151
  45.9 5.8 %collective-permute-start.17 = (f32[256,1024]{1,0:T(8,128)S(1)}, f32[256,1024]{1,0:T(8,128)S(1)}, u32[]{:S(2)}, u32[]{:S(2)}) collective-permute-start(f32[256,1024]{1,0:T(8,128)S(1)} %shard_map.48), channel_id=1, source_target_pairs={{0,1},{2,3},{4,5},{6,7},{9,8},{11,10},{13,12},{15,14},{16,17},{18,... | collective-permute-start | bytes 3145736 | tf_op jit(solution)/shard_map/ppermute | solution.py:151
  48.3 15.2 %collective-permute-start.8 = (f32[128,1024]{1,0:T(8,128)}, f32[128,1024]{1,0:T(8,128)S(1)}, u32[]{:S(2)}, u32[]{:S(2)}) collective-permute-start(f32[128,1024]{1,0:T(8,128)} %get-tuple-element.14), channel_id=1, source_target_pairs={{0,16},{2,18},{4,20},{6,22},{9,25},{11,27},{13,29},{15,31},{16,0},... | collective-permute-start | bytes 1572872 | tf_op jit(solution)/shard_map/ppermute | solution.py:157
  52.7 10.8 %collective-permute-start.18 = (f32[128,1024]{1,0:T(8,128)}, f32[128,1024]{1,0:T(8,128)S(1)}, u32[]{:S(2)}, u32[]{:S(2)}) collective-permute-start(f32[128,1024]{1,0:T(8,128)} %get-tuple-element.11), channel_id=1, source_target_pairs={{1,17},{3,19},{5,21},{7,23},{8,24},{10,26},{12,28},{14,30},{17,1},... | collective-permute-start | bytes 1572872 | tf_op jit(solution)/shard_map/ppermute | solution.py:157

commit v3 on v2

v3 whole, which is shorter than its diff:
```python
import jax
import jax.numpy as jnp
from jax import lax
from jax.experimental import pallas as pl
from jax.experimental.pallas import tpu as pltpu
from jax.sharding import PartitionSpec as P

AXES = ("src", "tp", "row")


def gathered(tokens, coefficients, gate_weights, up_weights):
    local_rows = tokens.shape[1]
    half_width = tokens.shape[2]
    candidates = coefficients.shape[0]
    sources = coefficients.shape[1]
    per_candidate = local_rows * lax.axis_size("tp")
    out_rows = per_candidate // lax.axis_size("row")
    own_source = lax.axis_index("src")
    picked = (jnp.arange(sources, dtype=jnp.int32) == own_source).astype(jnp.float32)
    own_factors = jnp.sum(coefficients * picked[None, :], axis=1)
    gate_local = gate_weights[0]
    up_local = up_weights[0]
    hidden_width = gate_local.shape[1]
    flat_tokens = tokens.reshape(local_rows, half_width)
    row_block = lax.all_gather(flat_tokens, ("src", "tp"), axis=0, tiled=True)
    owner_ids = jnp.arange(row_block.shape[0], dtype=jnp.int32) // per_candidate
    one_hot = (owner_ids[:, None] == jnp.arange(candidates, dtype=jnp.int32)[None, :]).astype(
        jnp.float32
    )
    factor = jnp.sum(one_hot * own_factors[None, :], axis=1)[:, None]
    gate_part = jnp.dot(row_block, gate_local, preferred_element_type=jnp.float32)
    up_part = jnp.dot(row_block, up_local, preferred_element_type=jnp.float32)
    collected = jnp.concatenate((gate_part, up_part), axis=1) * factor
    summed = lax.psum_scatter(collected, ("src", "row"), scatter_dimension=0, tiled=True)
    hidden = (jax.nn.silu(summed[:, :hidden_width]) * summed[:, hidden_width:]).astype(jnp.bfloat16)
    return hidden.reshape(1, out_rows, hidden_width)


def after(array, *others):
    return lax.optimization_barrier((array,) + others)[0]


def keeps_near(half):
    return lax.axis_index("row") == (lax.axis_index("tp") >> 1) // half


def products(other, own, coefficients, weights, work, half, near=None):
    blocks = other + own
    count = len(blocks)
    rows, depth = blocks[0].shape
    width = weights[0].shape[2]
    span = len(other) * rows
    extra = 0 if near is None else 2

    def kernel(*refs):
        table, block_refs = refs[0], refs[1 : count + 1]
        gate, up = refs[count + 1 : count + 3]
        near_refs = refs[count + 3 : count + 3 + extra]
        outs = refs[count + 3 + extra :]
        source = lax.axis_index("src")
        lhs = jnp.concatenate([ref[...] for ref in block_refs], axis=0)
        factors = (table[1 - source, source], table[source, source])

        def store(targets):
            for start, held in ((0, gate), (width, up)):
                part = jnp.dot(lhs, held[0], preferred_element_type=jnp.float32)
                for i in range(2):
                    targets[i][:, start : start + width] = part[i * span : (i + 1) * span] * factors[i]

        if near is None:
            store(outs)
        else:
            sent, kept = outs[:2], outs[2:]
            mine = keeps_near(half)

            @pl.when(mine)
            def _():
                store(sent)
                for i in range(2):
                    kept[i][...] = near_refs[i][...]

            @pl.when(jnp.logical_not(mine))
            def _():
                store(kept)
                for i in range(2):
                    sent[i][...] = near_refs[i][...]

    whole = pl.BlockSpec(memory_space=pltpu.VMEM)
    result = jax.ShapeDtypeStruct((span, 2 * width), jnp.float32)
    return pl.pallas_call(
        kernel,
        out_shape=[result] * (2 + extra),
        in_specs=[pl.BlockSpec(memory_space=pltpu.SMEM)] + [whole] * (count + 2 + extra),
        out_specs=[whole] * (2 + extra),
        compiler_params=pltpu.CompilerParams(vmem_limit_bytes=24 * 2**20),
        cost_estimate=pl.CostEstimate(
            flops=work * 4 * count * rows * depth * width,
            bytes_accessed=4 * depth * width + 2 * count * rows * depth,
            transcendentals=0,
        ),
    )(coefficients, *blocks, *weights, *(near or ()))


def resident(gate_weights, up_weights, work):
    def kernel(gate, up, gate_out, up_out, sems):
        copies = [
            pltpu.make_async_copy(gate, gate_out, sems.at[0]),
            pltpu.make_async_copy(up, up_out, sems.at[1]),
        ]
        for copy in copies:
            copy.start()
        for copy in copies:
            copy.wait()

    size = gate_weights.size + up_weights.size
    return pl.pallas_call(
        kernel,
        out_shape=[pltpu.VMEM(w.shape, w.dtype) for w in (gate_weights, up_weights)],
        in_specs=[pl.BlockSpec(memory_space=pltpu.HBM)] * 2,
        out_specs=[pl.BlockSpec(memory_space=pltpu.VMEM)] * 2,
        scratch_shapes=[pltpu.SemaphoreType.DMA((2,))],
        compiler_params=pltpu.CompilerParams(vmem_limit_bytes=48 * 2**20),
        cost_estimate=pl.CostEstimate(
            flops=work * size, bytes_accessed=4 * size, transcendentals=0
        ),
    )(gate_weights, up_weights)


def activated(parts, rows):
    width = parts[0].shape[1] // 2

    def kernel(*refs):
        out = refs[-1]
        tp = lax.axis_index("tp")
        for i in range(4):
            span = slice(i * rows, (i + 1) * rows)
            total = refs[0][span, :] + refs[1][span, :] + refs[2][span, :]
            gate, up = total[:, :width], total[:, width:]
            value = (gate / (1 + jnp.exp(-gate)) * up).astype(jnp.bfloat16)
            at = i ^ (tp & 3)
            out[0, pl.ds(pl.multiple_of(at * rows, rows), rows), :] = value

    whole = pl.BlockSpec(memory_space=pltpu.VMEM)
    return pl.pallas_call(
        kernel,
        out_shape=jax.ShapeDtypeStruct((1, 4 * rows, width), jnp.bfloat16),
        in_specs=[whole] * 3,
        out_specs=whole,
        compiler_params=pltpu.CompilerParams(vmem_limit_bytes=24 * 2**20),
    )(*parts)


def paired(mesh):
    tp = mesh.shape["tp"]
    levels = tp // 2
    half = levels // 2

    def place(src, z, x, row):
        return (src * tp + z * 2 + x) * 2 + row

    every = [(s, z, x, r) for s in range(2) for z in range(levels) for x in range(2) for r in range(2)]

    def swap(array, src=0, z=0, x=0, row=0):
        pairs = [(place(*at), place(at[0] ^ src, at[1] ^ z, at[2] ^ x, at[3] ^ row)) for at in every]
        return lax.ppermute(array, AXES, pairs)

    def shards(tokens, coefficients, gate_weights, up_weights):
        rows = tokens.shape[1]
        b0 = tokens[0]
        held = resident(gate_weights, up_weights, 1)
        z3 = swap(b0, z=3)
        z1 = swap(b0, z=1)
        y0 = swap(b0, src=1)
        x0 = swap(b0, x=1)
        d0 = swap(after(x0, y0, held[0]), src=1)
        z2 = swap(z3, z=1)
        y1 = swap(z1, src=1)
        x1 = swap(z1, x=1)
        d1 = swap(after(y1, x1), x=1)
        y3 = swap(z3, src=1)
        x3 = swap(z3, x=1)
        d3 = swap(d0, z=3)
        near = products([y0, d0, y1, d1], [b0, x0, z1, x1], coefficients, held, 1, half)
        y2 = swap(z2, src=1)
        x2 = swap(z2, x=1)
        d2 = swap(d3, z=1)
        sent, sent_own, kept, kept_own = products(
            [y2, d2, y3, d3], [z2, x2, z3, x3], coefficients, held, 1, half, near
        )
        other = kept + swap(sent, row=1)
        core_own = swap(sent_own, row=1)
        from_other = swap(other, src=1)
        return activated((kept_own, core_own, from_other), rows)

    return shards


def solution(mesh):
    fits = mesh.shape["src"] == 2 and mesh.shape["tp"] == 8 and mesh.shape["row"] == 2
    return jax.shard_map(
        paired(mesh) if fits else gathered,
        mesh=mesh,
        in_specs=(P("src", "tp", "row"), P(), P("src", "row", "tp"), P("src", "row", "tp")),
        out_specs=P("src", "row", "tp"),
        check_vma=False,
    )
```

time: 66.1 us -> 62.4 us (0.944); the launches traced: 64.9 us -> 62.3 us
  other arithmetic: 2.04 us -> 0.06 us
  waiting for transfers between devices: 25 us -> 24.3 us
    ppermute x4 -> x0, waiting for transfers between devices: 10.1 us -> none  [the longest x2 10 us: owner_src(): return lax.ppermute(array, AXES, pairs)]
    ppermute x15 -> x18, waiting for transfers between devices: 15 us -> 24.3 us  [swap(): return lax.ppermute(array, AXES, pairs)]
    ppermute x15 -> x18, starting transfers between devices: 20.3 us -> 27.6 us  [swap(): return lax.ppermute(array, AXES, pairs)]
    ppermute x4 -> x0, starting transfers between devices: 6.73 us -> none  [the longest x2 4.1 us: owner_src(): return lax.ppermute(array, AXES, pairs)]
    add x2 -> x1, other arithmetic: 1.96 us -> 0.06 us  [shards(): other = kept + swap(sent, row=1)]
  transfers between devices with their start and end apart: 19 -> 18, of which waited for: 9 -> 8; matrix products, arithmetic and copies ran while one was open for 3% -> 0% of each run, Pallas kernels for 14% -> 10%
where the time goes in v3:
time: 62.4 us; the launch traced here: 62.3 us
  starting transfers between devices  27.6 us (44%)
  waiting for transfers between devices  24.3 us (39%)
  Pallas kernels  10.2 us (16%)
    ppermute x18, starting transfers between devices, swap(): return lax.ppermute(array, AXES, pairs)  27.6 us
    ppermute x18, waiting for transfers between devices, swap(): return lax.ppermute(array, AXES, pairs)  24.3 us
    pallas_call x2, Pallas kernels, products(): pl.pallas_call(kernel, out_shape=[result] * (2 + extra), in_specs=[pl.Blo...  5.93 us
    pallas_call x1, Pallas kernels, resident(): pl.pallas_call(kernel, out_shape=[pltpu.VMEM(w.shape, w.dtype) for w in (...  3.48 us
  transfers between devices with their start and end apart: 18, of which 8 were waited for; matrix products, arithmetic and copies ran while one was open for 0% of the time, Pallas kernels for 10%

profile of v3, /device:TPU:0, one launch (start us, length us, event | category | flops | bytes accessed | tf_op | source)
XLA Modules:
  0.0 62.3 jit_solution(5876705934652537662)
XLA Ops:
  0.0 0.0 copy-start
  0.0 0.0 copy-start.1
  0.0 3.0 %collective-permute-start.11 = (bf16[32,4096]{1,0:T(8,128)(2,1)}, bf16[32,4096]{1,0:T(8,128)(2,1)S(1)}, u32[]{:S(2)}, u32[]{:S(2)}) collective-permute-start(bf16[32,4096]{1,0:T(8,128)(2,1)} %bitcast.1), channel_id=1, source_target_pairs={{0,4},{1,5},{2,6},{3,7},{4,0},{5,1},{6,2},{7,3},{8,12},{9,13},{10,... | collective-permute-start | bytes 786440 | tf_op jit(solution)/shard_map/ppermute | solution.py:165
  3.0 1.5 %collective-permute-start.4 = (bf16[32,4096]{1,0:T(8,128)(2,1)}, bf16[32,4096]{1,0:T(8,128)(2,1)S(1)}, u32[]{:S(2)}, u32[]{:S(2)}) collective-permute-start(bf16[32,4096]{1,0:T(8,128)(2,1)} %bitcast.2), channel_id=1, source_target_pairs={{0,16},{1,17},{2,18},{3,19},{4,20},{5,21},{6,22},{7,23},{8,24},{9,... | collective-permute-start | bytes 786440 | tf_op jit(solution)/shard_map/ppermute | solution.py:165
  4.5 1.5 %collective-permute-start.3 = (bf16[32,4096]{1,0:T(8,128)(2,1)}, bf16[32,4096]{1,0:T(8,128)(2,1)S(1)}, u32[]{:S(2)}, u32[]{:S(2)}) collective-permute-start(bf16[32,4096]{1,0:T(8,128)(2,1)} %bitcast.3), channel_id=1, source_target_pairs={{0,2},{1,3},{2,0},{3,1},{4,6},{5,7},{6,4},{7,5},{8,10},{9,11},{10,... | collective-permute-start | bytes 786440 | tf_op jit(solution)/shard_map/ppermute | solution.py:165
  6.0 2.5 %collective-permute-start = (bf16[32,4096]{1,0:T(8,128)(2,1)}, bf16[32,4096]{1,0:T(8,128)(2,1)S(1)}, u32[]{:S(2)}, u32[]{:S(2)}) collective-permute-start(bf16[32,4096]{1,0:T(8,128)(2,1)} %bitcast.4), channel_id=1, source_target_pairs={{0,12},{1,13},{2,14},{3,15},{4,8},{5,9},{6,10},{7,11},{8,4},{9,5},... | collective-permute-start | bytes 786440 | tf_op jit(solution)/shard_map/ppermute | solution.py:165
  8.5 3.5 %shard_map.46 = (bf16[1,4096,512]{2,1,0:T(8,128)(2,1)S(1)}, bf16[1,4096,512]{2,1,0:T(8,128)(2,1)S(1)}) custom-call(bf16[1,4096,512]{2,1,0:T(8,128)(2,1)} %gate.1, bf16[1,4096,512]{2,1,0:T(8,128)(2,1)} %up.1), custom_call_target="tpu_custom_call" | custom-call | flops 4194304 | bytes 16777216 | tf_op jit(solution)/shard_map/pallas_call | solution.py:116
  12.0 0.0 collective-permute-done.11.refs_7_
  12.0 0.6 collective-permute-start.13
  12.6 0.5 collective-permute-start.12
  13.1 0.0 collective-permute-done.4.refs_1_
  13.1 0.0 collective-permute-done.3.refs_6_
  13.1 1.5 %collective-permute-start.5 = (bf16[32,4096]{1,0:T(8,128)(2,1)S(1)}, bf16[32,4096]{1,0:T(8,128)(2,1)S(1)}, u32[]{:S(2)}, u32[]{:S(2)}) collective-permute-start(bf16[32,4096]{1,0:T(8,128)(2,1)S(1)} %collective-permute-done.3.refs_6_), channel_id=1, source_target_pairs={{0,16},{1,17},{2,18},{3,19},{4,20},{5,21},{6,22},{7,23},{8,24},{9,... | collective-permute-start | bytes 786440 | tf_op jit(solution)/shard_map/ppermute | solution.py:165
  14.7 2.8 %collective-permute-done.refs_7_ = bf16[32,4096]{1,0:T(8,128)(2,1)S(1)} collective-permute-done((bf16[32,4096]{1,0:T(8,128)(2,1)}, bf16[32,4096]{1,0:T(8,128)(2,1)S(1)}, u32[]{:S(2)}, u32[]{:S(2)}) %collective-permute-start) | collective-permute-done | bytes 262176 | tf_op jit(solution)/shard_map/ppermute | solution.py:165
  17.5 3.1 %collective-permute-start.1 = (bf16[32,4096]{1,0:T(8,128)(2,1)S(1)}, bf16[32,4096]{1,0:T(8,128)(2,1)S(1)}, u32[]{:S(2)}, u32[]{:S(2)}) collective-permute-start(bf16[32,4096]{1,0:T(8,128)(2,1)S(1)} %collective-permute-done.refs_7_), channel_id=1, source_target_pairs={{0,4},{1,5},{2,6},{3,7},{4,0},{5,1},{6,2},{7,3},{8,12},{9,13},{10,... | collective-permute-start | bytes 786440 | tf_op jit(solution)/shard_map/ppermute | solution.py:165
  20.5 0.0 collective-permute-done.13.refs_8_
  20.5 1.3 %collective-permute-done.12.refs_3_ = bf16[32,4096]{1,0:T(8,128)(2,1)S(1)} collective-permute-done((bf16[32,4096]{1,0:T(8,128)(2,1)S(1)}, bf16[32,4096]{1,0:T(8,128)(2,1)S(1)}, u32[]{:S(2)}, u32[]{:S(2)}) %collective-permute-start.12) | collective-permute-done | bytes 262176 | tf_op jit(solution)/shard_map/ppermute | solution.py:165
  21.9 1.5 %collective-permute-start.14 = (bf16[32,4096]{1,0:T(8,128)(2,1)S(1)}, bf16[32,4096]{1,0:T(8,128)(2,1)S(1)}, u32[]{:S(2)}, u32[]{:S(2)}) collective-permute-start(bf16[32,4096]{1,0:T(8,128)(2,1)S(1)} %collective-permute-done.12.refs_3_), channel_id=1, source_target_pairs={{0,2},{1,3},{2,0},{3,1},{4,6},{5,7},{6,4},{7,5},{8,10},{9,11},{10,... | collective-permute-start | bytes 786440 | tf_op jit(solution)/shard_map/ppermute | solution.py:165
  23.4 1.5 %collective-permute-done.5.refs_2_ = bf16[32,4096]{1,0:T(8,128)(2,1)S(1)} collective-permute-done((bf16[32,4096]{1,0:T(8,128)(2,1)S(1)}, bf16[32,4096]{1,0:T(8,128)(2,1)S(1)}, u32[]{:S(2)}, u32[]{:S(2)}) %collective-permute-start.5) | collective-permute-done | bytes 262176 | tf_op jit(solution)/shard_map/ppermute | solution.py:165
  24.9 4.7 %collective-permute-start.6 = (bf16[32,4096]{1,0:T(8,128)(2,1)S(1)}, bf16[32,4096]{1,0:T(8,128)(2,1)S(1)}, u32[]{:S(2)}, u32[]{:S(2)}) collective-permute-start(bf16[32,4096]{1,0:T(8,128)(2,1)S(1)} %collective-permute-done.5.refs_2_), channel_id=1, source_target_pairs={{0,12},{1,13},{2,14},{3,15},{4,8},{5,9},{6,10},{7,11},{8,4},{9,5},... | collective-permute-start | bytes 786440 | tf_op jit(solution)/shard_map/ppermute | solution.py:165
  29.6 0.5 collective-permute-start.10
  30.1 2.3 %collective-permute-start.8 = (bf16[32,4096]{1,0:T(8,128)(2,1)S(1)}, bf16[32,4096]{1,0:T(8,128)(2,1)S(1)}, u32[]{:S(2)}, u32[]{:S(2)}) collective-permute-start(bf16[32,4096]{1,0:T(8,128)(2,1)S(1)} %collective-permute-done.refs_7_), channel_id=1, source_target_pairs={{0,16},{1,17},{2,18},{3,19},{4,20},{5,21},{6,22},{7,23},{8,24},{9,... | collective-permute-start | bytes 786440 | tf_op jit(solution)/shard_map/ppermute | solution.py:165
  32.5 0.0 collective-permute-done.1.refs_5_
  32.5 1.5 %collective-permute-start.9 = (bf16[32,4096]{1,0:T(8,128)(2,1)S(1)}, bf16[32,4096]{1,0:T(8,128)(2,1)S(1)}, u32[]{:S(2)}, u32[]{:S(2)}) collective-permute-start(bf16[32,4096]{1,0:T(8,128)(2,1)S(1)} %collective-permute-done.1.refs_5_), channel_id=1, source_target_pairs={{0,2},{1,3},{2,0},{3,1},{4,6},{5,7},{6,4},{7,5},{8,10},{9,11},{10,... | collective-permute-start | bytes 786440 | tf_op jit(solution)/shard_map/ppermute | solution.py:165
  34.0 0.0 collective-permute-done.14.refs_4_
  34.0 0.0 collective-permute-start.2
  34.0 2.0 %collective-permute-done.6.refs_4_ = bf16[32,4096]{1,0:T(8,128)(2,1)S(1)} collective-permute-done((bf16[32,4096]{1,0:T(8,128)(2,1)S(1)}, bf16[32,4096]{1,0:T(8,128)(2,1)S(1)}, u32[]{:S(2)}, u32[]{:S(2)}) %collective-permute-start.6) | collective-permute-done | bytes 262176 | tf_op jit(solution)/shard_map/ppermute | solution.py:165
  36.0 0.7 %collective-permute-start.7 = (bf16[32,4096]{1,0:T(8,128)(2,1)S(1)}, bf16[32,4096]{1,0:T(8,128)(2,1)S(1)}, u32[]{:S(2)}, u32[]{:S(2)}) collective-permute-start(bf16[32,4096]{1,0:T(8,128)(2,1)S(1)} %collective-permute-done.6.refs_4_), channel_id=1, source_target_pairs={{0,4},{1,5},{2,6},{3,7},{4,0},{5,1},{6,2},{7,3},{8,12},{9,13},{10,... | collective-permute-start | bytes 786440 | tf_op jit(solution)/shard_map/ppermute | solution.py:165
  36.7 0.0 copy-done
  36.7 0.0 copy-done.1
  36.7 2.9 %shard_map.47 = (f32[128,1024]{1,0:T(8,128)S(1)}, f32[128,1024]{1,0:T(8,128)S(1)}) custom-call(f32[2,2]{1,0:T(2,128)S(1)} %copy-done.1, bf16[32,4096]{1,0:T(8,128)(2,1)S(1)} %collective-permute-done.4.refs_1_, bf16[32,4096]{1,0:T(8,128)(2,1)S(1)} %collective-permute-done.5.refs_2_, bf16[32,4096]{1,0:T(8,128)(2,1)S(1)} %collective-permute-done.12.refs_3_, ...), custom_call_target="tpu_custom_call" | custom-call | flops 2147483648 | bytes 10485760 | tf_op jit(solution)/shard_map/pallas_call | solution.py:90
  39.6 0.0 collective-permute-done.10.refs_8_
  39.6 0.0 collective-permute-done.8.refs_3_
  39.6 0.0 collective-permute-done.9.refs_6_
  39.6 0.7 %collective-permute-done.2.refs_1_ = bf16[32,4096]{1,0:T(8,128)(2,1)S(1)} collective-permute-done((bf16[32,4096]{1,0:T(8,128)(2,1)S(1)}, bf16[32,4096]{1,0:T(8,128)(2,1)S(1)}, u32[]{:S(2)}, u32[]{:S(2)}) %collective-permute-start.2) | collective-permute-done | bytes 262176 | tf_op jit(solution)/shard_map/ppermute | solution.py:165
  40.3 2.0 %collective-permute-done.7.refs_2_ = bf16[32,4096]{1,0:T(8,128)(2,1)S(1)} collective-permute-done((bf16[32,4096]{1,0:T(8,128)(2,1)S(1)}, bf16[32,4096]{1,0:T(8,128)(2,1)S(1)}, u32[]{:S(2)}, u32[]{:S(2)}) %collective-permute-start.7) | collective-permute-done | bytes 262176 | tf_op jit(solution)/shard_map/ppermute | solution.py:165
  42.4 3.0 %shard_map.48 = (f32[128,1024]{1,0:T(8,128)S(1)}, f32[128,1024]{1,0:T(8,128)S(1)}, f32[128,1024]{1,0:T(8,128)S(1)}, f32[128,1024]{1,0:T(8,128)S(1)}) custom-call(f32[2,2]{1,0:T(2,128)S(1)} %copy-done.1, bf16[32,4096]{1,0:T(8,128)(2,1)S(1)} %collective-permute-done.2.refs_1_, bf16[32,4096]{1,0:T(8,128)(2,1)S(1)} %collective-permute-done.7.refs_2_, ...), custom_call_target="tpu_custom_call" | custom-call | flops 2147483648 | bytes 10485760 | tf_op jit(solution)/shard_map/pallas_call | solution.py:90
  45.4 0.1 collective-permute-start.16
  45.5 0.5 collective-permute-start.15
  46.0 1.4 %collective-permute-done.16 = f32[128,1024]{1,0:T(8,128)S(1)} collective-permute-done((f32[128,1024]{1,0:T(8,128)S(1)}, f32[128,1024]{1,0:T(8,128)S(1)}, u32[]{:S(2)}, u32[]{:S(2)}) %collective-permute-start.16) | collective-permute-done | bytes 524320 | tf_op jit(solution)/shard_map/ppermute | solution.py:165
  47.4 0.1 add.3
  47.4 1.6 %collective-permute-start.17 = (f32[128,1024]{1,0:T(8,128)S(1)}, f32[128,1024]{1,0:T(8,128)S(1)}, u32[]{:S(2)}, u32[]{:S(2)}) collective-permute-start(f32[128,1024]{1,0:T(8,128)S(1)} %add.3), channel_id=1, source_target_pairs={{0,16},{1,17},{2,18},{3,19},{4,20},{5,21},{6,22},{7,23},{8,24},{9,... | collective-permute-start | bytes 1572872 | tf_op jit(solution)/shard_map/ppermute | solution.py:165
  49.0 0.0 collective-permute-done.15.refs_1_
  49.0 12.4 %collective-permute-done.17.refs_2_ = f32[128,1024]{1,0:T(8,128)S(1)} collective-permute-done((f32[128,1024]{1,0:T(8,128)S(1)}, f32[128,1024]{1,0:T(8,128)S(1)}, u32[]{:S(2)}, u32[]{:S(2)}) %collective-permute-start.17) | collective-permute-done | bytes 524320 | tf_op jit(solution)/shard_map/ppermute | solution.py:165
  61.5 0.8 %shard_map.49 = bf16[1,128,512]{2,1,0:T(8,128)(2,1)} custom-call(f32[128,1024]{1,0:T(8,128)S(1)} %get-tuple-element.21.refs_0_, f32[128,1024]{1,0:T(8,128)S(1)} %collective-permute-done.15.refs_1_, f32[128,1024]{1,0:T(8,128)S(1)} %collective-permute-done.17.refs_2_), custom_call_target="tpu_custom_call" | custom-call | tf_op jit(solution)/shard_map/pallas_call | solution.py:144
Async XLA Ops:
  0.0 36.7 %copy-start = (bf16[1,32,4096]{2,1,0:T(8,128)(2,1)S(1)}, bf16[1,32,4096]{2,1,0:T(8,128)(2,1)}, u32[]{:S(2)}) copy-start(bf16[1,32,4096]{2,1,0:T(8,128)(2,1)} %param.4) | copy-start | bytes 786436
  0.0 36.7 %copy-start.1 = (f32[2,2]{1,0:T(2,128)S(1)}, f32[2,2]{1,0:T(2,128)}, u32[]{:S(2)}) copy-start(f32[2,2]{1,0:T(2,128)} %refs_0_.3) | copy-start | bytes 52
  0.0 12.0 %collective-permute-start.11 = (bf16[32,4096]{1,0:T(8,128)(2,1)}, bf16[32,4096]{1,0:T(8,128)(2,1)S(1)}, u32[]{:S(2)}, u32[]{:S(2)}) collective-permute-start(bf16[32,4096]{1,0:T(8,128)(2,1)} %bitcast.1), channel_id=1, source_target_pairs={{0,4},{1,5},{2,6},{3,7},{4,0},{5,1},{6,2},{7,3},{8,12},{9,13},{10,... | collective-permute-start | bytes 786440 | tf_op jit(solution)/shard_map/ppermute | solution.py:165
  3.0 10.1 %collective-permute-start.4 = (bf16[32,4096]{1,0:T(8,128)(2,1)}, bf16[32,4096]{1,0:T(8,128)(2,1)S(1)}, u32[]{:S(2)}, u32[]{:S(2)}) collective-permute-start(bf16[32,4096]{1,0:T(8,128)(2,1)} %bitcast.2), channel_id=1, source_target_pairs={{0,16},{1,17},{2,18},{3,19},{4,20},{5,21},{6,22},{7,23},{8,24},{9,... | collective-permute-start | bytes 786440 | tf_op jit(solution)/shard_map/ppermute | solution.py:165
  4.5 8.6 %collective-permute-start.3 = (bf16[32,4096]{1,0:T(8,128)(2,1)}, bf16[32,4096]{1,0:T(8,128)(2,1)S(1)}, u32[]{:S(2)}, u32[]{:S(2)}) collective-permute-start(bf16[32,4096]{1,0:T(8,128)(2,1)} %bitcast.3), channel_id=1, source_target_pairs={{0,2},{1,3},{2,0},{3,1},{4,6},{5,7},{6,4},{7,5},{8,10},{9,11},{10,... | collective-permute-start | bytes 786440 | tf_op jit(solution)/shard_map/ppermute | solution.py:165
  6.0 11.4 %collective-permute-start = (bf16[32,4096]{1,0:T(8,128)(2,1)}, bf16[32,4096]{1,0:T(8,128)(2,1)S(1)}, u32[]{:S(2)}, u32[]{:S(2)}) collective-permute-start(bf16[32,4096]{1,0:T(8,128)(2,1)} %bitcast.4), channel_id=1, source_target_pairs={{0,12},{1,13},{2,14},{3,15},{4,8},{5,9},{6,10},{7,11},{8,4},{9,5},... | collective-permute-start | bytes 786440 | tf_op jit(solution)/shard_map/ppermute | solution.py:165
  12.0 8.5 %collective-permute-start.13 = (bf16[32,4096]{1,0:T(8,128)(2,1)S(1)}, bf16[32,4096]{1,0:T(8,128)(2,1)S(1)}, u32[]{:S(2)}, u32[]{:S(2)}) collective-permute-start(bf16[32,4096]{1,0:T(8,128)(2,1)S(1)} %collective-permute-done.11.refs_7_), channel_id=1, source_target_pairs={{0,2},{1,3},{2,0},{3,1},{4,6},{5,7},{6,4},{7,5},{8,10},{9,11},{10,... | collective-permute-start | bytes 786440 | tf_op jit(solution)/shard_map/ppermute | solution.py:165
  12.6 9.2 %collective-permute-start.12 = (bf16[32,4096]{1,0:T(8,128)(2,1)S(1)}, bf16[32,4096]{1,0:T(8,128)(2,1)S(1)}, u32[]{:S(2)}, u32[]{:S(2)}) collective-permute-start(bf16[32,4096]{1,0:T(8,128)(2,1)S(1)} %collective-permute-done.11.refs_7_), channel_id=1, source_target_pairs={{0,16},{1,17},{2,18},{3,19},{4,20},{5,21},{6,22},{7,23},{8,24},{9,... | collective-permute-start | bytes 786440 | tf_op jit(solution)/shard_map/ppermute | solution.py:165
  13.1 11.8 %collective-permute-start.5 = (bf16[32,4096]{1,0:T(8,128)(2,1)S(1)}, bf16[32,4096]{1,0:T(8,128)(2,1)S(1)}, u32[]{:S(2)}, u32[]{:S(2)}) collective-permute-start(bf16[32,4096]{1,0:T(8,128)(2,1)S(1)} %collective-permute-done.3.refs_6_), channel_id=1, source_target_pairs={{0,16},{1,17},{2,18},{3,19},{4,20},{5,21},{6,22},{7,23},{8,24},{9,... | collective-permute-start | bytes 786440 | tf_op jit(solution)/shard_map/ppermute | solution.py:165
  17.5 15.0 %collective-permute-start.1 = (bf16[32,4096]{1,0:T(8,128)(2,1)S(1)}, bf16[32,4096]{1,0:T(8,128)(2,1)S(1)}, u32[]{:S(2)}, u32[]{:S(2)}) collective-permute-start(bf16[32,4096]{1,0:T(8,128)(2,1)S(1)} %collective-permute-done.refs_7_), channel_id=1, source_target_pairs={{0,4},{1,5},{2,6},{3,7},{4,0},{5,1},{6,2},{7,3},{8,12},{9,13},{10,... | collective-permute-start | bytes 786440 | tf_op jit(solution)/shard_map/ppermute | solution.py:165
  21.9 12.1 %collective-permute-start.14 = (bf16[32,4096]{1,0:T(8,128)(2,1)S(1)}, bf16[32,4096]{1,0:T(8,128)(2,1)S(1)}, u32[]{:S(2)}, u32[]{:S(2)}) collective-permute-start(bf16[32,4096]{1,0:T(8,128)(2,1)S(1)} %collective-permute-done.12.refs_3_), channel_id=1, source_target_pairs={{0,2},{1,3},{2,0},{3,1},{4,6},{5,7},{6,4},{7,5},{8,10},{9,11},{10,... | collective-permute-start | bytes 786440 | tf_op jit(solution)/shard_map/ppermute | solution.py:165
  24.9 11.1 %collective-permute-start.6 = (bf16[32,4096]{1,0:T(8,128)(2,1)S(1)}, bf16[32,4096]{1,0:T(8,128)(2,1)S(1)}, u32[]{:S(2)}, u32[]{:S(2)}) collective-permute-start(bf16[32,4096]{1,0:T(8,128)(2,1)S(1)} %collective-permute-done.5.refs_2_), channel_id=1, source_target_pairs={{0,12},{1,13},{2,14},{3,15},{4,8},{5,9},{6,10},{7,11},{8,4},{9,5},... | collective-permute-start | bytes 786440 | tf_op jit(solution)/shard_map/ppermute | solution.py:165
  29.6 10.0 %collective-permute-start.10 = (bf16[32,4096]{1,0:T(8,128)(2,1)S(1)}, bf16[32,4096]{1,0:T(8,128)(2,1)S(1)}, u32[]{:S(2)}, u32[]{:S(2)}) collective-permute-start(bf16[32,4096]{1,0:T(8,128)(2,1)S(1)} %collective-permute-done.refs_7_), channel_id=1, source_target_pairs={{0,2},{1,3},{2,0},{3,1},{4,6},{5,7},{6,4},{7,5},{8,10},{9,11},{10,... | collective-permute-start | bytes 786440 | tf_op jit(solution)/shard_map/ppermute | solution.py:165
  30.1 9.5 %collective-permute-start.8 = (bf16[32,4096]{1,0:T(8,128)(2,1)S(1)}, bf16[32,4096]{1,0:T(8,128)(2,1)S(1)}, u32[]{:S(2)}, u32[]{:S(2)}) collective-permute-start(bf16[32,4096]{1,0:T(8,128)(2,1)S(1)} %collective-permute-done.refs_7_), channel_id=1, source_target_pairs={{0,16},{1,17},{2,18},{3,19},{4,20},{5,21},{6,22},{7,23},{8,24},{9,... | collective-permute-start | bytes 786440 | tf_op jit(solution)/shard_map/ppermute | solution.py:165
  32.5 7.2 %collective-permute-start.9 = (bf16[32,4096]{1,0:T(8,128)(2,1)S(1)}, bf16[32,4096]{1,0:T(8,128)(2,1)S(1)}, u32[]{:S(2)}, u32[]{:S(2)}) collective-permute-start(bf16[32,4096]{1,0:T(8,128)(2,1)S(1)} %collective-permute-done.1.refs_5_), channel_id=1, source_target_pairs={{0,2},{1,3},{2,0},{3,1},{4,6},{5,7},{6,4},{7,5},{8,10},{9,11},{10,... | collective-permute-start | bytes 786440 | tf_op jit(solution)/shard_map/ppermute | solution.py:165
  34.0 6.4 %collective-permute-start.2 = (bf16[32,4096]{1,0:T(8,128)(2,1)S(1)}, bf16[32,4096]{1,0:T(8,128)(2,1)S(1)}, u32[]{:S(2)}, u32[]{:S(2)}) collective-permute-start(bf16[32,4096]{1,0:T(8,128)(2,1)S(1)} %collective-permute-done.1.refs_5_), channel_id=1, source_target_pairs={{0,16},{1,17},{2,18},{3,19},{4,20},{5,21},{6,22},{7,23},{8,24},{9,... | collective-permute-start | bytes 786440 | tf_op jit(solution)/shard_map/ppermute | solution.py:165
  36.0 6.4 %collective-permute-start.7 = (bf16[32,4096]{1,0:T(8,128)(2,1)S(1)}, bf16[32,4096]{1,0:T(8,128)(2,1)S(1)}, u32[]{:S(2)}, u32[]{:S(2)}) collective-permute-start(bf16[32,4096]{1,0:T(8,128)(2,1)S(1)} %collective-permute-done.6.refs_4_), channel_id=1, source_target_pairs={{0,4},{1,5},{2,6},{3,7},{4,0},{5,1},{6,2},{7,3},{8,12},{9,13},{10,... | collective-permute-start | bytes 786440 | tf_op jit(solution)/shard_map/ppermute | solution.py:165
  45.4 2.0 %collective-permute-start.16 = (f32[128,1024]{1,0:T(8,128)S(1)}, f32[128,1024]{1,0:T(8,128)S(1)}, u32[]{:S(2)}, u32[]{:S(2)}) collective-permute-start(f32[128,1024]{1,0:T(8,128)S(1)} %get-tuple-element.24), channel_id=1, source_target_pairs={{0,1},{1,0},{2,3},{3,2},{4,5},{5,4},{6,7},{7,6},{8,9},{9,8},{10,11... | collective-permute-start | bytes 1572872 | tf_op jit(solution)/shard_map/ppermute | solution.py:165
  45.5 3.6 %collective-permute-start.15 = (f32[128,1024]{1,0:T(8,128)S(1)}, f32[128,1024]{1,0:T(8,128)S(1)}, u32[]{:S(2)}, u32[]{:S(2)}) collective-permute-start(f32[128,1024]{1,0:T(8,128)S(1)} %get-tuple-element.22), channel_id=1, source_target_pairs={{0,1},{1,0},{2,3},{3,2},{4,5},{5,4},{6,7},{7,6},{8,9},{9,8},{10,11... | collective-permute-start | bytes 1572872 | tf_op jit(solution)/shard_map/ppermute | solution.py:165
  47.4 14.0 %collective-permute-start.17 = (f32[128,1024]{1,0:T(8,128)S(1)}, f32[128,1024]{1,0:T(8,128)S(1)}, u32[]{:S(2)}, u32[]{:S(2)}) collective-permute-start(f32[128,1024]{1,0:T(8,128)S(1)} %add.3), channel_id=1, source_target_pairs={{0,16},{1,17},{2,18},{3,19},{4,20},{5,21},{6,22},{7,23},{8,24},{9,... | collective-permute-start | bytes 1572872 | tf_op jit(solution)/shard_map/ppermute | solution.py:165

commit v4 on v3

--- a/solution.py
+++ b/solution.py
@@ -126,16 +126,74 @@
     )(gate_weights, up_weights)
 
 
-def activated(parts, rows):
-    width = parts[0].shape[1] // 2
-
-    def kernel(*refs):
-        out = refs[-1]
+SEGMENTS = 7
+STEPS = 4016
+FIELD = 128
+SHIFT = 125
+
+
+def coded(kept, received):
+    rows, width = kept.shape
+    side = width // 2
+
+    def kernel(kept_ref, received_ref, out):
+        lane = lax.broadcasted_iota(jnp.int32, (rows, FIELD), 1)
+        scales = []
+        for start in (0, side):
+            columns = slice(start, start + side)
+            total = kept_ref[:, columns] + received_ref[:, columns]
+            size = jnp.abs(total)
+            top = jnp.maximum(jnp.max(size, axis=1, keepdims=True), 1e-30) * 1.01
+            top = top.astype(jnp.bfloat16).astype(jnp.float32)
+            scales.append(top)
+            part = size * (1 / top)
+            level = part * 2.0**SEGMENTS
+            for k in range(1, SEGMENTS):
+                level = jnp.minimum(level, part * 2.0 ** (SEGMENTS - k) + k)
+            number = jnp.floor(level * STEPS + 0.5)
+            power = jnp.floor(number * (1 / FIELD))
+            fraction = (number - power * FIELD) * (1 / FIELD)
+            value = jnp.exp2(power - SHIFT) * (1 + fraction)
+            out[:, columns] = jnp.where(total < 0, -value, value).astype(jnp.bfloat16)
+        out[:, width:] = jnp.where(lane < FIELD // 2, scales[0], scales[1]).astype(jnp.bfloat16)
+
+    whole = pl.BlockSpec(memory_space=pltpu.VMEM)
+    return pl.pallas_call(
+        kernel,
+        out_shape=jax.ShapeDtypeStruct((rows, width + FIELD), jnp.bfloat16),
+        in_specs=[whole] * 2,
+        out_specs=whole,
+        compiler_params=pltpu.CompilerParams(vmem_limit_bytes=24 * 2**20),
+    )(kept, received)
+
+
+def decoded(values, scale):
+    values = values.astype(jnp.float32)
+    size = jnp.abs(values)
+    power = jnp.floor(jnp.log2(size) + 0.001)
+    fraction = jnp.floor((size * jnp.exp2(-power) - 1) * FIELD + 0.5)
+    level = ((power + SHIFT) * FIELD + fraction) * (1 / STEPS)
+    part = level * 2.0**-SEGMENTS
+    for k in range(1, SEGMENTS):
+        part = jnp.maximum(part, (level - k) * 2.0 ** (k - SEGMENTS))
+    return jnp.where(values < 0, -part, part) * scale
+
+
+def activated(kept, received, code, rows):
+    width = kept.shape[1] // 2
+
+    def kernel(kept_ref, received_ref, code_ref, out):
         tp = lax.axis_index("tp")
         for i in range(4):
             span = slice(i * rows, (i + 1) * rows)
-            total = refs[0][span, :] + refs[1][span, :] + refs[2][span, :]
-            gate, up = total[:, :width], total[:, width:]
+            total = []
+            for j in range(2):
+                columns = slice(j * width, (j + 1) * width)
+                at = 2 * width + j * (FIELD // 2)
+                scale = code_ref[span, at : at + 1].astype(jnp.float32)
+                own = kept_ref[span, columns] + received_ref[span, columns]
+                total.append(own + decoded(code_ref[span, columns], scale))
+            gate, up = total
             value = (gate / (1 + jnp.exp(-gate)) * up).astype(jnp.bfloat16)
             at = i ^ (tp & 3)
             out[0, pl.ds(pl.multiple_of(at * rows, rows), rows), :] = value
@@ -147,7 +205,7 @@
         in_specs=[whole] * 3,
         out_specs=whole,
         compiler_params=pltpu.CompilerParams(vmem_limit_bytes=24 * 2**20),
-    )(*parts)
+    )(kept, received, code)
 
 
 def paired(mesh):
@@ -176,7 +234,7 @@
         z2 = swap(z3, z=1)
         y1 = swap(z1, src=1)
         x1 = swap(z1, x=1)
-        d1 = swap(after(y1, x1), x=1)
+        d1 = swap(after(y1, y1), x=1)
         y3 = swap(z3, src=1)
         x3 = swap(z3, x=1)
         d3 = swap(d0, z=3)
@@ -187,10 +245,10 @@
         sent, sent_own, kept, kept_own = products(
             [y2, d2, y3, d3], [z2, x2, z3, x3], coefficients, held, 1, half, near
         )
-        other = kept + swap(sent, row=1)
+        other = coded(kept, swap(sent, row=1))
         core_own = swap(sent_own, row=1)
         from_other = swap(other, src=1)
-        return activated((kept_own, core_own, from_other), rows)
+        return activated(kept_own, core_own, from_other, rows)
 
     return shards
 

time: 62.4 us -> 58.1 us (0.931)
  waiting for transfers between devices: 24.3 us -> 18.5 us
  Pallas kernels: 10.2 us -> 12 us
    ppermute x18, waiting for transfers between devices: 24.3 us -> 18.5 us  [swap(): return lax.ppermute(array, AXES, pairs)]
    pallas_call x0 -> x1, Pallas kernels: none -> 0.97 us  [coded(): pl.pallas_call(kernel, out_shape=jax.ShapeDtypeStruct((rows, width + FIEL...]
    pallas_call x1, Pallas kernels: 0.78 us -> 1.57 us  [activated(): pl.pallas_call(kernel, out_shape=jax.ShapeDtypeStruct((1, 4 * rows, width...]
  transfers between devices with their start and end apart: 18 -> 18, of which waited for: 8 -> 7; matrix products, arithmetic and copies ran while one was open for 0% -> 0% of each run, Pallas kernels for 10% -> 13%
where the time goes in v4:
time: 58.1 us; the launch traced here: 58 us
  starting transfers between devices  27.4 us (47%)
  waiting for transfers between devices  18.5 us (32%)
  Pallas kernels  12 us (21%)
    ppermute x18, starting transfers between devices, swap(): return lax.ppermute(array, AXES, pairs)  27.4 us
    ppermute x18, waiting for transfers between devices, swap(): return lax.ppermute(array, AXES, pairs)  18.5 us
    pallas_call x2, Pallas kernels, products(): pl.pallas_call(kernel, out_shape=[result] * (2 + extra), in_specs=[pl.Blo...  5.93 us
    pallas_call x1, Pallas kernels, resident(): pl.pallas_call(kernel, out_shape=[pltpu.VMEM(w.shape, w.dtype) for w in (...  3.48 us
    pallas_call x1, Pallas kernels, activated(): pl.pallas_call(kernel, out_shape=jax.ShapeDtypeStruct((1, 4 * rows, width...  1.57 us
  transfers between devices with their start and end apart: 18, of which 7 were waited for; matrix products, arithmetic and copies ran while one was open for 0% of the time, Pallas kernels for 13%

profile of v4, /device:TPU:0, one launch (start us, length us, event | category | flops | bytes accessed | tf_op | source)
XLA Modules:
  0.0 58.0 jit_solution(12990050112382345904)
XLA Ops:
  0.0 0.0 copy-start
  0.0 0.0 copy-start.1
  0.0 3.0 %collective-permute-start.11 = (bf16[32,4096]{1,0:T(8,128)(2,1)}, bf16[32,4096]{1,0:T(8,128)(2,1)S(1)}, u32[]{:S(2)}, u32[]{:S(2)}) collective-permute-start(bf16[32,4096]{1,0:T(8,128)(2,1)} %bitcast.1), channel_id=1, source_target_pairs={{0,4},{1,5},{2,6},{3,7},{4,0},{5,1},{6,2},{7,3},{8,12},{9,13},{10,... | collective-permute-start | bytes 786440 | tf_op jit(solution)/shard_map/ppermute | solution.py:223
  3.0 1.5 %collective-permute-start.4 = (bf16[32,4096]{1,0:T(8,128)(2,1)}, bf16[32,4096]{1,0:T(8,128)(2,1)S(1)}, u32[]{:S(2)}, u32[]{:S(2)}) collective-permute-start(bf16[32,4096]{1,0:T(8,128)(2,1)} %bitcast.2), channel_id=1, source_target_pairs={{0,16},{1,17},{2,18},{3,19},{4,20},{5,21},{6,22},{7,23},{8,24},{9,... | collective-permute-start | bytes 786440 | tf_op jit(solution)/shard_map/ppermute | solution.py:223
  4.5 1.5 %collective-permute-start.3 = (bf16[32,4096]{1,0:T(8,128)(2,1)}, bf16[32,4096]{1,0:T(8,128)(2,1)S(1)}, u32[]{:S(2)}, u32[]{:S(2)}) collective-permute-start(bf16[32,4096]{1,0:T(8,128)(2,1)} %bitcast.3), channel_id=1, source_target_pairs={{0,2},{1,3},{2,0},{3,1},{4,6},{5,7},{6,4},{7,5},{8,10},{9,11},{10,... | collective-permute-start | bytes 786440 | tf_op jit(solution)/shard_map/ppermute | solution.py:223
  6.0 2.5 %collective-permute-start = (bf16[32,4096]{1,0:T(8,128)(2,1)}, bf16[32,4096]{1,0:T(8,128)(2,1)S(1)}, u32[]{:S(2)}, u32[]{:S(2)}) collective-permute-start(bf16[32,4096]{1,0:T(8,128)(2,1)} %bitcast.4), channel_id=1, source_target_pairs={{0,12},{1,13},{2,14},{3,15},{4,8},{5,9},{6,10},{7,11},{8,4},{9,5},... | collective-permute-start | bytes 786440 | tf_op jit(solution)/shard_map/ppermute | solution.py:223
  8.5 3.5 %shard_map.46 = (bf16[1,4096,512]{2,1,0:T(8,128)(2,1)S(1)}, bf16[1,4096,512]{2,1,0:T(8,128)(2,1)S(1)}) custom-call(bf16[1,4096,512]{2,1,0:T(8,128)(2,1)} %gate.1, bf16[1,4096,512]{2,1,0:T(8,128)(2,1)} %up.1), custom_call_target="tpu_custom_call" | custom-call | flops 4194304 | bytes 16777216 | tf_op jit(solution)/shard_map/pallas_call | solution.py:116
  12.0 0.0 collective-permute-done.11.refs_7_
  12.0 0.6 collective-permute-start.12
  12.6 0.0 collective-permute-done.4.refs_1_
  12.6 0.0 collective-permute-done.3.refs_6_
  12.6 1.5 %collective-permute-start.5 = (bf16[32,4096]{1,0:T(8,128)(2,1)S(1)}, bf16[32,4096]{1,0:T(8,128)(2,1)S(1)}, u32[]{:S(2)}, u32[]{:S(2)}) collective-permute-start(bf16[32,4096]{1,0:T(8,128)(2,1)S(1)} %collective-permute-done.3.refs_6_), channel_id=1, source_target_pairs={{0,16},{1,17},{2,18},{3,19},{4,20},{5,21},{6,22},{7,23},{8,24},{9,... | collective-permute-start | bytes 786440 | tf_op jit(solution)/shard_map/ppermute | solution.py:223
  14.1 0.5 collective-permute-start.14
  14.7 2.8 %collective-permute-done.refs_7_ = bf16[32,4096]{1,0:T(8,128)(2,1)S(1)} collective-permute-done((bf16[32,4096]{1,0:T(8,128)(2,1)}, bf16[32,4096]{1,0:T(8,128)(2,1)S(1)}, u32[]{:S(2)}, u32[]{:S(2)}) %collective-permute-start) | collective-permute-done | bytes 262176 | tf_op jit(solution)/shard_map/ppermute | solution.py:223
  17.5 3.1 %collective-permute-start.1 = (bf16[32,4096]{1,0:T(8,128)(2,1)S(1)}, bf16[32,4096]{1,0:T(8,128)(2,1)S(1)}, u32[]{:S(2)}, u32[]{:S(2)}) collective-permute-start(bf16[32,4096]{1,0:T(8,128)(2,1)S(1)} %collective-permute-done.refs_7_), channel_id=1, source_target_pairs={{0,4},{1,5},{2,6},{3,7},{4,0},{5,1},{6,2},{7,3},{8,12},{9,13},{10,... | collective-permute-start | bytes 786440 | tf_op jit(solution)/shard_map/ppermute | solution.py:223
  20.5 0.8 %collective-permute-done.12.refs_3_ = bf16[32,4096]{1,0:T(8,128)(2,1)S(1)} collective-permute-done((bf16[32,4096]{1,0:T(8,128)(2,1)S(1)}, bf16[32,4096]{1,0:T(8,128)(2,1)S(1)}, u32[]{:S(2)}, u32[]{:S(2)}) %collective-permute-start.12) | collective-permute-done | bytes 262176 | tf_op jit(solution)/shard_map/ppermute | solution.py:223
  21.3 0.5 collective-permute-start.13
  21.9 2.8 %collective-permute-done.5.refs_2_ = bf16[32,4096]{1,0:T(8,128)(2,1)S(1)} collective-permute-done((bf16[32,4096]{1,0:T(8,128)(2,1)S(1)}, bf16[32,4096]{1,0:T(8,128)(2,1)S(1)}, u32[]{:S(2)}, u32[]{:S(2)}) %collective-permute-start.5) | collective-permute-done | bytes 262176 | tf_op jit(solution)/shard_map/ppermute | solution.py:223
  24.6 3.5 %collective-permute-start.6 = (bf16[32,4096]{1,0:T(8,128)(2,1)S(1)}, bf16[32,4096]{1,0:T(8,128)(2,1)S(1)}, u32[]{:S(2)}, u32[]{:S(2)}) collective-permute-start(bf16[32,4096]{1,0:T(8,128)(2,1)S(1)} %collective-permute-done.5.refs_2_), channel_id=1, source_target_pairs={{0,12},{1,13},{2,14},{3,15},{4,8},{5,9},{6,10},{7,11},{8,4},{9,5},... | collective-permute-start | bytes 786440 | tf_op jit(solution)/shard_map/ppermute | solution.py:223
  28.1 1.5 %collective-permute-start.10 = (bf16[32,4096]{1,0:T(8,128)(2,1)S(1)}, bf16[32,4096]{1,0:T(8,128)(2,1)S(1)}, u32[]{:S(2)}, u32[]{:S(2)}) collective-permute-start(bf16[32,4096]{1,0:T(8,128)(2,1)S(1)} %collective-permute-done.refs_7_), channel_id=1, source_target_pairs={{0,2},{1,3},{2,0},{3,1},{4,6},{5,7},{6,4},{7,5},{8,10},{9,11},{10,... | collective-permute-start | bytes 786440 | tf_op jit(solution)/shard_map/ppermute | solution.py:223
  29.6 0.0 collective-permute-done.14.refs_8_
  29.6 1.8 %collective-permute-start.8 = (bf16[32,4096]{1,0:T(8,128)(2,1)S(1)}, bf16[32,4096]{1,0:T(8,128)(2,1)S(1)}, u32[]{:S(2)}, u32[]{:S(2)}) collective-permute-start(bf16[32,4096]{1,0:T(8,128)(2,1)S(1)} %collective-permute-done.refs_7_), channel_id=1, source_target_pairs={{0,16},{1,17},{2,18},{3,19},{4,20},{5,21},{6,22},{7,23},{8,24},{9,... | collective-permute-start | bytes 786440 | tf_op jit(solution)/shard_map/ppermute | solution.py:223
  31.4 0.0 collective-permute-done.1.refs_5_
  31.4 0.5 collective-permute-start.9
  31.9 0.0 collective-permute-done.13.refs_4_
  31.9 0.3 collective-permute-start.2
  32.2 1.5 %collective-permute-done.6.refs_4_ = bf16[32,4096]{1,0:T(8,128)(2,1)S(1)} collective-permute-done((bf16[32,4096]{1,0:T(8,128)(2,1)S(1)}, bf16[32,4096]{1,0:T(8,128)(2,1)S(1)}, u32[]{:S(2)}, u32[]{:S(2)}) %collective-permute-start.6) | collective-permute-done | bytes 262176 | tf_op jit(solution)/shard_map/ppermute | solution.py:223
  33.7 3.3 %collective-permute-start.7 = (bf16[32,4096]{1,0:T(8,128)(2,1)S(1)}, bf16[32,4096]{1,0:T(8,128)(2,1)S(1)}, u32[]{:S(2)}, u32[]{:S(2)}) collective-permute-start(bf16[32,4096]{1,0:T(8,128)(2,1)S(1)} %collective-permute-done.6.refs_4_), channel_id=1, source_target_pairs={{0,4},{1,5},{2,6},{3,7},{4,0},{5,1},{6,2},{7,3},{8,12},{9,13},{10,... | collective-permute-start | bytes 786440 | tf_op jit(solution)/shard_map/ppermute | solution.py:223
  36.9 0.0 copy-done
  36.9 0.0 copy-done.1
  36.9 2.9 %shard_map.47 = (f32[128,1024]{1,0:T(8,128)S(1)}, f32[128,1024]{1,0:T(8,128)S(1)}) custom-call(f32[2,2]{1,0:T(2,128)S(1)} %copy-done.1, bf16[32,4096]{1,0:T(8,128)(2,1)S(1)} %collective-permute-done.4.refs_1_, bf16[32,4096]{1,0:T(8,128)(2,1)S(1)} %collective-permute-done.5.refs_2_, bf16[32,4096]{1,0:T(8,128)(2,1)S(1)} %collective-permute-done.12.refs_3_, ...), custom_call_target="tpu_custom_call" | custom-call | flops 2147483648 | bytes 10485760 | tf_op jit(solution)/shard_map/pallas_call | solution.py:90
  39.8 0.0 collective-permute-done.10.refs_8_
  39.8 0.0 collective-permute-done.8.refs_3_
  39.9 0.0 collective-permute-done.9.refs_6_
  39.9 0.0 collective-permute-done.2.refs_1_
  39.9 1.4 %collective-permute-done.7.refs_2_ = bf16[32,4096]{1,0:T(8,128)(2,1)S(1)} collective-permute-done((bf16[32,4096]{1,0:T(8,128)(2,1)S(1)}, bf16[32,4096]{1,0:T(8,128)(2,1)S(1)}, u32[]{:S(2)}, u32[]{:S(2)}) %collective-permute-start.7) | collective-permute-done | bytes 262176 | tf_op jit(solution)/shard_map/ppermute | solution.py:223
  41.3 3.0 %shard_map.48 = (f32[128,1024]{1,0:T(8,128)S(1)}, f32[128,1024]{1,0:T(8,128)S(1)}, f32[128,1024]{1,0:T(8,128)S(1)}, f32[128,1024]{1,0:T(8,128)S(1)}) custom-call(f32[2,2]{1,0:T(2,128)S(1)} %copy-done.1, bf16[32,4096]{1,0:T(8,128)(2,1)S(1)} %collective-permute-done.2.refs_1_, bf16[32,4096]{1,0:T(8,128)(2,1)S(1)} %collective-permute-done.7.refs_2_, ...), custom_call_target="tpu_custom_call" | custom-call | flops 2147483648 | bytes 10485760 | tf_op jit(solution)/shard_map/pallas_call | solution.py:90
  44.3 0.1 collective-permute-start.16
  44.4 0.5 collective-permute-start.15
  44.9 1.4 %collective-permute-done.16.received_ref = f32[128,1024]{1,0:T(8,128)S(1)} collective-permute-done((f32[128,1024]{1,0:T(8,128)S(1)}, f32[128,1024]{1,0:T(8,128)S(1)}, u32[]{:S(2)}, u32[]{:S(2)}) %collective-permute-start.16) | collective-permute-done | bytes 524320 | tf_op jit(solution)/shard_map/ppermute | solution.py:223
  46.3 1.0 %shard_map.49 = bf16[128,1152]{1,0:T(8,128)(2,1)S(1)} custom-call(f32[128,1024]{1,0:T(8,128)S(1)} %get-tuple-element.23.kept_ref, f32[128,1024]{1,0:T(8,128)S(1)} %collective-permute-done.16.received_ref), custom_call_target="tpu_custom_call" | custom-call | tf_op jit(solution)/shard_map/pallas_call | solution.py:161
  47.3 1.3 %collective-permute-start.17 = (bf16[128,1152]{1,0:T(8,128)(2,1)S(1)}, bf16[128,1152]{1,0:T(8,128)(2,1)S(1)}, u32[]{:S(2)}, u32[]{:S(2)}) collective-permute-start(bf16[128,1152]{1,0:T(8,128)(2,1)S(1)} %shard_map.49), channel_id=1, source_target_pairs={{0,16},{1,17},{2,18},{3,19},{4,20},{5,21},{6,22},{7,23},{8,24},{9,... | collective-permute-start | bytes 884744 | tf_op jit(solution)/shard_map/ppermute | solution.py:223
  48.6 0.0 collective-permute-done.15.received_ref
  48.6 7.8 %collective-permute-done.17.code_ref = bf16[128,1152]{1,0:T(8,128)(2,1)S(1)} collective-permute-done((bf16[128,1152]{1,0:T(8,128)(2,1)S(1)}, bf16[128,1152]{1,0:T(8,128)(2,1)S(1)}, u32[]{:S(2)}, u32[]{:S(2)}) %collective-permute-start.17) | collective-permute-done | bytes 294944 | tf_op jit(solution)/shard_map/ppermute | solution.py:223
  56.4 1.6 %shard_map.50 = bf16[1,128,512]{2,1,0:T(8,128)(2,1)} custom-call(f32[128,1024]{1,0:T(8,128)S(1)} %get-tuple-element.21.kept_ref, f32[128,1024]{1,0:T(8,128)S(1)} %collective-permute-done.15.received_ref, bf16[128,1152]{1,0:T(8,128)(2,1)S(1)} %collective-permute-done.17.code_ref), custom_call_target="tpu_custom_call" | custom-call | tf_op jit(solution)/shard_map/pallas_call | solution.py:202
Async XLA Ops:
  0.0 36.9 %copy-start = (bf16[1,32,4096]{2,1,0:T(8,128)(2,1)S(1)}, bf16[1,32,4096]{2,1,0:T(8,128)(2,1)}, u32[]{:S(2)}) copy-start(bf16[1,32,4096]{2,1,0:T(8,128)(2,1)} %param.4) | copy-start | bytes 786436
  0.0 36.9 %copy-start.1 = (f32[2,2]{1,0:T(2,128)S(1)}, f32[2,2]{1,0:T(2,128)}, u32[]{:S(2)}) copy-start(f32[2,2]{1,0:T(2,128)} %refs_0_.3) | copy-start | bytes 52
  0.0 12.0 %collective-permute-start.11 = (bf16[32,4096]{1,0:T(8,128)(2,1)}, bf16[32,4096]{1,0:T(8,128)(2,1)S(1)}, u32[]{:S(2)}, u32[]{:S(2)}) collective-permute-start(bf16[32,4096]{1,0:T(8,128)(2,1)} %bitcast.1), channel_id=1, source_target_pairs={{0,4},{1,5},{2,6},{3,7},{4,0},{5,1},{6,2},{7,3},{8,12},{9,13},{10,... | collective-permute-start | bytes 786440 | tf_op jit(solution)/shard_map/ppermute | solution.py:223
  3.0 9.6 %collective-permute-start.4 = (bf16[32,4096]{1,0:T(8,128)(2,1)}, bf16[32,4096]{1,0:T(8,128)(2,1)S(1)}, u32[]{:S(2)}, u32[]{:S(2)}) collective-permute-start(bf16[32,4096]{1,0:T(8,128)(2,1)} %bitcast.2), channel_id=1, source_target_pairs={{0,16},{1,17},{2,18},{3,19},{4,20},{5,21},{6,22},{7,23},{8,24},{9,... | collective-permute-start | bytes 786440 | tf_op jit(solution)/shard_map/ppermute | solution.py:223
  4.5 8.0 %collective-permute-start.3 = (bf16[32,4096]{1,0:T(8,128)(2,1)}, bf16[32,4096]{1,0:T(8,128)(2,1)S(1)}, u32[]{:S(2)}, u32[]{:S(2)}) collective-permute-start(bf16[32,4096]{1,0:T(8,128)(2,1)} %bitcast.3), channel_id=1, source_target_pairs={{0,2},{1,3},{2,0},{3,1},{4,6},{5,7},{6,4},{7,5},{8,10},{9,11},{10,... | collective-permute-start | bytes 786440 | tf_op jit(solution)/shard_map/ppermute | solution.py:223
  6.0 11.4 %collective-permute-start = (bf16[32,4096]{1,0:T(8,128)(2,1)}, bf16[32,4096]{1,0:T(8,128)(2,1)S(1)}, u32[]{:S(2)}, u32[]{:S(2)}) collective-permute-start(bf16[32,4096]{1,0:T(8,128)(2,1)} %bitcast.4), channel_id=1, source_target_pairs={{0,12},{1,13},{2,14},{3,15},{4,8},{5,9},{6,10},{7,11},{8,4},{9,5},... | collective-permute-start | bytes 786440 | tf_op jit(solution)/shard_map/ppermute | solution.py:223
  12.0 9.3 %collective-permute-start.12 = (bf16[32,4096]{1,0:T(8,128)(2,1)S(1)}, bf16[32,4096]{1,0:T(8,128)(2,1)S(1)}, u32[]{:S(2)}, u32[]{:S(2)}) collective-permute-start(bf16[32,4096]{1,0:T(8,128)(2,1)S(1)} %collective-permute-done.11.refs_7_), channel_id=1, source_target_pairs={{0,16},{1,17},{2,18},{3,19},{4,20},{5,21},{6,22},{7,23},{8,24},{9,... | collective-permute-start | bytes 786440 | tf_op jit(solution)/shard_map/ppermute | solution.py:223
  12.6 12.0 %collective-permute-start.5 = (bf16[32,4096]{1,0:T(8,128)(2,1)S(1)}, bf16[32,4096]{1,0:T(8,128)(2,1)S(1)}, u32[]{:S(2)}, u32[]{:S(2)}) collective-permute-start(bf16[32,4096]{1,0:T(8,128)(2,1)S(1)} %collective-permute-done.3.refs_6_), channel_id=1, source_target_pairs={{0,16},{1,17},{2,18},{3,19},{4,20},{5,21},{6,22},{7,23},{8,24},{9,... | collective-permute-start | bytes 786440 | tf_op jit(solution)/shard_map/ppermute | solution.py:223
  14.1 15.5 %collective-permute-start.14 = (bf16[32,4096]{1,0:T(8,128)(2,1)S(1)}, bf16[32,4096]{1,0:T(8,128)(2,1)S(1)}, u32[]{:S(2)}, u32[]{:S(2)}) collective-permute-start(bf16[32,4096]{1,0:T(8,128)(2,1)S(1)} %collective-permute-done.11.refs_7_), channel_id=1, source_target_pairs={{0,2},{1,3},{2,0},{3,1},{4,6},{5,7},{6,4},{7,5},{8,10},{9,11},{10,... | collective-permute-start | bytes 786440 | tf_op jit(solution)/shard_map/ppermute | solution.py:223
  17.5 13.9 %collective-permute-start.1 = (bf16[32,4096]{1,0:T(8,128)(2,1)S(1)}, bf16[32,4096]{1,0:T(8,128)(2,1)S(1)}, u32[]{:S(2)}, u32[]{:S(2)}) collective-permute-start(bf16[32,4096]{1,0:T(8,128)(2,1)S(1)} %collective-permute-done.refs_7_), channel_id=1, source_target_pairs={{0,4},{1,5},{2,6},{3,7},{4,0},{5,1},{6,2},{7,3},{8,12},{9,13},{10,... | collective-permute-start | bytes 786440 | tf_op jit(solution)/shard_map/ppermute | solution.py:223
  21.3 10.6 %collective-permute-start.13 = (bf16[32,4096]{1,0:T(8,128)(2,1)S(1)}, bf16[32,4096]{1,0:T(8,128)(2,1)S(1)}, u32[]{:S(2)}, u32[]{:S(2)}) collective-permute-start(bf16[32,4096]{1,0:T(8,128)(2,1)S(1)} %collective-permute-done.12.refs_3_), channel_id=1, source_target_pairs={{0,2},{1,3},{2,0},{3,1},{4,6},{5,7},{6,4},{7,5},{8,10},{9,11},{10,... | collective-permute-start | bytes 786440 | tf_op jit(solution)/shard_map/ppermute | solution.py:223
  24.6 9.0 %collective-permute-start.6 = (bf16[32,4096]{1,0:T(8,128)(2,1)S(1)}, bf16[32,4096]{1,0:T(8,128)(2,1)S(1)}, u32[]{:S(2)}, u32[]{:S(2)}) collective-permute-start(bf16[32,4096]{1,0:T(8,128)(2,1)S(1)} %collective-permute-done.5.refs_2_), channel_id=1, source_target_pairs={{0,12},{1,13},{2,14},{3,15},{4,8},{5,9},{6,10},{7,11},{8,4},{9,5},... | collective-permute-start | bytes 786440 | tf_op jit(solution)/shard_map/ppermute | solution.py:223
  28.1 11.7 %collective-permute-start.10 = (bf16[32,4096]{1,0:T(8,128)(2,1)S(1)}, bf16[32,4096]{1,0:T(8,128)(2,1)S(1)}, u32[]{:S(2)}, u32[]{:S(2)}) collective-permute-start(bf16[32,4096]{1,0:T(8,128)(2,1)S(1)} %collective-permute-done.refs_7_), channel_id=1, source_target_pairs={{0,2},{1,3},{2,0},{3,1},{4,6},{5,7},{6,4},{7,5},{8,10},{9,11},{10,... | collective-permute-start | bytes 786440 | tf_op jit(solution)/shard_map/ppermute | solution.py:223
  29.6 10.2 %collective-permute-start.8 = (bf16[32,4096]{1,0:T(8,128)(2,1)S(1)}, bf16[32,4096]{1,0:T(8,128)(2,1)S(1)}, u32[]{:S(2)}, u32[]{:S(2)}) collective-permute-start(bf16[32,4096]{1,0:T(8,128)(2,1)S(1)} %collective-permute-done.refs_7_), channel_id=1, source_target_pairs={{0,16},{1,17},{2,18},{3,19},{4,20},{5,21},{6,22},{7,23},{8,24},{9,... | collective-permute-start | bytes 786440 | tf_op jit(solution)/shard_map/ppermute | solution.py:223
  31.4 8.5 %collective-permute-start.9 = (bf16[32,4096]{1,0:T(8,128)(2,1)S(1)}, bf16[32,4096]{1,0:T(8,128)(2,1)S(1)}, u32[]{:S(2)}, u32[]{:S(2)}) collective-permute-start(bf16[32,4096]{1,0:T(8,128)(2,1)S(1)} %collective-permute-done.1.refs_5_), channel_id=1, source_target_pairs={{0,2},{1,3},{2,0},{3,1},{4,6},{5,7},{6,4},{7,5},{8,10},{9,11},{10,... | collective-permute-start | bytes 786440 | tf_op jit(solution)/shard_map/ppermute | solution.py:223
  31.9 8.0 %collective-permute-start.2 = (bf16[32,4096]{1,0:T(8,128)(2,1)S(1)}, bf16[32,4096]{1,0:T(8,128)(2,1)S(1)}, u32[]{:S(2)}, u32[]{:S(2)}) collective-permute-start(bf16[32,4096]{1,0:T(8,128)(2,1)S(1)} %collective-permute-done.1.refs_5_), channel_id=1, source_target_pairs={{0,16},{1,17},{2,18},{3,19},{4,20},{5,21},{6,22},{7,23},{8,24},{9,... | collective-permute-start | bytes 786440 | tf_op jit(solution)/shard_map/ppermute | solution.py:223
  33.7 7.6 %collective-permute-start.7 = (bf16[32,4096]{1,0:T(8,128)(2,1)S(1)}, bf16[32,4096]{1,0:T(8,128)(2,1)S(1)}, u32[]{:S(2)}, u32[]{:S(2)}) collective-permute-start(bf16[32,4096]{1,0:T(8,128)(2,1)S(1)} %collective-permute-done.6.refs_4_), channel_id=1, source_target_pairs={{0,4},{1,5},{2,6},{3,7},{4,0},{5,1},{6,2},{7,3},{8,12},{9,13},{10,... | collective-permute-start | bytes 786440 | tf_op jit(solution)/shard_map/ppermute | solution.py:223
  44.3 2.0 %collective-permute-start.16 = (f32[128,1024]{1,0:T(8,128)S(1)}, f32[128,1024]{1,0:T(8,128)S(1)}, u32[]{:S(2)}, u32[]{:S(2)}) collective-permute-start(f32[128,1024]{1,0:T(8,128)S(1)} %get-tuple-element.24), channel_id=1, source_target_pairs={{0,1},{1,0},{2,3},{3,2},{4,5},{5,4},{6,7},{7,6},{8,9},{9,8},{10,11... | collective-permute-start | bytes 1572872 | tf_op jit(solution)/shard_map/ppermute | solution.py:223
  44.4 4.2 %collective-permute-start.15 = (f32[128,1024]{1,0:T(8,128)S(1)}, f32[128,1024]{1,0:T(8,128)S(1)}, u32[]{:S(2)}, u32[]{:S(2)}) collective-permute-start(f32[128,1024]{1,0:T(8,128)S(1)} %get-tuple-element.22), channel_id=1, source_target_pairs={{0,1},{1,0},{2,3},{3,2},{4,5},{5,4},{6,7},{7,6},{8,9},{9,8},{10,11... | collective-permute-start | bytes 1572872 | tf_op jit(solution)/shard_map/ppermute | solution.py:223
  47.3 9.1 %collective-permute-start.17 = (bf16[128,1152]{1,0:T(8,128)(2,1)S(1)}, bf16[128,1152]{1,0:T(8,128)(2,1)S(1)}, u32[]{:S(2)}, u32[]{:S(2)}) collective-permute-start(bf16[128,1152]{1,0:T(8,128)(2,1)S(1)} %shard_map.49), channel_id=1, source_target_pairs={{0,16},{1,17},{2,18},{3,19},{4,20},{5,21},{6,22},{7,23},{8,24},{9,... | collective-permute-start | bytes 884744 | tf_op jit(solution)/shard_map/ppermute | solution.py:223

commit v5 on v4

--- a/solution.py
+++ b/solution.py
@@ -44,61 +44,65 @@
     return lax.axis_index("row") == (lax.axis_index("tp") >> 1) // half
 
 
-def products(other, own, coefficients, weights, work, half, near=None):
-    blocks = other + own
+def products(blocks, own, coefficients, weights, work, half=None, near=None):
     count = len(blocks)
     rows, depth = blocks[0].shape
     width = weights[0].shape[2]
-    span = len(other) * rows
-    extra = 0 if near is None else 2
+    earlier = () if near is None else (near,)
+    split = half is not None and near is None
+    span = count * rows // 2 if split else count * rows
 
     def kernel(*refs):
         table, block_refs = refs[0], refs[1 : count + 1]
-        gate, up = refs[count + 1 : count + 3]
-        near_refs = refs[count + 3 : count + 3 + extra]
-        outs = refs[count + 3 + extra :]
+        held = refs[count + 1 : count + 3]
+        near_refs = refs[count + 3 : count + 3 + len(earlier)]
+        outs = refs[count + 3 + len(earlier) :]
         source = lax.axis_index("src")
+        factor = table[source, source] if own else table[1 - source, source]
         lhs = jnp.concatenate([ref[...] for ref in block_refs], axis=0)
-        factors = (table[1 - source, source], table[source, source])
-
-        def store(targets):
-            for start, held in ((0, gate), (width, up)):
-                part = jnp.dot(lhs, held[0], preferred_element_type=jnp.float32)
-                for i in range(2):
-                    targets[i][:, start : start + width] = part[i * span : (i + 1) * span] * factors[i]
-
-        if near is None:
-            store(outs)
+
+        def store(*targets):
+            for i in range(2):
+                product = jnp.dot(lhs, held[i][0], preferred_element_type=jnp.float32)
+                for j, target in enumerate(targets):
+                    part = product[j * span : (j + 1) * span]
+                    target[:, i * width : (i + 1) * width] = part * factor
+
+        def fill(near_target, far_target):
+            if split:
+                store(near_target, far_target)
+            else:
+                store(far_target)
+                near_target[...] = near_refs[0][...]
+
+        if half is None:
+            store(outs[0])
         else:
-            sent, kept = outs[:2], outs[2:]
             mine = keeps_near(half)
 
             @pl.when(mine)
             def _():
-                store(sent)
-                for i in range(2):
-                    kept[i][...] = near_refs[i][...]
+                fill(outs[1], outs[0])
 
             @pl.when(jnp.logical_not(mine))
             def _():
-                store(kept)
-                for i in range(2):
-                    sent[i][...] = near_refs[i][...]
-
-    whole = pl.BlockSpec(memory_space=pltpu.VMEM)
-    result = jax.ShapeDtypeStruct((span, 2 * width), jnp.float32)
-    return pl.pallas_call(
-        kernel,
-        out_shape=[result] * (2 + extra),
-        in_specs=[pl.BlockSpec(memory_space=pltpu.SMEM)] + [whole] * (count + 2 + extra),
-        out_specs=[whole] * (2 + extra),
+                fill(outs[0], outs[1])
+
+    whole = pl.BlockSpec(memory_space=pltpu.VMEM)
+    results = 1 if half is None else 2
+    out = pl.pallas_call(
+        kernel,
+        out_shape=[jax.ShapeDtypeStruct((span, 2 * width), jnp.float32)] * results,
+        in_specs=[pl.BlockSpec(memory_space=pltpu.SMEM)] + [whole] * (count + 2 + len(earlier)),
+        out_specs=[whole] * results,
         compiler_params=pltpu.CompilerParams(vmem_limit_bytes=24 * 2**20),
         cost_estimate=pl.CostEstimate(
             flops=work * 4 * count * rows * depth * width,
             bytes_accessed=4 * depth * width + 2 * count * rows * depth,
             transcendentals=0,
         ),
-    )(coefficients, *blocks, *weights, *(near or ()))
+    )(coefficients, *blocks, *weights, *earlier)
+    return out if half is not None else out[0]
 
 
 def resident(gate_weights, up_weights, work):
@@ -167,33 +171,47 @@
     )(kept, received)
 
 
-def decoded(values, scale):
-    values = values.astype(jnp.float32)
-    size = jnp.abs(values)
-    power = jnp.floor(jnp.log2(size) + 0.001)
-    fraction = jnp.floor((size * jnp.exp2(-power) - 1) * FIELD + 0.5)
-    level = ((power + SHIFT) * FIELD + fraction) * (1 / STEPS)
-    part = level * 2.0**-SEGMENTS
-    for k in range(1, SEGMENTS):
-        part = jnp.maximum(part, (level - k) * 2.0 ** (k - SEGMENTS))
-    return jnp.where(values < 0, -part, part) * scale
-
-
-def activated(kept, received, code, rows):
-    width = kept.shape[1] // 2
-
-    def kernel(kept_ref, received_ref, code_ref, out):
+def decoded(values, work):
+    rows, side = values.shape[0], (values.shape[1] - FIELD) // 2
+
+    def kernel(values_ref, out):
+        for j in range(2):
+            columns = slice(j * side, (j + 1) * side)
+            at = 2 * side + j * (FIELD // 2)
+            scale = values_ref[:, at : at + 1].astype(jnp.float32)
+            value = values_ref[:, columns].astype(jnp.float32)
+            size = jnp.abs(value)
+            power = jnp.floor(jnp.log2(size) + 0.001)
+            fraction = jnp.floor((size * jnp.exp2(-power) - 1) * FIELD + 0.5)
+            level = ((power + SHIFT) * FIELD + fraction) * (1 / STEPS)
+            part = level * 2.0**-SEGMENTS
+            for k in range(1, SEGMENTS):
+                part = jnp.maximum(part, (level - k) * 2.0 ** (k - SEGMENTS))
+            out[:, columns] = jnp.where(value < 0, -part, part) * scale
+
+    whole = pl.BlockSpec(memory_space=pltpu.VMEM)
+    return pl.pallas_call(
+        kernel,
+        out_shape=jax.ShapeDtypeStruct((rows, 2 * side), jnp.float32),
+        in_specs=[whole],
+        out_specs=whole,
+        compiler_params=pltpu.CompilerParams(vmem_limit_bytes=24 * 2**20),
+        cost_estimate=pl.CostEstimate(
+            flops=work * 60 * rows * side, bytes_accessed=2 * values.size, transcendentals=0
+        ),
+    )(values)
+
+
+def activated(parts, rows):
+    width = parts[0].shape[1] // 2
+
+    def kernel(*refs):
+        out = refs[-1]
         tp = lax.axis_index("tp")
         for i in range(4):
             span = slice(i * rows, (i + 1) * rows)
-            total = []
-            for j in range(2):
-                columns = slice(j * width, (j + 1) * width)
-                at = 2 * width + j * (FIELD // 2)
-                scale = code_ref[span, at : at + 1].astype(jnp.float32)
-                own = kept_ref[span, columns] + received_ref[span, columns]
-                total.append(own + decoded(code_ref[span, columns], scale))
-            gate, up = total
+            total = refs[0][span, :] + refs[1][span, :] + refs[2][span, :]
+            gate, up = total[:, :width], total[:, width:]
             value = (gate / (1 + jnp.exp(-gate)) * up).astype(jnp.bfloat16)
             at = i ^ (tp & 3)
             out[0, pl.ds(pl.multiple_of(at * rows, rows), rows), :] = value
@@ -205,7 +223,7 @@
         in_specs=[whole] * 3,
         out_specs=whole,
         compiler_params=pltpu.CompilerParams(vmem_limit_bytes=24 * 2**20),
-    )(kept, received, code)
+    )(*parts)
 
 
 def paired(mesh):
@@ -230,25 +248,25 @@
         z1 = swap(b0, z=1)
         y0 = swap(b0, src=1)
         x0 = swap(b0, x=1)
-        d0 = swap(after(x0, y0, held[0]), src=1)
+        d0 = swap(b0, src=1, x=1)
+        y1 = swap(after(z1, y0, x0, held[0]), src=1)
+        x1 = swap(z1, x=1)
         z2 = swap(z3, z=1)
-        y1 = swap(z1, src=1)
-        x1 = swap(z1, x=1)
-        d1 = swap(after(y1, y1), x=1)
+        d1 = swap(y1, x=1)
         y3 = swap(z3, src=1)
         x3 = swap(z3, x=1)
         d3 = swap(d0, z=3)
-        near = products([y0, d0, y1, d1], [b0, x0, z1, x1], coefficients, held, 1, half)
+        near = products([y0, d0, y1, d1], False, coefficients, held, 1)
         y2 = swap(z2, src=1)
         x2 = swap(z2, x=1)
         d2 = swap(d3, z=1)
-        sent, sent_own, kept, kept_own = products(
-            [y2, d2, y3, d3], [z2, x2, z3, x3], coefficients, held, 1, half, near
-        )
-        other = coded(kept, swap(sent, row=1))
+        sent, kept = products([after(y2, x3), d2, y3, d3], False, coefficients, held, 1, half, near)
+        other = coded(kept, swap(after(sent, x1), row=1))
+        from_other = swap(other, src=1)
+        sent_own, kept_own = products([after(b0, other), x0, z1, x1, z2, x2, z3, x3], True, coefficients, held, 1, half)
         core_own = swap(sent_own, row=1)
-        from_other = swap(other, src=1)
-        return activated(kept_own, core_own, from_other, rows)
+        theirs = decoded(from_other, 3000)
+        return activated((kept_own, core_own, theirs), rows)
 
     return shards
 

time: 58.1 us -> 54.9 us (0.945)
  waiting for transfers between devices: 18.5 us -> 14.5 us
  Pallas kernels: 12 us -> 13 us
    ppermute x18, waiting for transfers between devices: 18.5 us -> 14.5 us  [swap(): return lax.ppermute(array, AXES, pairs)]
    pallas_call x2 -> x4, Pallas kernels: 5.93 us -> 7.77 us  [the longest x3 6.69 us: products(): pl.pallas_call(kernel, out_shape=[jax.ShapeDtypeStruct((span, 2 * width),...]
    pallas_call x1, Pallas kernels: 1.57 us -> 0.77 us  [activated(): pl.pallas_call(kernel, out_shape=jax.ShapeDtypeStruct((1, 4 * rows, width...]
  transfers between devices with their start and end apart: 18 -> 18, of which waited for: 7 -> 14; matrix products, arithmetic and copies ran while one was open for 0% -> 0% of each run, Pallas kernels for 13% -> 22%
where the time goes in v5:
time: 54.9 us; the launch traced here: 54.6 us
  starting transfers between devices  27 us (49%)
  waiting for transfers between devices  14.5 us (26%)
  Pallas kernels  13 us (24%)
    ppermute x18, starting transfers between devices, swap(): return lax.ppermute(array, AXES, pairs)  27 us
    ppermute x18, waiting for transfers between devices, swap(): return lax.ppermute(array, AXES, pairs)  14.5 us
    pallas_call x3, Pallas kernels, products(): pl.pallas_call(kernel, out_shape=[jax.ShapeDtypeStruct((span, 2 * width),...  6.69 us
    pallas_call x1, Pallas kernels, resident(): pl.pallas_call(kernel, out_shape=[pltpu.VMEM(w.shape, w.dtype) for w in (...  3.48 us
  transfers between devices with their start and end apart: 18, of which 14 were waited for; matrix products, arithmetic and copies ran while one was open for 0% of the time, Pallas kernels for 22%

profile of v5, /device:TPU:0, one launch (start us, length us, event | category | flops | bytes accessed | tf_op | source)
XLA Modules:
  0.0 54.6 jit_solution(11079819745200986232)
XLA Ops:
  0.0 0.0 copy-start.1
  0.0 5.0 %collective-permute-start = (bf16[32,4096]{1,0:T(8,128)(2,1)}, bf16[32,4096]{1,0:T(8,128)(2,1)S(1)}, u32[]{:S(2)}, u32[]{:S(2)}) collective-permute-start(bf16[32,4096]{1,0:T(8,128)(2,1)} %bitcast.1), channel_id=1, source_target_pairs={{0,12},{1,13},{2,14},{3,15},{4,8},{5,9},{6,10},{7,11},{8,4},{9,5},... | collective-permute-start | bytes 786440 | tf_op jit(solution)/shard_map/ppermute | solution.py:241
  5.1 0.0 collective-permute-start.9
  5.1 1.5 %collective-permute-start.10 = (bf16[32,4096]{1,0:T(8,128)(2,1)}, bf16[32,4096]{1,0:T(8,128)(2,1)S(1)}, u32[]{:S(2)}, u32[]{:S(2)}) collective-permute-start(bf16[32,4096]{1,0:T(8,128)(2,1)} %bitcast.3), channel_id=1, source_target_pairs={{0,2},{1,3},{2,0},{3,1},{4,6},{5,7},{6,4},{7,5},{8,10},{9,11},{10,... | collective-permute-start | bytes 786440 | tf_op jit(solution)/shard_map/ppermute | solution.py:241
  6.5 1.5 %collective-permute-start.8 = (bf16[32,4096]{1,0:T(8,128)(2,1)}, bf16[32,4096]{1,0:T(8,128)(2,1)S(1)}, u32[]{:S(2)}, u32[]{:S(2)}) collective-permute-start(bf16[32,4096]{1,0:T(8,128)(2,1)} %bitcast.4), channel_id=1, source_target_pairs={{0,16},{1,17},{2,18},{3,19},{4,20},{5,21},{6,22},{7,23},{8,24},{9,... | collective-permute-start | bytes 786440 | tf_op jit(solution)/shard_map/ppermute | solution.py:241
  8.1 0.5 collective-permute-start.4
  8.5 3.5 %shard_map.46 = (bf16[1,4096,512]{2,1,0:T(8,128)(2,1)S(1)}, bf16[1,4096,512]{2,1,0:T(8,128)(2,1)S(1)}) custom-call(bf16[1,4096,512]{2,1,0:T(8,128)(2,1)} %gate.1, bf16[1,4096,512]{2,1,0:T(8,128)(2,1)} %up.1), custom_call_target="tpu_custom_call" | custom-call | flops 4194304 | bytes 16777216 | tf_op jit(solution)/shard_map/pallas_call | solution.py:120
  12.0 0.5 collective-permute-done.refs_7_
  12.5 4.4 %collective-permute-start.1 = (bf16[32,4096]{1,0:T(8,128)(2,1)S(1)}, bf16[32,4096]{1,0:T(8,128)(2,1)S(1)}, u32[]{:S(2)}, u32[]{:S(2)}) collective-permute-start(bf16[32,4096]{1,0:T(8,128)(2,1)S(1)} %collective-permute-done.refs_7_), channel_id=1, source_target_pairs={{0,4},{1,5},{2,6},{3,7},{4,0},{5,1},{6,2},{7,3},{8,12},{9,13},{10,... | collective-permute-start | bytes 786440 | tf_op jit(solution)/shard_map/ppermute | solution.py:241
  16.9 0.5 collective-permute-done.9.refs_3_
  17.4 0.0 collective-permute-done.10.refs_2_
  17.4 2.5 %collective-permute-done.8.refs_1_ = bf16[32,4096]{1,0:T(8,128)(2,1)S(1)} collective-permute-done((bf16[32,4096]{1,0:T(8,128)(2,1)}, bf16[32,4096]{1,0:T(8,128)(2,1)S(1)}, u32[]{:S(2)}, u32[]{:S(2)}) %collective-permute-start.8) | collective-permute-done | bytes 262176 | tf_op jit(solution)/shard_map/ppermute | solution.py:241
  19.9 1.5 %collective-permute-start.11 = (bf16[32,4096]{1,0:T(8,128)(2,1)S(1)}, bf16[32,4096]{1,0:T(8,128)(2,1)S(1)}, u32[]{:S(2)}, u32[]{:S(2)}) collective-permute-start(bf16[32,4096]{1,0:T(8,128)(2,1)S(1)} %collective-permute-done.9.refs_3_), channel_id=1, source_target_pairs={{0,16},{1,17},{2,18},{3,19},{4,20},{5,21},{6,22},{7,23},{8,24},{9,... | collective-permute-start | bytes 786440 | tf_op jit(solution)/shard_map/ppermute | solution.py:241
  21.4 0.0 collective-permute-done.4.refs_2_
  21.4 0.6 %collective-permute-start.5 = (bf16[32,4096]{1,0:T(8,128)(2,1)S(1)}, bf16[32,4096]{1,0:T(8,128)(2,1)S(1)}, u32[]{:S(2)}, u32[]{:S(2)}) collective-permute-start(bf16[32,4096]{1,0:T(8,128)(2,1)S(1)} %collective-permute-done.4.refs_2_), channel_id=1, source_target_pairs={{0,12},{1,13},{2,14},{3,15},{4,8},{5,9},{6,10},{7,11},{8,4},{9,5},... | collective-permute-start | bytes 786440 | tf_op jit(solution)/shard_map/ppermute | solution.py:241
  22.0 0.5 collective-permute-start.3
  22.5 1.1 %collective-permute-done.1.refs_5_ = bf16[32,4096]{1,0:T(8,128)(2,1)S(1)} collective-permute-done((bf16[32,4096]{1,0:T(8,128)(2,1)S(1)}, bf16[32,4096]{1,0:T(8,128)(2,1)S(1)}, u32[]{:S(2)}, u32[]{:S(2)}) %collective-permute-start.1) | collective-permute-done | bytes 262176 | tf_op jit(solution)/shard_map/ppermute | solution.py:241
  23.7 1.5 %collective-permute-start.2 = (bf16[32,4096]{1,0:T(8,128)(2,1)S(1)}, bf16[32,4096]{1,0:T(8,128)(2,1)S(1)}, u32[]{:S(2)}, u32[]{:S(2)}) collective-permute-start(bf16[32,4096]{1,0:T(8,128)(2,1)S(1)} %collective-permute-done.1.refs_5_), channel_id=1, source_target_pairs={{0,16},{1,17},{2,18},{3,19},{4,20},{5,21},{6,22},{7,23},{8,24},{9,... | collective-permute-start | bytes 786440 | tf_op jit(solution)/shard_map/ppermute | solution.py:241
  25.2 2.9 %collective-permute-done.11.refs_3_ = bf16[32,4096]{1,0:T(8,128)(2,1)S(1)} collective-permute-done((bf16[32,4096]{1,0:T(8,128)(2,1)S(1)}, bf16[32,4096]{1,0:T(8,128)(2,1)S(1)}, u32[]{:S(2)}, u32[]{:S(2)}) %collective-permute-start.11) | collective-permute-done | bytes 262176 | tf_op jit(solution)/shard_map/ppermute | solution.py:241
  28.1 0.0 collective-permute-start.12
  28.1 1.5 %collective-permute-start.7 = (bf16[32,4096]{1,0:T(8,128)(2,1)S(1)}, bf16[32,4096]{1,0:T(8,128)(2,1)S(1)}, u32[]{:S(2)}, u32[]{:S(2)}) collective-permute-start(bf16[32,4096]{1,0:T(8,128)(2,1)S(1)} %collective-permute-done.refs_7_), channel_id=1, source_target_pairs={{0,16},{1,17},{2,18},{3,19},{4,20},{5,21},{6,22},{7,23},{8,24},{9,... | collective-permute-start | bytes 786440 | tf_op jit(solution)/shard_map/ppermute | solution.py:241
  29.6 0.6 %collective-permute-done.5.refs_4_ = bf16[32,4096]{1,0:T(8,128)(2,1)S(1)} collective-permute-done((bf16[32,4096]{1,0:T(8,128)(2,1)S(1)}, bf16[32,4096]{1,0:T(8,128)(2,1)S(1)}, u32[]{:S(2)}, u32[]{:S(2)}) %collective-permute-start.5) | collective-permute-done | bytes 262176 | tf_op jit(solution)/shard_map/ppermute | solution.py:241
  30.3 3.3 %collective-permute-start.6 = (bf16[32,4096]{1,0:T(8,128)(2,1)S(1)}, bf16[32,4096]{1,0:T(8,128)(2,1)S(1)}, u32[]{:S(2)}, u32[]{:S(2)}) collective-permute-start(bf16[32,4096]{1,0:T(8,128)(2,1)S(1)} %collective-permute-done.5.refs_4_), channel_id=1, source_target_pairs={{0,4},{1,5},{2,6},{3,7},{4,0},{5,1},{6,2},{7,3},{8,12},{9,13},{10,... | collective-permute-start | bytes 786440 | tf_op jit(solution)/shard_map/ppermute | solution.py:241
  33.6 0.0 collective-permute-done.3.refs_8_
  33.6 1.6 %collective-permute-start.13 = (bf16[32,4096]{1,0:T(8,128)(2,1)S(1)}, bf16[32,4096]{1,0:T(8,128)(2,1)S(1)}, u32[]{:S(2)}, u32[]{:S(2)}) collective-permute-start(bf16[32,4096]{1,0:T(8,128)(2,1)S(1)} %collective-permute-done.9.refs_3_), channel_id=1, source_target_pairs={{0,2},{1,3},{2,0},{3,1},{4,6},{5,7},{6,4},{7,5},{8,10},{9,11},{10,... | collective-permute-start | bytes 786440 | tf_op jit(solution)/shard_map/ppermute | solution.py:241
  35.2 0.0 collective-permute-done.2.refs_1_
  35.2 0.4 collective-permute-done.12.refs_4_
  35.6 0.0 copy-done.1
  35.6 1.8 %shard_map.47.refs_7_ = f32[128,1024]{1,0:T(8,128)S(1)} custom-call(f32[2,2]{1,0:T(2,128)S(1)} %copy-done.1, bf16[32,4096]{1,0:T(8,128)(2,1)S(1)} %collective-permute-done.8.refs_1_, bf16[32,4096]{1,0:T(8,128)(2,1)S(1)} %collective-permute-done.4.refs_2_, bf16[32,4096]{1,0:T(8,128)(2,1)S(1)} %collective-permute-done.11.refs_3_, ...), custom_call_target="tpu_custom_call" | custom-call | flops 1073741824 | bytes 9437184 | tf_op jit(solution)/shard_map/pallas_call | solution.py:93
  37.4 0.0 copy-start
  37.4 0.1 collective-permute-done.7.refs_3_
  37.5 0.5 collective-permute-done.6.refs_2_
  37.9 1.9 %shard_map.48 = (f32[128,1024]{1,0:T(8,128)S(1)}, f32[128,1024]{1,0:T(8,128)S(1)}) custom-call(f32[2,2]{1,0:T(2,128)S(1)} %copy-done.1, bf16[32,4096]{1,0:T(8,128)(2,1)S(1)} %collective-permute-done.2.refs_1_, bf16[32,4096]{1,0:T(8,128)(2,1)S(1)} %collective-permute-done.6.refs_2_, bf16[32,4096]{1,0:T(8,128)(2,1)S(1)} %collective-permute-done.7.refs_3_, ...), custom_call_target="tpu_custom_call" | custom-call | flops 1073741824 | bytes 9437184 | tf_op jit(solution)/shard_map/pallas_call | solution.py:93
  39.8 0.3 collective-permute-done.13.refs_4_
  40.1 0.0 collective-permute-start.14
  40.1 1.5 %collective-permute-start.15 = (bf16[32,4096]{1,0:T(8,128)(2,1)S(1)}, bf16[32,4096]{1,0:T(8,128)(2,1)S(1)}, u32[]{:S(2)}, u32[]{:S(2)}) collective-permute-start(bf16[32,4096]{1,0:T(8,128)(2,1)S(1)} %collective-permute-done.1.refs_5_), channel_id=1, source_target_pairs={{0,2},{1,3},{2,0},{3,1},{4,6},{5,7},{6,4},{7,5},{8,10},{9,11},{10,... | collective-permute-start | bytes 786440 | tf_op jit(solution)/shard_map/ppermute | solution.py:241
  41.6 0.4 collective-permute-done.14.received_ref
  42.0 1.0 %shard_map.49 = bf16[128,1152]{1,0:T(8,128)(2,1)S(1)} custom-call(f32[128,1024]{1,0:T(8,128)S(1)} %get-tuple-element.19.kept_ref, f32[128,1024]{1,0:T(8,128)S(1)} %collective-permute-done.14.received_ref), custom_call_target="tpu_custom_call" | custom-call | tf_op jit(solution)/shard_map/pallas_call | solution.py:165
  43.0 1.8 %collective-permute-start.17 = (bf16[128,1152]{1,0:T(8,128)(2,1)S(1)}, bf16[128,1152]{1,0:T(8,128)(2,1)S(1)}, u32[]{:S(2)}, u32[]{:S(2)}) collective-permute-start(bf16[128,1152]{1,0:T(8,128)(2,1)S(1)} %shard_map.49), channel_id=1, source_target_pairs={{0,16},{1,17},{2,18},{3,19},{4,20},{5,21},{6,22},{7,23},{8,24},{9,... | collective-permute-start | bytes 884744 | tf_op jit(solution)/shard_map/ppermute | solution.py:241
  44.7 4.1 %collective-permute-done.15.refs_6_ = bf16[32,4096]{1,0:T(8,128)(2,1)S(1)} collective-permute-done((bf16[32,4096]{1,0:T(8,128)(2,1)S(1)}, bf16[32,4096]{1,0:T(8,128)(2,1)S(1)}, u32[]{:S(2)}, u32[]{:S(2)}) %collective-permute-start.15) | collective-permute-done | bytes 262176 | tf_op jit(solution)/shard_map/ppermute | solution.py:241
  48.8 0.0 copy-done
  48.8 3.0 %shard_map.50 = (f32[128,1024]{1,0:T(8,128)S(1)}, f32[128,1024]{1,0:T(8,128)S(1)}) custom-call(f32[2,2]{1,0:T(2,128)S(1)} %copy-done.1, bf16[32,4096]{1,0:T(8,128)(2,1)S(1)} %bitcast.6, bf16[32,4096]{1,0:T(8,128)(2,1)S(1)} %collective-permute-done.10.refs_2_, bf16[32,4096]{1,0:T(8,128)(2,1)S(1)} %collective-permute-done.9.refs_3_, ...), custom_call_target="tpu_custom_call" | custom-call | flops 2147483648 | bytes 10485760 | tf_op jit(solution)/shard_map/pallas_call | solution.py:93
  51.8 0.1 collective-permute-start.16
  51.9 0.2 collective-permute-done.17.values_ref
  52.1 1.1 %shard_map.51.refs_2_ = f32[128,1024]{1,0:T(8,128)S(1)} custom-call(bf16[128,1152]{1,0:T(8,128)(2,1)S(1)} %collective-permute-done.17.values_ref), custom_call_target="tpu_custom_call" | custom-call | flops 11796480000 | bytes 294912 | tf_op jit(solution)/shard_map/pallas_call | solution.py:193
  53.2 0.6 %collective-permute-done.16.refs_1_ = f32[128,1024]{1,0:T(8,128)S(1)} collective-permute-done((f32[128,1024]{1,0:T(8,128)S(1)}, f32[128,1024]{1,0:T(8,128)S(1)}, u32[]{:S(2)}, u32[]{:S(2)}) %collective-permute-start.16) | collective-permute-done | bytes 524320 | tf_op jit(solution)/shard_map/ppermute | solution.py:241
  53.8 0.8 %shard_map.52 = bf16[1,128,512]{2,1,0:T(8,128)(2,1)} custom-call(f32[128,1024]{1,0:T(8,128)S(1)} %get-tuple-element.23.refs_0_, f32[128,1024]{1,0:T(8,128)S(1)} %collective-permute-done.16.refs_1_, f32[128,1024]{1,0:T(8,128)S(1)} %shard_map.51.refs_2_), custom_call_target="tpu_custom_call" | custom-call | tf_op jit(solution)/shard_map/pallas_call | solution.py:220
Async XLA Ops:
  0.0 35.6 %copy-start.1 = (f32[2,2]{1,0:T(2,128)S(1)}, f32[2,2]{1,0:T(2,128)}, u32[]{:S(2)}) copy-start(f32[2,2]{1,0:T(2,128)} %refs_0_.5) | copy-start | bytes 52
  0.0 12.5 %collective-permute-start = (bf16[32,4096]{1,0:T(8,128)(2,1)}, bf16[32,4096]{1,0:T(8,128)(2,1)S(1)}, u32[]{:S(2)}, u32[]{:S(2)}) collective-permute-start(bf16[32,4096]{1,0:T(8,128)(2,1)} %bitcast.1), channel_id=1, source_target_pairs={{0,12},{1,13},{2,14},{3,15},{4,8},{5,9},{6,10},{7,11},{8,4},{9,5},... | collective-permute-start | bytes 786440 | tf_op jit(solution)/shard_map/ppermute | solution.py:241
  5.1 12.3 %collective-permute-start.9 = (bf16[32,4096]{1,0:T(8,128)(2,1)}, bf16[32,4096]{1,0:T(8,128)(2,1)S(1)}, u32[]{:S(2)}, u32[]{:S(2)}) collective-permute-start(bf16[32,4096]{1,0:T(8,128)(2,1)} %bitcast.2), channel_id=1, source_target_pairs={{0,4},{1,5},{2,6},{3,7},{4,0},{5,1},{6,2},{7,3},{8,12},{9,13},{10,... | collective-permute-start | bytes 786440 | tf_op jit(solution)/shard_map/ppermute | solution.py:241
  5.1 12.3 %collective-permute-start.10 = (bf16[32,4096]{1,0:T(8,128)(2,1)}, bf16[32,4096]{1,0:T(8,128)(2,1)S(1)}, u32[]{:S(2)}, u32[]{:S(2)}) collective-permute-start(bf16[32,4096]{1,0:T(8,128)(2,1)} %bitcast.3), channel_id=1, source_target_pairs={{0,2},{1,3},{2,0},{3,1},{4,6},{5,7},{6,4},{7,5},{8,10},{9,11},{10,... | collective-permute-start | bytes 786440 | tf_op jit(solution)/shard_map/ppermute | solution.py:241
  6.5 13.3 %collective-permute-start.8 = (bf16[32,4096]{1,0:T(8,128)(2,1)}, bf16[32,4096]{1,0:T(8,128)(2,1)S(1)}, u32[]{:S(2)}, u32[]{:S(2)}) collective-permute-start(bf16[32,4096]{1,0:T(8,128)(2,1)} %bitcast.4), channel_id=1, source_target_pairs={{0,16},{1,17},{2,18},{3,19},{4,20},{5,21},{6,22},{7,23},{8,24},{9,... | collective-permute-start | bytes 786440 | tf_op jit(solution)/shard_map/ppermute | solution.py:241
  8.1 13.3 %collective-permute-start.4 = (bf16[32,4096]{1,0:T(8,128)(2,1)}, bf16[32,4096]{1,0:T(8,128)(2,1)S(1)}, u32[]{:S(2)}, u32[]{:S(2)}) collective-permute-start(bf16[32,4096]{1,0:T(8,128)(2,1)} %bitcast.5), channel_id=1, source_target_pairs={{0,18},{1,19},{2,16},{3,17},{4,22},{5,23},{6,20},{7,21},{8,26},{9,... | collective-permute-start | bytes 786440 | tf_op jit(solution)/shard_map/ppermute | solution.py:241
  12.5 11.2 %collective-permute-start.1 = (bf16[32,4096]{1,0:T(8,128)(2,1)S(1)}, bf16[32,4096]{1,0:T(8,128)(2,1)S(1)}, u32[]{:S(2)}, u32[]{:S(2)}) collective-permute-start(bf16[32,4096]{1,0:T(8,128)(2,1)S(1)} %collective-permute-done.refs_7_), channel_id=1, source_target_pairs={{0,4},{1,5},{2,6},{3,7},{4,0},{5,1},{6,2},{7,3},{8,12},{9,13},{10,... | collective-permute-start | bytes 786440 | tf_op jit(solution)/shard_map/ppermute | solution.py:241
  19.9 8.2 %collective-permute-start.11 = (bf16[32,4096]{1,0:T(8,128)(2,1)S(1)}, bf16[32,4096]{1,0:T(8,128)(2,1)S(1)}, u32[]{:S(2)}, u32[]{:S(2)}) collective-permute-start(bf16[32,4096]{1,0:T(8,128)(2,1)S(1)} %collective-permute-done.9.refs_3_), channel_id=1, source_target_pairs={{0,16},{1,17},{2,18},{3,19},{4,20},{5,21},{6,22},{7,23},{8,24},{9,... | collective-permute-start | bytes 786440 | tf_op jit(solution)/shard_map/ppermute | solution.py:241
  21.4 8.9 %collective-permute-start.5 = (bf16[32,4096]{1,0:T(8,128)(2,1)S(1)}, bf16[32,4096]{1,0:T(8,128)(2,1)S(1)}, u32[]{:S(2)}, u32[]{:S(2)}) collective-permute-start(bf16[32,4096]{1,0:T(8,128)(2,1)S(1)} %collective-permute-done.4.refs_2_), channel_id=1, source_target_pairs={{0,12},{1,13},{2,14},{3,15},{4,8},{5,9},{6,10},{7,11},{8,4},{9,5},... | collective-permute-start | bytes 786440 | tf_op jit(solution)/shard_map/ppermute | solution.py:241
  22.0 11.6 %collective-permute-start.3 = (bf16[32,4096]{1,0:T(8,128)(2,1)S(1)}, bf16[32,4096]{1,0:T(8,128)(2,1)S(1)}, u32[]{:S(2)}, u32[]{:S(2)}) collective-permute-start(bf16[32,4096]{1,0:T(8,128)(2,1)S(1)} %collective-permute-done.refs_7_), channel_id=1, source_target_pairs={{0,2},{1,3},{2,0},{3,1},{4,6},{5,7},{6,4},{7,5},{8,10},{9,11},{10,... | collective-permute-start | bytes 786440 | tf_op jit(solution)/shard_map/ppermute | solution.py:241
  23.7 11.5 %collective-permute-start.2 = (bf16[32,4096]{1,0:T(8,128)(2,1)S(1)}, bf16[32,4096]{1,0:T(8,128)(2,1)S(1)}, u32[]{:S(2)}, u32[]{:S(2)}) collective-permute-start(bf16[32,4096]{1,0:T(8,128)(2,1)S(1)} %collective-permute-done.1.refs_5_), channel_id=1, source_target_pairs={{0,16},{1,17},{2,18},{3,19},{4,20},{5,21},{6,22},{7,23},{8,24},{9,... | collective-permute-start | bytes 786440 | tf_op jit(solution)/shard_map/ppermute | solution.py:241
  28.1 7.5 %collective-permute-start.12 = (bf16[32,4096]{1,0:T(8,128)(2,1)S(1)}, bf16[32,4096]{1,0:T(8,128)(2,1)S(1)}, u32[]{:S(2)}, u32[]{:S(2)}) collective-permute-start(bf16[32,4096]{1,0:T(8,128)(2,1)S(1)} %collective-permute-done.11.refs_3_), channel_id=1, source_target_pairs={{0,2},{1,3},{2,0},{3,1},{4,6},{5,7},{6,4},{7,5},{8,10},{9,11},{10,... | collective-permute-start | bytes 786440 | tf_op jit(solution)/shard_map/ppermute | solution.py:241
  28.1 9.4 %collective-permute-start.7 = (bf16[32,4096]{1,0:T(8,128)(2,1)S(1)}, bf16[32,4096]{1,0:T(8,128)(2,1)S(1)}, u32[]{:S(2)}, u32[]{:S(2)}) collective-permute-start(bf16[32,4096]{1,0:T(8,128)(2,1)S(1)} %collective-permute-done.refs_7_), channel_id=1, source_target_pairs={{0,16},{1,17},{2,18},{3,19},{4,20},{5,21},{6,22},{7,23},{8,24},{9,... | collective-permute-start | bytes 786440 | tf_op jit(solution)/shard_map/ppermute | solution.py:241
  30.3 7.7 %collective-permute-start.6 = (bf16[32,4096]{1,0:T(8,128)(2,1)S(1)}, bf16[32,4096]{1,0:T(8,128)(2,1)S(1)}, u32[]{:S(2)}, u32[]{:S(2)}) collective-permute-start(bf16[32,4096]{1,0:T(8,128)(2,1)S(1)} %collective-permute-done.5.refs_4_), channel_id=1, source_target_pairs={{0,4},{1,5},{2,6},{3,7},{4,0},{5,1},{6,2},{7,3},{8,12},{9,13},{10,... | collective-permute-start | bytes 786440 | tf_op jit(solution)/shard_map/ppermute | solution.py:241
  33.6 6.5 %collective-permute-start.13 = (bf16[32,4096]{1,0:T(8,128)(2,1)S(1)}, bf16[32,4096]{1,0:T(8,128)(2,1)S(1)}, u32[]{:S(2)}, u32[]{:S(2)}) collective-permute-start(bf16[32,4096]{1,0:T(8,128)(2,1)S(1)} %collective-permute-done.9.refs_3_), channel_id=1, source_target_pairs={{0,2},{1,3},{2,0},{3,1},{4,6},{5,7},{6,4},{7,5},{8,10},{9,11},{10,... | collective-permute-start | bytes 786440 | tf_op jit(solution)/shard_map/ppermute | solution.py:241
  37.4 11.4 %copy-start = (bf16[1,32,4096]{2,1,0:T(8,128)(2,1)S(1)}, bf16[1,32,4096]{2,1,0:T(8,128)(2,1)}, u32[]{:S(2)}) copy-start(bf16[1,32,4096]{2,1,0:T(8,128)(2,1)} %param.4) | copy-start | bytes 786436
  40.1 1.9 %collective-permute-start.14 = (f32[128,1024]{1,0:T(8,128)S(1)}, f32[128,1024]{1,0:T(8,128)S(1)}, u32[]{:S(2)}, u32[]{:S(2)}) collective-permute-start(f32[128,1024]{1,0:T(8,128)S(1)} %get-tuple-element.21), channel_id=1, source_target_pairs={{0,1},{1,0},{2,3},{3,2},{4,5},{5,4},{6,7},{7,6},{8,9},{9,8},{10,11... | collective-permute-start | bytes 1572872 | tf_op jit(solution)/shard_map/ppermute | solution.py:241
  40.1 8.7 %collective-permute-start.15 = (bf16[32,4096]{1,0:T(8,128)(2,1)S(1)}, bf16[32,4096]{1,0:T(8,128)(2,1)S(1)}, u32[]{:S(2)}, u32[]{:S(2)}) collective-permute-start(bf16[32,4096]{1,0:T(8,128)(2,1)S(1)} %collective-permute-done.1.refs_5_), channel_id=1, source_target_pairs={{0,2},{1,3},{2,0},{3,1},{4,6},{5,7},{6,4},{7,5},{8,10},{9,11},{10,... | collective-permute-start | bytes 786440 | tf_op jit(solution)/shard_map/ppermute | solution.py:241
  43.0 9.1 %collective-permute-start.17 = (bf16[128,1152]{1,0:T(8,128)(2,1)S(1)}, bf16[128,1152]{1,0:T(8,128)(2,1)S(1)}, u32[]{:S(2)}, u32[]{:S(2)}) collective-permute-start(bf16[128,1152]{1,0:T(8,128)(2,1)S(1)} %shard_map.49), channel_id=1, source_target_pairs={{0,16},{1,17},{2,18},{3,19},{4,20},{5,21},{6,22},{7,23},{8,24},{9,... | collective-permute-start | bytes 884744 | tf_op jit(solution)/shard_map/ppermute | solution.py:241
  51.8 2.0 %collective-permute-start.16 = (f32[128,1024]{1,0:T(8,128)S(1)}, f32[128,1024]{1,0:T(8,128)S(1)}, u32[]{:S(2)}, u32[]{:S(2)}) collective-permute-start(f32[128,1024]{1,0:T(8,128)S(1)} %get-tuple-element.24), channel_id=1, source_target_pairs={{0,1},{1,0},{2,3},{3,2},{4,5},{5,4},{6,7},{7,6},{8,9},{9,8},{10,11... | collective-permute-start | bytes 1572872 | tf_op jit(solution)/shard_map/ppermute | solution.py:241

commit v6 on v5

--- a/solution.py
+++ b/solution.py
@@ -134,6 +134,12 @@
 STEPS = 4016
 FIELD = 128
 SHIFT = 125
+TAIL = 16
+
+
+def diagonal(side):
+    shape = (side, side)
+    return lax.broadcasted_iota(jnp.int32, shape, 0) == lax.broadcasted_iota(jnp.int32, shape, 1)
 
 
 def coded(kept, received):
@@ -141,15 +147,14 @@
     side = width // 2
 
     def kernel(kept_ref, received_ref, out):
-        lane = lax.broadcasted_iota(jnp.int32, (rows, FIELD), 1)
         scales = []
         for start in (0, side):
             columns = slice(start, start + side)
             total = kept_ref[:, columns] + received_ref[:, columns]
             size = jnp.abs(total)
-            top = jnp.maximum(jnp.max(size, axis=1, keepdims=True), 1e-30) * 1.01
+            top = jnp.maximum(jnp.max(size, axis=1, keepdims=True), 1e-36) * 1.01
             top = top.astype(jnp.bfloat16).astype(jnp.float32)
-            scales.append(top)
+            scales.append(jnp.sum(jnp.where(diagonal(rows), top, 0.0), axis=0, keepdims=True))
             part = size * (1 / top)
             level = part * 2.0**SEGMENTS
             for k in range(1, SEGMENTS):
@@ -158,13 +163,16 @@
             power = jnp.floor(number * (1 / FIELD))
             fraction = (number - power * FIELD) * (1 / FIELD)
             value = jnp.exp2(power - SHIFT) * (1 + fraction)
-            out[:, columns] = jnp.where(total < 0, -value, value).astype(jnp.bfloat16)
-        out[:, width:] = jnp.where(lane < FIELD // 2, scales[0], scales[1]).astype(jnp.bfloat16)
-
-    whole = pl.BlockSpec(memory_space=pltpu.VMEM)
-    return pl.pallas_call(
-        kernel,
-        out_shape=jax.ShapeDtypeStruct((rows, width + FIELD), jnp.bfloat16),
+            value = jnp.where(total < 0, -value, value).astype(jnp.bfloat16)
+            for at in range(0, side, rows):
+                out[start + at : start + at + rows, :] = value[:, at : at + rows]
+        row = lax.broadcasted_iota(jnp.int32, (TAIL, rows), 0)
+        out[width:, :] = jnp.where(row == 0, scales[0], scales[1]).astype(jnp.bfloat16)
+
+    whole = pl.BlockSpec(memory_space=pltpu.VMEM)
+    return pl.pallas_call(
+        kernel,
+        out_shape=jax.ShapeDtypeStruct((width + TAIL, rows), jnp.bfloat16),
         in_specs=[whole] * 2,
         out_specs=whole,
         compiler_params=pltpu.CompilerParams(vmem_limit_bytes=24 * 2**20),
@@ -172,32 +180,34 @@
 
 
 def decoded(values, work):
-    rows, side = values.shape[0], (values.shape[1] - FIELD) // 2
+    rows = values.shape[1]
+    width = values.shape[0] - TAIL
+    side = width // 2
 
     def kernel(values_ref, out):
+        scales = values_ref[width:, :].astype(jnp.float32)
         for j in range(2):
-            columns = slice(j * side, (j + 1) * side)
-            at = 2 * side + j * (FIELD // 2)
-            scale = values_ref[:, at : at + 1].astype(jnp.float32)
-            value = values_ref[:, columns].astype(jnp.float32)
-            size = jnp.abs(value)
-            power = jnp.floor(jnp.log2(size) + 0.001)
-            fraction = jnp.floor((size * jnp.exp2(-power) - 1) * FIELD + 0.5)
-            level = ((power + SHIFT) * FIELD + fraction) * (1 / STEPS)
-            part = level * 2.0**-SEGMENTS
-            for k in range(1, SEGMENTS):
-                part = jnp.maximum(part, (level - k) * 2.0 ** (k - SEGMENTS))
-            out[:, columns] = jnp.where(value < 0, -part, part) * scale
-
-    whole = pl.BlockSpec(memory_space=pltpu.VMEM)
-    return pl.pallas_call(
-        kernel,
-        out_shape=jax.ShapeDtypeStruct((rows, 2 * side), jnp.float32),
+            scale = jnp.sum(jnp.where(diagonal(rows), scales[j : j + 1, :], 0.0), axis=1, keepdims=True)
+            for at in range(j * side, (j + 1) * side, rows):
+                value = values_ref[at : at + rows, :].astype(jnp.float32)
+                size = jnp.abs(value)
+                power = jnp.floor(jnp.log2(size) + 0.001)
+                fraction = jnp.floor((size * jnp.exp2(-power) - 1) * FIELD + 0.5)
+                level = ((power + SHIFT) * FIELD + fraction) * (1 / STEPS)
+                part = level * 2.0**-SEGMENTS
+                for k in range(1, SEGMENTS):
+                    part = jnp.maximum(part, (level - k) * 2.0 ** (k - SEGMENTS))
+                out[:, at : at + rows] = jnp.where(value < 0, -part, part) * scale
+
+    whole = pl.BlockSpec(memory_space=pltpu.VMEM)
+    return pl.pallas_call(
+        kernel,
+        out_shape=jax.ShapeDtypeStruct((rows, width), jnp.float32),
         in_specs=[whole],
         out_specs=whole,
         compiler_params=pltpu.CompilerParams(vmem_limit_bytes=24 * 2**20),
         cost_estimate=pl.CostEstimate(
-            flops=work * 60 * rows * side, bytes_accessed=2 * values.size, transcendentals=0
+            flops=work * 30 * values.size, bytes_accessed=2 * values.size, transcendentals=0
         ),
     )(values)
 
@@ -263,7 +273,8 @@
         sent, kept = products([after(y2, x3), d2, y3, d3], False, coefficients, held, 1, half, near)
         other = coded(kept, swap(after(sent, x1), row=1))
         from_other = swap(other, src=1)
-        sent_own, kept_own = products([after(b0, other), x0, z1, x1, z2, x2, z3, x3], True, coefficients, held, 1, half)
+        near_own = products([b0, x0, z1, x1], True, coefficients, held, 1)
+        sent_own, kept_own = products([z2, x2, z3, x3], True, coefficients, held, 1, half, near_own)
         core_own = swap(sent_own, row=1)
         theirs = decoded(from_other, 3000)
         return activated((kept_own, core_own, theirs), rows)

time: 54.9 us -> 53.4 us (0.973)
  waiting for transfers between devices: 14.5 us -> 10.1 us
  starting transfers between devices: 27 us -> 29.6 us
    ppermute x18, waiting for transfers between devices: 14.5 us -> 10.1 us  [swap(): return lax.ppermute(array, AXES, pairs)]
    ppermute x18, starting transfers between devices: 27 us -> 29.6 us  [swap(): return lax.ppermute(array, AXES, pairs)]
    pallas_call x3 -> x4, Pallas kernels: 6.69 us -> 7.36 us  [products(): pl.pallas_call(kernel, out_shape=[jax.ShapeDtypeStruct((span, 2 * width),...]
  transfers between devices with their start and end apart: 18 -> 18, of which waited for: 14 -> 12; matrix products, arithmetic and copies ran while one was open for 0% -> 0% of each run, Pallas kernels for 22% -> 24%
where the time goes in v6:
time: 53.4 us; the launch traced here: 53.2 us
  starting transfers between devices  29.6 us (55%)
  Pallas kernels  13.4 us (25%)
  waiting for transfers between devices  10.1 us (19%)
    ppermute x18, starting transfers between devices, swap(): return lax.ppermute(array, AXES, pairs)  29.6 us
    ppermute x18, waiting for transfers between devices, swap(): return lax.ppermute(array, AXES, pairs)  10.1 us
    pallas_call x4, Pallas kernels, products(): pl.pallas_call(kernel, out_shape=[jax.ShapeDtypeStruct((span, 2 * width),...  7.36 us
    pallas_call x1, Pallas kernels, resident(): pl.pallas_call(kernel, out_shape=[pltpu.VMEM(w.shape, w.dtype) for w in (...  3.48 us
  transfers between devices with their start and end apart: 18, of which 12 were waited for; matrix products, arithmetic and copies ran while one was open for 0% of the time, Pallas kernels for 24%

profile of v6, /device:TPU:0, one launch (start us, length us, event | category | flops | bytes accessed | tf_op | source)
XLA Modules:
  0.0 53.2 jit_solution(9903359963181923964)
XLA Ops:
  0.0 0.0 copy-start.1
  0.0 5.0 %collective-permute-start = (bf16[32,4096]{1,0:T(8,128)(2,1)}, bf16[32,4096]{1,0:T(8,128)(2,1)S(1)}, u32[]{:S(2)}, u32[]{:S(2)}) collective-permute-start(bf16[32,4096]{1,0:T(8,128)(2,1)} %bitcast.1), channel_id=1, source_target_pairs={{0,12},{1,13},{2,14},{3,15},{4,8},{5,9},{6,10},{7,11},{8,4},{9,5},... | collective-permute-start | bytes 786440 | tf_op jit(solution)/shard_map/ppermute | solution.py:251
  5.1 0.0 collective-permute-start.5
  5.1 1.5 %collective-permute-start.13 = (bf16[32,4096]{1,0:T(8,128)(2,1)}, bf16[32,4096]{1,0:T(8,128)(2,1)S(1)}, u32[]{:S(2)}, u32[]{:S(2)}) collective-permute-start(bf16[32,4096]{1,0:T(8,128)(2,1)} %bitcast.3), channel_id=1, source_target_pairs={{0,16},{1,17},{2,18},{3,19},{4,20},{5,21},{6,22},{7,23},{8,24},{9,... | collective-permute-start | bytes 786440 | tf_op jit(solution)/shard_map/ppermute | solution.py:251
  6.6 1.5 %collective-permute-start.4 = (bf16[32,4096]{1,0:T(8,128)(2,1)}, bf16[32,4096]{1,0:T(8,128)(2,1)S(1)}, u32[]{:S(2)}, u32[]{:S(2)}) collective-permute-start(bf16[32,4096]{1,0:T(8,128)(2,1)} %bitcast.4), channel_id=1, source_target_pairs={{0,2},{1,3},{2,0},{3,1},{4,6},{5,7},{6,4},{7,5},{8,10},{9,11},{10,... | collective-permute-start | bytes 786440 | tf_op jit(solution)/shard_map/ppermute | solution.py:251
  8.1 0.5 collective-permute-start.9
  8.5 3.5 %shard_map.46 = (bf16[1,4096,512]{2,1,0:T(8,128)(2,1)S(1)}, bf16[1,4096,512]{2,1,0:T(8,128)(2,1)S(1)}) custom-call(bf16[1,4096,512]{2,1,0:T(8,128)(2,1)} %gate.1, bf16[1,4096,512]{2,1,0:T(8,128)(2,1)} %up.1), custom_call_target="tpu_custom_call" | custom-call | flops 4194304 | bytes 16777216 | tf_op jit(solution)/shard_map/pallas_call | solution.py:120
  12.0 0.5 collective-permute-done.refs_3_
  12.5 4.4 %collective-permute-start.1 = (bf16[32,4096]{1,0:T(8,128)(2,1)S(1)}, bf16[32,4096]{1,0:T(8,128)(2,1)S(1)}, u32[]{:S(2)}, u32[]{:S(2)}) collective-permute-start(bf16[32,4096]{1,0:T(8,128)(2,1)S(1)} %collective-permute-done.refs_3_), channel_id=1, source_target_pairs={{0,4},{1,5},{2,6},{3,7},{4,0},{5,1},{6,2},{7,3},{8,12},{9,13},{10,... | collective-permute-start | bytes 786440 | tf_op jit(solution)/shard_map/ppermute | solution.py:251
  16.9 0.5 collective-permute-done.5.refs_3_
  17.4 0.0 collective-permute-done.13.refs_1_
  17.4 0.0 collective-permute-done.4.refs_2_
  17.4 1.5 %collective-permute-start.14 = (bf16[32,4096]{1,0:T(8,128)(2,1)S(1)}, bf16[32,4096]{1,0:T(8,128)(2,1)S(1)}, u32[]{:S(2)}, u32[]{:S(2)}) collective-permute-start(bf16[32,4096]{1,0:T(8,128)(2,1)S(1)} %collective-permute-done.5.refs_3_), channel_id=1, source_target_pairs={{0,16},{1,17},{2,18},{3,19},{4,20},{5,21},{6,22},{7,23},{8,24},{9,... | collective-permute-start | bytes 786440 | tf_op jit(solution)/shard_map/ppermute | solution.py:251
  18.9 0.9 %collective-permute-done.9.refs_2_ = bf16[32,4096]{1,0:T(8,128)(2,1)S(1)} collective-permute-done((bf16[32,4096]{1,0:T(8,128)(2,1)}, bf16[32,4096]{1,0:T(8,128)(2,1)S(1)}, u32[]{:S(2)}, u32[]{:S(2)}) %collective-permute-start.9) | collective-permute-done | bytes 262176 | tf_op jit(solution)/shard_map/ppermute | solution.py:251
  19.8 1.1 %collective-permute-start.10 = (bf16[32,4096]{1,0:T(8,128)(2,1)S(1)}, bf16[32,4096]{1,0:T(8,128)(2,1)S(1)}, u32[]{:S(2)}, u32[]{:S(2)}) collective-permute-start(bf16[32,4096]{1,0:T(8,128)(2,1)S(1)} %collective-permute-done.9.refs_2_), channel_id=1, source_target_pairs={{0,12},{1,13},{2,14},{3,15},{4,8},{5,9},{6,10},{7,11},{8,4},{9,5},... | collective-permute-start | bytes 786440 | tf_op jit(solution)/shard_map/ppermute | solution.py:251
  21.0 1.5 %collective-permute-start.3 = (bf16[32,4096]{1,0:T(8,128)(2,1)S(1)}, bf16[32,4096]{1,0:T(8,128)(2,1)S(1)}, u32[]{:S(2)}, u32[]{:S(2)}) collective-permute-start(bf16[32,4096]{1,0:T(8,128)(2,1)S(1)} %collective-permute-done.refs_3_), channel_id=1, source_target_pairs={{0,2},{1,3},{2,0},{3,1},{4,6},{5,7},{6,4},{7,5},{8,10},{9,11},{10,... | collective-permute-start | bytes 786440 | tf_op jit(solution)/shard_map/ppermute | solution.py:251
  22.5 1.2 %collective-permute-done.1.refs_1_ = bf16[32,4096]{1,0:T(8,128)(2,1)S(1)} collective-permute-done((bf16[32,4096]{1,0:T(8,128)(2,1)S(1)}, bf16[32,4096]{1,0:T(8,128)(2,1)S(1)}, u32[]{:S(2)}, u32[]{:S(2)}) %collective-permute-start.1) | collective-permute-done | bytes 262176 | tf_op jit(solution)/shard_map/ppermute | solution.py:251
  23.7 1.5 %collective-permute-start.8 = (bf16[32,4096]{1,0:T(8,128)(2,1)S(1)}, bf16[32,4096]{1,0:T(8,128)(2,1)S(1)}, u32[]{:S(2)}, u32[]{:S(2)}) collective-permute-start(bf16[32,4096]{1,0:T(8,128)(2,1)S(1)} %collective-permute-done.1.refs_1_), channel_id=1, source_target_pairs={{0,16},{1,17},{2,18},{3,19},{4,20},{5,21},{6,22},{7,23},{8,24},{9,... | collective-permute-start | bytes 786440 | tf_op jit(solution)/shard_map/ppermute | solution.py:251
  25.2 1.4 %collective-permute-done.14.refs_3_ = bf16[32,4096]{1,0:T(8,128)(2,1)S(1)} collective-permute-done((bf16[32,4096]{1,0:T(8,128)(2,1)S(1)}, bf16[32,4096]{1,0:T(8,128)(2,1)S(1)}, u32[]{:S(2)}, u32[]{:S(2)}) %collective-permute-start.14) | collective-permute-done | bytes 262176 | tf_op jit(solution)/shard_map/ppermute | solution.py:251
  26.6 1.5 %collective-permute-start.15 = (bf16[32,4096]{1,0:T(8,128)(2,1)S(1)}, bf16[32,4096]{1,0:T(8,128)(2,1)S(1)}, u32[]{:S(2)}, u32[]{:S(2)}) collective-permute-start(bf16[32,4096]{1,0:T(8,128)(2,1)S(1)} %collective-permute-done.14.refs_3_), channel_id=1, source_target_pairs={{0,2},{1,3},{2,0},{3,1},{4,6},{5,7},{6,4},{7,5},{8,10},{9,11},{10,... | collective-permute-start | bytes 786440 | tf_op jit(solution)/shard_map/ppermute | solution.py:251
  28.1 1.5 %collective-permute-start.12 = (bf16[32,4096]{1,0:T(8,128)(2,1)S(1)}, bf16[32,4096]{1,0:T(8,128)(2,1)S(1)}, u32[]{:S(2)}, u32[]{:S(2)}) collective-permute-start(bf16[32,4096]{1,0:T(8,128)(2,1)S(1)} %collective-permute-done.refs_3_), channel_id=1, source_target_pairs={{0,16},{1,17},{2,18},{3,19},{4,20},{5,21},{6,22},{7,23},{8,24},{9,... | collective-permute-start | bytes 786440 | tf_op jit(solution)/shard_map/ppermute | solution.py:251
  29.6 0.7 %collective-permute-done.10.refs_4_ = bf16[32,4096]{1,0:T(8,128)(2,1)S(1)} collective-permute-done((bf16[32,4096]{1,0:T(8,128)(2,1)S(1)}, bf16[32,4096]{1,0:T(8,128)(2,1)S(1)}, u32[]{:S(2)}, u32[]{:S(2)}) %collective-permute-start.10) | collective-permute-done | bytes 262176 | tf_op jit(solution)/shard_map/ppermute | solution.py:251
  30.2 3.2 %collective-permute-start.11 = (bf16[32,4096]{1,0:T(8,128)(2,1)S(1)}, bf16[32,4096]{1,0:T(8,128)(2,1)S(1)}, u32[]{:S(2)}, u32[]{:S(2)}) collective-permute-start(bf16[32,4096]{1,0:T(8,128)(2,1)S(1)} %collective-permute-done.10.refs_4_), channel_id=1, source_target_pairs={{0,4},{1,5},{2,6},{3,7},{4,0},{5,1},{6,2},{7,3},{8,12},{9,13},{10,... | collective-permute-start | bytes 786440 | tf_op jit(solution)/shard_map/ppermute | solution.py:251
  33.5 0.0 collective-permute-done.3.refs_4_
  33.5 1.5 %collective-permute-start.6 = (bf16[32,4096]{1,0:T(8,128)(2,1)S(1)}, bf16[32,4096]{1,0:T(8,128)(2,1)S(1)}, u32[]{:S(2)}, u32[]{:S(2)}) collective-permute-start(bf16[32,4096]{1,0:T(8,128)(2,1)S(1)} %collective-permute-done.5.refs_3_), channel_id=1, source_target_pairs={{0,2},{1,3},{2,0},{3,1},{4,6},{5,7},{6,4},{7,5},{8,10},{9,11},{10,... | collective-permute-start | bytes 786440 | tf_op jit(solution)/shard_map/ppermute | solution.py:251
  35.0 0.0 collective-permute-done.8.refs_1_
  35.0 0.0 collective-permute-done.15.refs_4_
  35.0 0.0 copy-done.1
  35.0 1.8 %shard_map.49.refs_7_ = f32[128,1024]{1,0:T(8,128)S(1)} custom-call(f32[2,2]{1,0:T(2,128)S(1)} %copy-done.1, bf16[32,4096]{1,0:T(8,128)(2,1)S(1)} %collective-permute-done.13.refs_1_, bf16[32,4096]{1,0:T(8,128)(2,1)S(1)} %collective-permute-done.9.refs_2_, bf16[32,4096]{1,0:T(8,128)(2,1)S(1)} %collective-permute-done.14.refs_3_, ...), custom_call_target="tpu_custom_call" | custom-call | flops 1073741824 | bytes 9437184 | tf_op jit(solution)/shard_map/pallas_call | solution.py:93
  36.8 0.0 copy-start
  36.8 0.0 collective-permute-done.12.refs_3_
  36.8 1.0 %collective-permute-done.11.refs_2_ = bf16[32,4096]{1,0:T(8,128)(2,1)S(1)} collective-permute-done((bf16[32,4096]{1,0:T(8,128)(2,1)S(1)}, bf16[32,4096]{1,0:T(8,128)(2,1)S(1)}, u32[]{:S(2)}, u32[]{:S(2)}) %collective-permute-start.11) | collective-permute-done | bytes 262176 | tf_op jit(solution)/shard_map/ppermute | solution.py:251
  37.8 1.9 %shard_map.50 = (f32[128,1024]{1,0:T(8,128)S(1)}, f32[128,1024]{1,0:T(8,128)S(1)}) custom-call(f32[2,2]{1,0:T(2,128)S(1)} %copy-done.1, bf16[32,4096]{1,0:T(8,128)(2,1)S(1)} %collective-permute-done.8.refs_1_, bf16[32,4096]{1,0:T(8,128)(2,1)S(1)} %collective-permute-done.11.refs_2_, bf16[32,4096]{1,0:T(8,128)(2,1)S(1)} %collective-permute-done.12.refs_3_, ...), custom_call_target="tpu_custom_call" | custom-call | flops 1073741824 | bytes 9437184 | tf_op jit(solution)/shard_map/pallas_call | solution.py:93
  39.7 0.1 collective-permute-done.6.refs_4_
  39.9 0.0 collective-permute-start.16
  39.9 1.5 %collective-permute-start.2 = (bf16[32,4096]{1,0:T(8,128)(2,1)S(1)}, bf16[32,4096]{1,0:T(8,128)(2,1)S(1)}, u32[]{:S(2)}, u32[]{:S(2)}) collective-permute-start(bf16[32,4096]{1,0:T(8,128)(2,1)S(1)} %collective-permute-done.1.refs_1_), channel_id=1, source_target_pairs={{0,2},{1,3},{2,0},{3,1},{4,6},{5,7},{6,4},{7,5},{8,10},{9,11},{10,... | collective-permute-start | bytes 786440 | tf_op jit(solution)/shard_map/ppermute | solution.py:251
  41.3 0.4 collective-permute-done.16.received_ref
  41.8 1.0 %shard_map.51 = bf16[1040,128]{1,0:T(8,128)(2,1)S(1)} custom-call(f32[128,1024]{1,0:T(8,128)S(1)} %get-tuple-element.20.kept_ref, f32[128,1024]{1,0:T(8,128)S(1)} %collective-permute-done.16.received_ref), custom_call_target="tpu_custom_call" | custom-call | tf_op jit(solution)/shard_map/pallas_call | solution.py:173
  42.8 1.7 %collective-permute-start.17 = (bf16[1040,128]{1,0:T(8,128)(2,1)S(1)}, bf16[1040,128]{1,0:T(8,128)(2,1)S(1)}, u32[]{:S(2)}, u32[]{:S(2)}) collective-permute-start(bf16[1040,128]{1,0:T(8,128)(2,1)S(1)} %shard_map.51), channel_id=1, source_target_pairs={{0,16},{1,17},{2,18},{3,19},{4,20},{5,21},{6,22},{7,23},{8,24},{9,... | collective-permute-start | bytes 798728 | tf_op jit(solution)/shard_map/ppermute | solution.py:251
  44.4 0.0 copy-done
  44.4 1.8 %shard_map.47.refs_7_ = f32[128,1024]{1,0:T(8,128)S(1)} custom-call(f32[2,2]{1,0:T(2,128)S(1)} %copy-done.1, bf16[32,4096]{1,0:T(8,128)(2,1)S(1)} %bitcast.6, bf16[32,4096]{1,0:T(8,128)(2,1)S(1)} %collective-permute-done.4.refs_2_, bf16[32,4096]{1,0:T(8,128)(2,1)S(1)} %collective-permute-done.5.refs_3_, bf16[32,4096]{1,0:T(8,128)(2,1)S(1)} %collective-permute-done.6.refs_4_, ...), custom_call_target="tpu_custom_call" | custom-call | flops 1073741824 | bytes 9437184 | tf_op jit(solution)/shard_map/pallas_call | solution.py:93
  46.3 2.3 %collective-permute-done.2.refs_2_ = bf16[32,4096]{1,0:T(8,128)(2,1)S(1)} collective-permute-done((bf16[32,4096]{1,0:T(8,128)(2,1)S(1)}, bf16[32,4096]{1,0:T(8,128)(2,1)S(1)}, u32[]{:S(2)}, u32[]{:S(2)}) %collective-permute-start.2) | collective-permute-done | bytes 262176 | tf_op jit(solution)/shard_map/ppermute | solution.py:251
  48.6 1.9 %shard_map.48 = (f32[128,1024]{1,0:T(8,128)S(1)}, f32[128,1024]{1,0:T(8,128)S(1)}) custom-call(f32[2,2]{1,0:T(2,128)S(1)} %copy-done.1, bf16[32,4096]{1,0:T(8,128)(2,1)S(1)} %collective-permute-done.1.refs_1_, bf16[32,4096]{1,0:T(8,128)(2,1)S(1)} %collective-permute-done.2.refs_2_, bf16[32,4096]{1,0:T(8,128)(2,1)S(1)} %collective-permute-done.refs_3_, ...), custom_call_target="tpu_custom_call" | custom-call | flops 1073741824 | bytes 9437184 | tf_op jit(solution)/shard_map/pallas_call | solution.py:93
  50.4 0.1 collective-permute-start.7
  50.5 0.7 %collective-permute-done.17.values_ref = bf16[1040,128]{1,0:T(8,128)(2,1)S(1)} collective-permute-done((bf16[1040,128]{1,0:T(8,128)(2,1)S(1)}, bf16[1040,128]{1,0:T(8,128)(2,1)S(1)}, u32[]{:S(2)}, u32[]{:S(2)}) %collective-permute-start.17) | collective-permute-done | bytes 266272 | tf_op jit(solution)/shard_map/ppermute | solution.py:251
  51.3 0.8 %shard_map.52.refs_2_ = f32[128,1024]{1,0:T(8,128)S(1)} custom-call(bf16[1040,128]{1,0:T(8,128)(2,1)S(1)} %collective-permute-done.17.values_ref), custom_call_target="tpu_custom_call" | custom-call | flops 11980800000 | bytes 266240 | tf_op jit(solution)/shard_map/pallas_call | solution.py:203
  52.1 0.3 collective-permute-done.7.refs_1_
  52.4 0.8 %shard_map.53 = bf16[1,128,512]{2,1,0:T(8,128)(2,1)} custom-call(f32[128,1024]{1,0:T(8,128)S(1)} %get-tuple-element.16.refs_0_, f32[128,1024]{1,0:T(8,128)S(1)} %collective-permute-done.7.refs_1_, f32[128,1024]{1,0:T(8,128)S(1)} %shard_map.52.refs_2_), custom_call_target="tpu_custom_call" | custom-call | tf_op jit(solution)/shard_map/pallas_call | solution.py:230
Async XLA Ops:
  0.0 35.0 %copy-start.1 = (f32[2,2]{1,0:T(2,128)S(1)}, f32[2,2]{1,0:T(2,128)}, u32[]{:S(2)}) copy-start(f32[2,2]{1,0:T(2,128)} %refs_0_.7) | copy-start | bytes 52
  0.0 12.5 %collective-permute-start = (bf16[32,4096]{1,0:T(8,128)(2,1)}, bf16[32,4096]{1,0:T(8,128)(2,1)S(1)}, u32[]{:S(2)}, u32[]{:S(2)}) collective-permute-start(bf16[32,4096]{1,0:T(8,128)(2,1)} %bitcast.1), channel_id=1, source_target_pairs={{0,12},{1,13},{2,14},{3,15},{4,8},{5,9},{6,10},{7,11},{8,4},{9,5},... | collective-permute-start | bytes 786440 | tf_op jit(solution)/shard_map/ppermute | solution.py:251
  5.1 12.3 %collective-permute-start.5 = (bf16[32,4096]{1,0:T(8,128)(2,1)}, bf16[32,4096]{1,0:T(8,128)(2,1)S(1)}, u32[]{:S(2)}, u32[]{:S(2)}) collective-permute-start(bf16[32,4096]{1,0:T(8,128)(2,1)} %bitcast.2), channel_id=1, source_target_pairs={{0,4},{1,5},{2,6},{3,7},{4,0},{5,1},{6,2},{7,3},{8,12},{9,13},{10,... | collective-permute-start | bytes 786440 | tf_op jit(solution)/shard_map/ppermute | solution.py:251
  5.1 12.3 %collective-permute-start.13 = (bf16[32,4096]{1,0:T(8,128)(2,1)}, bf16[32,4096]{1,0:T(8,128)(2,1)S(1)}, u32[]{:S(2)}, u32[]{:S(2)}) collective-permute-start(bf16[32,4096]{1,0:T(8,128)(2,1)} %bitcast.3), channel_id=1, source_target_pairs={{0,16},{1,17},{2,18},{3,19},{4,20},{5,21},{6,22},{7,23},{8,24},{9,... | collective-permute-start | bytes 786440 | tf_op jit(solution)/shard_map/ppermute | solution.py:251
  6.6 10.8 %collective-permute-start.4 = (bf16[32,4096]{1,0:T(8,128)(2,1)}, bf16[32,4096]{1,0:T(8,128)(2,1)S(1)}, u32[]{:S(2)}, u32[]{:S(2)}) collective-permute-start(bf16[32,4096]{1,0:T(8,128)(2,1)} %bitcast.4), channel_id=1, source_target_pairs={{0,2},{1,3},{2,0},{3,1},{4,6},{5,7},{6,4},{7,5},{8,10},{9,11},{10,... | collective-permute-start | bytes 786440 | tf_op jit(solution)/shard_map/ppermute | solution.py:251
  8.1 11.8 %collective-permute-start.9 = (bf16[32,4096]{1,0:T(8,128)(2,1)}, bf16[32,4096]{1,0:T(8,128)(2,1)S(1)}, u32[]{:S(2)}, u32[]{:S(2)}) collective-permute-start(bf16[32,4096]{1,0:T(8,128)(2,1)} %bitcast.5), channel_id=1, source_target_pairs={{0,18},{1,19},{2,16},{3,17},{4,22},{5,23},{6,20},{7,21},{8,26},{9,... | collective-permute-start | bytes 786440 | tf_op jit(solution)/shard_map/ppermute | solution.py:251
  12.5 11.2 %collective-permute-start.1 = (bf16[32,4096]{1,0:T(8,128)(2,1)S(1)}, bf16[32,4096]{1,0:T(8,128)(2,1)S(1)}, u32[]{:S(2)}, u32[]{:S(2)}) collective-permute-start(bf16[32,4096]{1,0:T(8,128)(2,1)S(1)} %collective-permute-done.refs_3_), channel_id=1, source_target_pairs={{0,4},{1,5},{2,6},{3,7},{4,0},{5,1},{6,2},{7,3},{8,12},{9,13},{10,... | collective-permute-start | bytes 786440 | tf_op jit(solution)/shard_map/ppermute | solution.py:251
  17.4 9.2 %collective-permute-start.14 = (bf16[32,4096]{1,0:T(8,128)(2,1)S(1)}, bf16[32,4096]{1,0:T(8,128)(2,1)S(1)}, u32[]{:S(2)}, u32[]{:S(2)}) collective-permute-start(bf16[32,4096]{1,0:T(8,128)(2,1)S(1)} %collective-permute-done.5.refs_3_), channel_id=1, source_target_pairs={{0,16},{1,17},{2,18},{3,19},{4,20},{5,21},{6,22},{7,23},{8,24},{9,... | collective-permute-start | bytes 786440 | tf_op jit(solution)/shard_map/ppermute | solution.py:251
  19.8 10.4 %collective-permute-start.10 = (bf16[32,4096]{1,0:T(8,128)(2,1)S(1)}, bf16[32,4096]{1,0:T(8,128)(2,1)S(1)}, u32[]{:S(2)}, u32[]{:S(2)}) collective-permute-start(bf16[32,4096]{1,0:T(8,128)(2,1)S(1)} %collective-permute-done.9.refs_2_), channel_id=1, source_target_pairs={{0,12},{1,13},{2,14},{3,15},{4,8},{5,9},{6,10},{7,11},{8,4},{9,5},... | collective-permute-start | bytes 786440 | tf_op jit(solution)/shard_map/ppermute | solution.py:251
  21.0 12.5 %collective-permute-start.3 = (bf16[32,4096]{1,0:T(8,128)(2,1)S(1)}, bf16[32,4096]{1,0:T(8,128)(2,1)S(1)}, u32[]{:S(2)}, u32[]{:S(2)}) collective-permute-start(bf16[32,4096]{1,0:T(8,128)(2,1)S(1)} %collective-permute-done.refs_3_), channel_id=1, source_target_pairs={{0,2},{1,3},{2,0},{3,1},{4,6},{5,7},{6,4},{7,5},{8,10},{9,11},{10,... | collective-permute-start | bytes 786440 | tf_op jit(solution)/shard_map/ppermute | solution.py:251
  23.7 11.3 %collective-permute-start.8 = (bf16[32,4096]{1,0:T(8,128)(2,1)S(1)}, bf16[32,4096]{1,0:T(8,128)(2,1)S(1)}, u32[]{:S(2)}, u32[]{:S(2)}) collective-permute-start(bf16[32,4096]{1,0:T(8,128)(2,1)S(1)} %collective-permute-done.1.refs_1_), channel_id=1, source_target_pairs={{0,16},{1,17},{2,18},{3,19},{4,20},{5,21},{6,22},{7,23},{8,24},{9,... | collective-permute-start | bytes 786440 | tf_op jit(solution)/shard_map/ppermute | solution.py:251
  26.6 8.4 %collective-permute-start.15 = (bf16[32,4096]{1,0:T(8,128)(2,1)S(1)}, bf16[32,4096]{1,0:T(8,128)(2,1)S(1)}, u32[]{:S(2)}, u32[]{:S(2)}) collective-permute-start(bf16[32,4096]{1,0:T(8,128)(2,1)S(1)} %collective-permute-done.14.refs_3_), channel_id=1, source_target_pairs={{0,2},{1,3},{2,0},{3,1},{4,6},{5,7},{6,4},{7,5},{8,10},{9,11},{10,... | collective-permute-start | bytes 786440 | tf_op jit(solution)/shard_map/ppermute | solution.py:251
  28.1 8.8 %collective-permute-start.12 = (bf16[32,4096]{1,0:T(8,128)(2,1)S(1)}, bf16[32,4096]{1,0:T(8,128)(2,1)S(1)}, u32[]{:S(2)}, u32[]{:S(2)}) collective-permute-start(bf16[32,4096]{1,0:T(8,128)(2,1)S(1)} %collective-permute-done.refs_3_), channel_id=1, source_target_pairs={{0,16},{1,17},{2,18},{3,19},{4,20},{5,21},{6,22},{7,23},{8,24},{9,... | collective-permute-start | bytes 786440 | tf_op jit(solution)/shard_map/ppermute | solution.py:251
  30.2 7.6 %collective-permute-start.11 = (bf16[32,4096]{1,0:T(8,128)(2,1)S(1)}, bf16[32,4096]{1,0:T(8,128)(2,1)S(1)}, u32[]{:S(2)}, u32[]{:S(2)}) collective-permute-start(bf16[32,4096]{1,0:T(8,128)(2,1)S(1)} %collective-permute-done.10.refs_4_), channel_id=1, source_target_pairs={{0,4},{1,5},{2,6},{3,7},{4,0},{5,1},{6,2},{7,3},{8,12},{9,13},{10,... | collective-permute-start | bytes 786440 | tf_op jit(solution)/shard_map/ppermute | solution.py:251
  33.5 6.4 %collective-permute-start.6 = (bf16[32,4096]{1,0:T(8,128)(2,1)S(1)}, bf16[32,4096]{1,0:T(8,128)(2,1)S(1)}, u32[]{:S(2)}, u32[]{:S(2)}) collective-permute-start(bf16[32,4096]{1,0:T(8,128)(2,1)S(1)} %collective-permute-done.5.refs_3_), channel_id=1, source_target_pairs={{0,2},{1,3},{2,0},{3,1},{4,6},{5,7},{6,4},{7,5},{8,10},{9,11},{10,... | collective-permute-start | bytes 786440 | tf_op jit(solution)/shard_map/ppermute | solution.py:251
  36.8 7.6 %copy-start = (bf16[1,32,4096]{2,1,0:T(8,128)(2,1)S(1)}, bf16[1,32,4096]{2,1,0:T(8,128)(2,1)}, u32[]{:S(2)}) copy-start(bf16[1,32,4096]{2,1,0:T(8,128)(2,1)} %param.4) | copy-start | bytes 786436
  39.9 1.9 %collective-permute-start.16 = (f32[128,1024]{1,0:T(8,128)S(1)}, f32[128,1024]{1,0:T(8,128)S(1)}, u32[]{:S(2)}, u32[]{:S(2)}) collective-permute-start(f32[128,1024]{1,0:T(8,128)S(1)} %get-tuple-element.22), channel_id=1, source_target_pairs={{0,1},{1,0},{2,3},{3,2},{4,5},{5,4},{6,7},{7,6},{8,9},{9,8},{10,11... | collective-permute-start | bytes 1572872 | tf_op jit(solution)/shard_map/ppermute | solution.py:251
  39.9 8.7 %collective-permute-start.2 = (bf16[32,4096]{1,0:T(8,128)(2,1)S(1)}, bf16[32,4096]{1,0:T(8,128)(2,1)S(1)}, u32[]{:S(2)}, u32[]{:S(2)}) collective-permute-start(bf16[32,4096]{1,0:T(8,128)(2,1)S(1)} %collective-permute-done.1.refs_1_), channel_id=1, source_target_pairs={{0,2},{1,3},{2,0},{3,1},{4,6},{5,7},{6,4},{7,5},{8,10},{9,11},{10,... | collective-permute-start | bytes 786440 | tf_op jit(solution)/shard_map/ppermute | solution.py:251
  42.8 8.5 %collective-permute-start.17 = (bf16[1040,128]{1,0:T(8,128)(2,1)S(1)}, bf16[1040,128]{1,0:T(8,128)(2,1)S(1)}, u32[]{:S(2)}, u32[]{:S(2)}) collective-permute-start(bf16[1040,128]{1,0:T(8,128)(2,1)S(1)} %shard_map.51), channel_id=1, source_target_pairs={{0,16},{1,17},{2,18},{3,19},{4,20},{5,21},{6,22},{7,23},{8,24},{9,... | collective-permute-start | bytes 798728 | tf_op jit(solution)/shard_map/ppermute | solution.py:251
  50.4 2.0 %collective-permute-start.7 = (f32[128,1024]{1,0:T(8,128)S(1)}, f32[128,1024]{1,0:T(8,128)S(1)}, u32[]{:S(2)}, u32[]{:S(2)}) collective-permute-start(f32[128,1024]{1,0:T(8,128)S(1)} %get-tuple-element.17), channel_id=1, source_target_pairs={{0,1},{1,0},{2,3},{3,2},{4,5},{5,4},{6,7},{7,6},{8,9},{9,8},{10,11... | collective-permute-start | bytes 1572872 | tf_op jit(solution)/shard_map/ppermute | solution.py:251

commit v7 on v6

--- a/solution.py
+++ b/solution.py
@@ -259,9 +259,9 @@
         y0 = swap(b0, src=1)
         x0 = swap(b0, x=1)
         d0 = swap(b0, src=1, x=1)
-        y1 = swap(after(z1, y0, x0, held[0]), src=1)
+        y1 = swap(after(z1, y0, x0), src=1)
         x1 = swap(z1, x=1)
-        z2 = swap(z3, z=1)
+        z2 = swap(after(z3, held[0]), z=1)
         d1 = swap(y1, x=1)
         y3 = swap(z3, src=1)
         x3 = swap(z3, x=1)

time: 53.4 us -> 53.4 us (level)
  no operation moved by 1% of the time
where the time goes in v7:
time: 53.4 us; the launch traced here: 53.2 us
  starting transfers between devices  29.6 us (55%)
  Pallas kernels  13.4 us (25%)
  waiting for transfers between devices  10.1 us (19%)
    ppermute x18, starting transfers between devices, swap(): return lax.ppermute(array, AXES, pairs)  29.6 us
    ppermute x18, waiting for transfers between devices, swap(): return lax.ppermute(array, AXES, pairs)  10.1 us
    pallas_call x4, Pallas kernels, products(): pl.pallas_call(kernel, out_shape=[jax.ShapeDtypeStruct((span, 2 * width),...  7.36 us
    pallas_call x1, Pallas kernels, resident(): pl.pallas_call(kernel, out_shape=[pltpu.VMEM(w.shape, w.dtype) for w in (...  3.48 us
  transfers between devices with their start and end apart: 18, of which 12 were waited for; matrix products, arithmetic and copies ran while one was open for 0% of the time, Pallas kernels for 24%

profile of v7, /device:TPU:0, one launch (start us, length us, event | category | flops | bytes accessed | tf_op | source)
XLA Modules:
  0.0 53.2 jit_solution(9903359963181923964)
XLA Ops:
  0.0 0.0 copy-start.1
  0.0 5.0 %collective-permute-start = (bf16[32,4096]{1,0:T(8,128)(2,1)}, bf16[32,4096]{1,0:T(8,128)(2,1)S(1)}, u32[]{:S(2)}, u32[]{:S(2)}) collective-permute-start(bf16[32,4096]{1,0:T(8,128)(2,1)} %bitcast.1), channel_id=1, source_target_pairs={{0,12},{1,13},{2,14},{3,15},{4,8},{5,9},{6,10},{7,11},{8,4},{9,5},... | collective-permute-start | bytes 786440 | tf_op jit(solution)/shard_map/ppermute | solution.py:251
  5.1 0.0 collective-permute-start.5
  5.1 1.5 %collective-permute-start.13 = (bf16[32,4096]{1,0:T(8,128)(2,1)}, bf16[32,4096]{1,0:T(8,128)(2,1)S(1)}, u32[]{:S(2)}, u32[]{:S(2)}) collective-permute-start(bf16[32,4096]{1,0:T(8,128)(2,1)} %bitcast.3), channel_id=1, source_target_pairs={{0,16},{1,17},{2,18},{3,19},{4,20},{5,21},{6,22},{7,23},{8,24},{9,... | collective-permute-start | bytes 786440 | tf_op jit(solution)/shard_map/ppermute | solution.py:251
  6.6 1.5 %collective-permute-start.4 = (bf16[32,4096]{1,0:T(8,128)(2,1)}, bf16[32,4096]{1,0:T(8,128)(2,1)S(1)}, u32[]{:S(2)}, u32[]{:S(2)}) collective-permute-start(bf16[32,4096]{1,0:T(8,128)(2,1)} %bitcast.4), channel_id=1, source_target_pairs={{0,2},{1,3},{2,0},{3,1},{4,6},{5,7},{6,4},{7,5},{8,10},{9,11},{10,... | collective-permute-start | bytes 786440 | tf_op jit(solution)/shard_map/ppermute | solution.py:251
  8.1 0.5 collective-permute-start.9
  8.5 3.5 %shard_map.46 = (bf16[1,4096,512]{2,1,0:T(8,128)(2,1)S(1)}, bf16[1,4096,512]{2,1,0:T(8,128)(2,1)S(1)}) custom-call(bf16[1,4096,512]{2,1,0:T(8,128)(2,1)} %gate.1, bf16[1,4096,512]{2,1,0:T(8,128)(2,1)} %up.1), custom_call_target="tpu_custom_call" | custom-call | flops 4194304 | bytes 16777216 | tf_op jit(solution)/shard_map/pallas_call | solution.py:120
  12.0 0.5 collective-permute-done.refs_3_
  12.5 4.4 %collective-permute-start.1 = (bf16[32,4096]{1,0:T(8,128)(2,1)S(1)}, bf16[32,4096]{1,0:T(8,128)(2,1)S(1)}, u32[]{:S(2)}, u32[]{:S(2)}) collective-permute-start(bf16[32,4096]{1,0:T(8,128)(2,1)S(1)} %collective-permute-done.refs_3_), channel_id=1, source_target_pairs={{0,4},{1,5},{2,6},{3,7},{4,0},{5,1},{6,2},{7,3},{8,12},{9,13},{10,... | collective-permute-start | bytes 786440 | tf_op jit(solution)/shard_map/ppermute | solution.py:251
  16.9 0.5 collective-permute-done.5.refs_3_
  17.4 0.0 collective-permute-done.13.refs_1_
  17.4 0.0 collective-permute-done.4.refs_2_
  17.4 1.5 %collective-permute-start.14 = (bf16[32,4096]{1,0:T(8,128)(2,1)S(1)}, bf16[32,4096]{1,0:T(8,128)(2,1)S(1)}, u32[]{:S(2)}, u32[]{:S(2)}) collective-permute-start(bf16[32,4096]{1,0:T(8,128)(2,1)S(1)} %collective-permute-done.5.refs_3_), channel_id=1, source_target_pairs={{0,16},{1,17},{2,18},{3,19},{4,20},{5,21},{6,22},{7,23},{8,24},{9,... | collective-permute-start | bytes 786440 | tf_op jit(solution)/shard_map/ppermute | solution.py:251
  18.9 0.9 %collective-permute-done.9.refs_2_ = bf16[32,4096]{1,0:T(8,128)(2,1)S(1)} collective-permute-done((bf16[32,4096]{1,0:T(8,128)(2,1)}, bf16[32,4096]{1,0:T(8,128)(2,1)S(1)}, u32[]{:S(2)}, u32[]{:S(2)}) %collective-permute-start.9) | collective-permute-done | bytes 262176 | tf_op jit(solution)/shard_map/ppermute | solution.py:251
  19.8 1.1 %collective-permute-start.10 = (bf16[32,4096]{1,0:T(8,128)(2,1)S(1)}, bf16[32,4096]{1,0:T(8,128)(2,1)S(1)}, u32[]{:S(2)}, u32[]{:S(2)}) collective-permute-start(bf16[32,4096]{1,0:T(8,128)(2,1)S(1)} %collective-permute-done.9.refs_2_), channel_id=1, source_target_pairs={{0,12},{1,13},{2,14},{3,15},{4,8},{5,9},{6,10},{7,11},{8,4},{9,5},... | collective-permute-start | bytes 786440 | tf_op jit(solution)/shard_map/ppermute | solution.py:251
  21.0 1.5 %collective-permute-start.3 = (bf16[32,4096]{1,0:T(8,128)(2,1)S(1)}, bf16[32,4096]{1,0:T(8,128)(2,1)S(1)}, u32[]{:S(2)}, u32[]{:S(2)}) collective-permute-start(bf16[32,4096]{1,0:T(8,128)(2,1)S(1)} %collective-permute-done.refs_3_), channel_id=1, source_target_pairs={{0,2},{1,3},{2,0},{3,1},{4,6},{5,7},{6,4},{7,5},{8,10},{9,11},{10,... | collective-permute-start | bytes 786440 | tf_op jit(solution)/shard_map/ppermute | solution.py:251
  22.5 1.2 %collective-permute-done.1.refs_1_ = bf16[32,4096]{1,0:T(8,128)(2,1)S(1)} collective-permute-done((bf16[32,4096]{1,0:T(8,128)(2,1)S(1)}, bf16[32,4096]{1,0:T(8,128)(2,1)S(1)}, u32[]{:S(2)}, u32[]{:S(2)}) %collective-permute-start.1) | collective-permute-done | bytes 262176 | tf_op jit(solution)/shard_map/ppermute | solution.py:251
  23.7 1.5 %collective-permute-start.8 = (bf16[32,4096]{1,0:T(8,128)(2,1)S(1)}, bf16[32,4096]{1,0:T(8,128)(2,1)S(1)}, u32[]{:S(2)}, u32[]{:S(2)}) collective-permute-start(bf16[32,4096]{1,0:T(8,128)(2,1)S(1)} %collective-permute-done.1.refs_1_), channel_id=1, source_target_pairs={{0,16},{1,17},{2,18},{3,19},{4,20},{5,21},{6,22},{7,23},{8,24},{9,... | collective-permute-start | bytes 786440 | tf_op jit(solution)/shard_map/ppermute | solution.py:251
  25.2 1.4 %collective-permute-done.14.refs_3_ = bf16[32,4096]{1,0:T(8,128)(2,1)S(1)} collective-permute-done((bf16[32,4096]{1,0:T(8,128)(2,1)S(1)}, bf16[32,4096]{1,0:T(8,128)(2,1)S(1)}, u32[]{:S(2)}, u32[]{:S(2)}) %collective-permute-start.14) | collective-permute-done | bytes 262176 | tf_op jit(solution)/shard_map/ppermute | solution.py:251
  26.6 1.5 %collective-permute-start.15 = (bf16[32,4096]{1,0:T(8,128)(2,1)S(1)}, bf16[32,4096]{1,0:T(8,128)(2,1)S(1)}, u32[]{:S(2)}, u32[]{:S(2)}) collective-permute-start(bf16[32,4096]{1,0:T(8,128)(2,1)S(1)} %collective-permute-done.14.refs_3_), channel_id=1, source_target_pairs={{0,2},{1,3},{2,0},{3,1},{4,6},{5,7},{6,4},{7,5},{8,10},{9,11},{10,... | collective-permute-start | bytes 786440 | tf_op jit(solution)/shard_map/ppermute | solution.py:251
  28.1 1.5 %collective-permute-start.12 = (bf16[32,4096]{1,0:T(8,128)(2,1)S(1)}, bf16[32,4096]{1,0:T(8,128)(2,1)S(1)}, u32[]{:S(2)}, u32[]{:S(2)}) collective-permute-start(bf16[32,4096]{1,0:T(8,128)(2,1)S(1)} %collective-permute-done.refs_3_), channel_id=1, source_target_pairs={{0,16},{1,17},{2,18},{3,19},{4,20},{5,21},{6,22},{7,23},{8,24},{9,... | collective-permute-start | bytes 786440 | tf_op jit(solution)/shard_map/ppermute | solution.py:251
  29.6 0.7 %collective-permute-done.10.refs_4_ = bf16[32,4096]{1,0:T(8,128)(2,1)S(1)} collective-permute-done((bf16[32,4096]{1,0:T(8,128)(2,1)S(1)}, bf16[32,4096]{1,0:T(8,128)(2,1)S(1)}, u32[]{:S(2)}, u32[]{:S(2)}) %collective-permute-start.10) | collective-permute-done | bytes 262176 | tf_op jit(solution)/shard_map/ppermute | solution.py:251
  30.2 3.2 %collective-permute-start.11 = (bf16[32,4096]{1,0:T(8,128)(2,1)S(1)}, bf16[32,4096]{1,0:T(8,128)(2,1)S(1)}, u32[]{:S(2)}, u32[]{:S(2)}) collective-permute-start(bf16[32,4096]{1,0:T(8,128)(2,1)S(1)} %collective-permute-done.10.refs_4_), channel_id=1, source_target_pairs={{0,4},{1,5},{2,6},{3,7},{4,0},{5,1},{6,2},{7,3},{8,12},{9,13},{10,... | collective-permute-start | bytes 786440 | tf_op jit(solution)/shard_map/ppermute | solution.py:251
  33.5 0.0 collective-permute-done.3.refs_4_
  33.5 1.5 %collective-permute-start.6 = (bf16[32,4096]{1,0:T(8,128)(2,1)S(1)}, bf16[32,4096]{1,0:T(8,128)(2,1)S(1)}, u32[]{:S(2)}, u32[]{:S(2)}) collective-permute-start(bf16[32,4096]{1,0:T(8,128)(2,1)S(1)} %collective-permute-done.5.refs_3_), channel_id=1, source_target_pairs={{0,2},{1,3},{2,0},{3,1},{4,6},{5,7},{6,4},{7,5},{8,10},{9,11},{10,... | collective-permute-start | bytes 786440 | tf_op jit(solution)/shard_map/ppermute | solution.py:251
  35.0 0.0 collective-permute-done.8.refs_1_
  35.0 0.0 collective-permute-done.15.refs_4_
  35.0 0.0 copy-done.1
  35.0 1.8 %shard_map.49.refs_7_ = f32[128,1024]{1,0:T(8,128)S(1)} custom-call(f32[2,2]{1,0:T(2,128)S(1)} %copy-done.1, bf16[32,4096]{1,0:T(8,128)(2,1)S(1)} %collective-permute-done.13.refs_1_, bf16[32,4096]{1,0:T(8,128)(2,1)S(1)} %collective-permute-done.9.refs_2_, bf16[32,4096]{1,0:T(8,128)(2,1)S(1)} %collective-permute-done.14.refs_3_, ...), custom_call_target="tpu_custom_call" | custom-call | flops 1073741824 | bytes 9437184 | tf_op jit(solution)/shard_map/pallas_call | solution.py:93
  36.8 0.0 copy-start
  36.8 0.0 collective-permute-done.12.refs_3_
  36.8 1.0 %collective-permute-done.11.refs_2_ = bf16[32,4096]{1,0:T(8,128)(2,1)S(1)} collective-permute-done((bf16[32,4096]{1,0:T(8,128)(2,1)S(1)}, bf16[32,4096]{1,0:T(8,128)(2,1)S(1)}, u32[]{:S(2)}, u32[]{:S(2)}) %collective-permute-start.11) | collective-permute-done | bytes 262176 | tf_op jit(solution)/shard_map/ppermute | solution.py:251
  37.8 1.9 %shard_map.50 = (f32[128,1024]{1,0:T(8,128)S(1)}, f32[128,1024]{1,0:T(8,128)S(1)}) custom-call(f32[2,2]{1,0:T(2,128)S(1)} %copy-done.1, bf16[32,4096]{1,0:T(8,128)(2,1)S(1)} %collective-permute-done.8.refs_1_, bf16[32,4096]{1,0:T(8,128)(2,1)S(1)} %collective-permute-done.11.refs_2_, bf16[32,4096]{1,0:T(8,128)(2,1)S(1)} %collective-permute-done.12.refs_3_, ...), custom_call_target="tpu_custom_call" | custom-call | flops 1073741824 | bytes 9437184 | tf_op jit(solution)/shard_map/pallas_call | solution.py:93
  39.7 0.1 collective-permute-done.6.refs_4_
  39.9 0.0 collective-permute-start.16
  39.9 1.5 %collective-permute-start.2 = (bf16[32,4096]{1,0:T(8,128)(2,1)S(1)}, bf16[32,4096]{1,0:T(8,128)(2,1)S(1)}, u32[]{:S(2)}, u32[]{:S(2)}) collective-permute-start(bf16[32,4096]{1,0:T(8,128)(2,1)S(1)} %collective-permute-done.1.refs_1_), channel_id=1, source_target_pairs={{0,2},{1,3},{2,0},{3,1},{4,6},{5,7},{6,4},{7,5},{8,10},{9,11},{10,... | collective-permute-start | bytes 786440 | tf_op jit(solution)/shard_map/ppermute | solution.py:251
  41.3 0.4 collective-permute-done.16.received_ref
  41.8 1.0 %shard_map.51 = bf16[1040,128]{1,0:T(8,128)(2,1)S(1)} custom-call(f32[128,1024]{1,0:T(8,128)S(1)} %get-tuple-element.22.kept_ref, f32[128,1024]{1,0:T(8,128)S(1)} %collective-permute-done.16.received_ref), custom_call_target="tpu_custom_call" | custom-call | tf_op jit(solution)/shard_map/pallas_call | solution.py:173
  42.8 1.7 %collective-permute-start.17 = (bf16[1040,128]{1,0:T(8,128)(2,1)S(1)}, bf16[1040,128]{1,0:T(8,128)(2,1)S(1)}, u32[]{:S(2)}, u32[]{:S(2)}) collective-permute-start(bf16[1040,128]{1,0:T(8,128)(2,1)S(1)} %shard_map.51), channel_id=1, source_target_pairs={{0,16},{1,17},{2,18},{3,19},{4,20},{5,21},{6,22},{7,23},{8,24},{9,... | collective-permute-start | bytes 798728 | tf_op jit(solution)/shard_map/ppermute | solution.py:251
  44.4 0.0 copy-done
  44.4 1.8 %shard_map.47.refs_7_ = f32[128,1024]{1,0:T(8,128)S(1)} custom-call(f32[2,2]{1,0:T(2,128)S(1)} %copy-done.1, bf16[32,4096]{1,0:T(8,128)(2,1)S(1)} %bitcast.6, bf16[32,4096]{1,0:T(8,128)(2,1)S(1)} %collective-permute-done.4.refs_2_, bf16[32,4096]{1,0:T(8,128)(2,1)S(1)} %collective-permute-done.5.refs_3_, bf16[32,4096]{1,0:T(8,128)(2,1)S(1)} %collective-permute-done.6.refs_4_, ...), custom_call_target="tpu_custom_call" | custom-call | flops 1073741824 | bytes 9437184 | tf_op jit(solution)/shard_map/pallas_call | solution.py:93
  46.3 2.3 %collective-permute-done.2.refs_2_ = bf16[32,4096]{1,0:T(8,128)(2,1)S(1)} collective-permute-done((bf16[32,4096]{1,0:T(8,128)(2,1)S(1)}, bf16[32,4096]{1,0:T(8,128)(2,1)S(1)}, u32[]{:S(2)}, u32[]{:S(2)}) %collective-permute-start.2) | collective-permute-done | bytes 262176 | tf_op jit(solution)/shard_map/ppermute | solution.py:251
  48.6 1.9 %shard_map.48 = (f32[128,1024]{1,0:T(8,128)S(1)}, f32[128,1024]{1,0:T(8,128)S(1)}) custom-call(f32[2,2]{1,0:T(2,128)S(1)} %copy-done.1, bf16[32,4096]{1,0:T(8,128)(2,1)S(1)} %collective-permute-done.1.refs_1_, bf16[32,4096]{1,0:T(8,128)(2,1)S(1)} %collective-permute-done.2.refs_2_, bf16[32,4096]{1,0:T(8,128)(2,1)S(1)} %collective-permute-done.refs_3_, ...), custom_call_target="tpu_custom_call" | custom-call | flops 1073741824 | bytes 9437184 | tf_op jit(solution)/shard_map/pallas_call | solution.py:93
  50.4 0.1 collective-permute-start.7
  50.5 0.7 %collective-permute-done.17.values_ref = bf16[1040,128]{1,0:T(8,128)(2,1)S(1)} collective-permute-done((bf16[1040,128]{1,0:T(8,128)(2,1)S(1)}, bf16[1040,128]{1,0:T(8,128)(2,1)S(1)}, u32[]{:S(2)}, u32[]{:S(2)}) %collective-permute-start.17) | collective-permute-done | bytes 266272 | tf_op jit(solution)/shard_map/ppermute | solution.py:251
  51.3 0.8 %shard_map.52.refs_2_ = f32[128,1024]{1,0:T(8,128)S(1)} custom-call(bf16[1040,128]{1,0:T(8,128)(2,1)S(1)} %collective-permute-done.17.values_ref), custom_call_target="tpu_custom_call" | custom-call | flops 11980800000 | bytes 266240 | tf_op jit(solution)/shard_map/pallas_call | solution.py:203
  52.1 0.3 collective-permute-done.7.refs_1_
  52.4 0.8 %shard_map.53 = bf16[1,128,512]{2,1,0:T(8,128)(2,1)} custom-call(f32[128,1024]{1,0:T(8,128)S(1)} %get-tuple-element.18.refs_0_, f32[128,1024]{1,0:T(8,128)S(1)} %collective-permute-done.7.refs_1_, f32[128,1024]{1,0:T(8,128)S(1)} %shard_map.52.refs_2_), custom_call_target="tpu_custom_call" | custom-call | tf_op jit(solution)/shard_map/pallas_call | solution.py:230
Async XLA Ops:
  0.0 35.0 %copy-start.1 = (f32[2,2]{1,0:T(2,128)S(1)}, f32[2,2]{1,0:T(2,128)}, u32[]{:S(2)}) copy-start(f32[2,2]{1,0:T(2,128)} %refs_0_.7) | copy-start | bytes 52
  0.0 12.5 %collective-permute-start = (bf16[32,4096]{1,0:T(8,128)(2,1)}, bf16[32,4096]{1,0:T(8,128)(2,1)S(1)}, u32[]{:S(2)}, u32[]{:S(2)}) collective-permute-start(bf16[32,4096]{1,0:T(8,128)(2,1)} %bitcast.1), channel_id=1, source_target_pairs={{0,12},{1,13},{2,14},{3,15},{4,8},{5,9},{6,10},{7,11},{8,4},{9,5},... | collective-permute-start | bytes 786440 | tf_op jit(solution)/shard_map/ppermute | solution.py:251
  5.1 12.3 %collective-permute-start.5 = (bf16[32,4096]{1,0:T(8,128)(2,1)}, bf16[32,4096]{1,0:T(8,128)(2,1)S(1)}, u32[]{:S(2)}, u32[]{:S(2)}) collective-permute-start(bf16[32,4096]{1,0:T(8,128)(2,1)} %bitcast.2), channel_id=1, source_target_pairs={{0,4},{1,5},{2,6},{3,7},{4,0},{5,1},{6,2},{7,3},{8,12},{9,13},{10,... | collective-permute-start | bytes 786440 | tf_op jit(solution)/shard_map/ppermute | solution.py:251
  5.1 12.3 %collective-permute-start.13 = (bf16[32,4096]{1,0:T(8,128)(2,1)}, bf16[32,4096]{1,0:T(8,128)(2,1)S(1)}, u32[]{:S(2)}, u32[]{:S(2)}) collective-permute-start(bf16[32,4096]{1,0:T(8,128)(2,1)} %bitcast.3), channel_id=1, source_target_pairs={{0,16},{1,17},{2,18},{3,19},{4,20},{5,21},{6,22},{7,23},{8,24},{9,... | collective-permute-start | bytes 786440 | tf_op jit(solution)/shard_map/ppermute | solution.py:251
  6.6 10.8 %collective-permute-start.4 = (bf16[32,4096]{1,0:T(8,128)(2,1)}, bf16[32,4096]{1,0:T(8,128)(2,1)S(1)}, u32[]{:S(2)}, u32[]{:S(2)}) collective-permute-start(bf16[32,4096]{1,0:T(8,128)(2,1)} %bitcast.4), channel_id=1, source_target_pairs={{0,2},{1,3},{2,0},{3,1},{4,6},{5,7},{6,4},{7,5},{8,10},{9,11},{10,... | collective-permute-start | bytes 786440 | tf_op jit(solution)/shard_map/ppermute | solution.py:251
  8.1 11.8 %collective-permute-start.9 = (bf16[32,4096]{1,0:T(8,128)(2,1)}, bf16[32,4096]{1,0:T(8,128)(2,1)S(1)}, u32[]{:S(2)}, u32[]{:S(2)}) collective-permute-start(bf16[32,4096]{1,0:T(8,128)(2,1)} %bitcast.5), channel_id=1, source_target_pairs={{0,18},{1,19},{2,16},{3,17},{4,22},{5,23},{6,20},{7,21},{8,26},{9,... | collective-permute-start | bytes 786440 | tf_op jit(solution)/shard_map/ppermute | solution.py:251
  12.5 11.2 %collective-permute-start.1 = (bf16[32,4096]{1,0:T(8,128)(2,1)S(1)}, bf16[32,4096]{1,0:T(8,128)(2,1)S(1)}, u32[]{:S(2)}, u32[]{:S(2)}) collective-permute-start(bf16[32,4096]{1,0:T(8,128)(2,1)S(1)} %collective-permute-done.refs_3_), channel_id=1, source_target_pairs={{0,4},{1,5},{2,6},{3,7},{4,0},{5,1},{6,2},{7,3},{8,12},{9,13},{10,... | collective-permute-start | bytes 786440 | tf_op jit(solution)/shard_map/ppermute | solution.py:251
  17.4 9.2 %collective-permute-start.14 = (bf16[32,4096]{1,0:T(8,128)(2,1)S(1)}, bf16[32,4096]{1,0:T(8,128)(2,1)S(1)}, u32[]{:S(2)}, u32[]{:S(2)}) collective-permute-start(bf16[32,4096]{1,0:T(8,128)(2,1)S(1)} %collective-permute-done.5.refs_3_), channel_id=1, source_target_pairs={{0,16},{1,17},{2,18},{3,19},{4,20},{5,21},{6,22},{7,23},{8,24},{9,... | collective-permute-start | bytes 786440 | tf_op jit(solution)/shard_map/ppermute | solution.py:251
  19.8 10.4 %collective-permute-start.10 = (bf16[32,4096]{1,0:T(8,128)(2,1)S(1)}, bf16[32,4096]{1,0:T(8,128)(2,1)S(1)}, u32[]{:S(2)}, u32[]{:S(2)}) collective-permute-start(bf16[32,4096]{1,0:T(8,128)(2,1)S(1)} %collective-permute-done.9.refs_2_), channel_id=1, source_target_pairs={{0,12},{1,13},{2,14},{3,15},{4,8},{5,9},{6,10},{7,11},{8,4},{9,5},... | collective-permute-start | bytes 786440 | tf_op jit(solution)/shard_map/ppermute | solution.py:251
  21.0 12.5 %collective-permute-start.3 = (bf16[32,4096]{1,0:T(8,128)(2,1)S(1)}, bf16[32,4096]{1,0:T(8,128)(2,1)S(1)}, u32[]{:S(2)}, u32[]{:S(2)}) collective-permute-start(bf16[32,4096]{1,0:T(8,128)(2,1)S(1)} %collective-permute-done.refs_3_), channel_id=1, source_target_pairs={{0,2},{1,3},{2,0},{3,1},{4,6},{5,7},{6,4},{7,5},{8,10},{9,11},{10,... | collective-permute-start | bytes 786440 | tf_op jit(solution)/shard_map/ppermute | solution.py:251
  23.7 11.3 %collective-permute-start.8 = (bf16[32,4096]{1,0:T(8,128)(2,1)S(1)}, bf16[32,4096]{1,0:T(8,128)(2,1)S(1)}, u32[]{:S(2)}, u32[]{:S(2)}) collective-permute-start(bf16[32,4096]{1,0:T(8,128)(2,1)S(1)} %collective-permute-done.1.refs_1_), channel_id=1, source_target_pairs={{0,16},{1,17},{2,18},{3,19},{4,20},{5,21},{6,22},{7,23},{8,24},{9,... | collective-permute-start | bytes 786440 | tf_op jit(solution)/shard_map/ppermute | solution.py:251
  26.6 8.4 %collective-permute-start.15 = (bf16[32,4096]{1,0:T(8,128)(2,1)S(1)}, bf16[32,4096]{1,0:T(8,128)(2,1)S(1)}, u32[]{:S(2)}, u32[]{:S(2)}) collective-permute-start(bf16[32,4096]{1,0:T(8,128)(2,1)S(1)} %collective-permute-done.14.refs_3_), channel_id=1, source_target_pairs={{0,2},{1,3},{2,0},{3,1},{4,6},{5,7},{6,4},{7,5},{8,10},{9,11},{10,... | collective-permute-start | bytes 786440 | tf_op jit(solution)/shard_map/ppermute | solution.py:251
  28.1 8.8 %collective-permute-start.12 = (bf16[32,4096]{1,0:T(8,128)(2,1)S(1)}, bf16[32,4096]{1,0:T(8,128)(2,1)S(1)}, u32[]{:S(2)}, u32[]{:S(2)}) collective-permute-start(bf16[32,4096]{1,0:T(8,128)(2,1)S(1)} %collective-permute-done.refs_3_), channel_id=1, source_target_pairs={{0,16},{1,17},{2,18},{3,19},{4,20},{5,21},{6,22},{7,23},{8,24},{9,... | collective-permute-start | bytes 786440 | tf_op jit(solution)/shard_map/ppermute | solution.py:251
  30.2 7.6 %collective-permute-start.11 = (bf16[32,4096]{1,0:T(8,128)(2,1)S(1)}, bf16[32,4096]{1,0:T(8,128)(2,1)S(1)}, u32[]{:S(2)}, u32[]{:S(2)}) collective-permute-start(bf16[32,4096]{1,0:T(8,128)(2,1)S(1)} %collective-permute-done.10.refs_4_), channel_id=1, source_target_pairs={{0,4},{1,5},{2,6},{3,7},{4,0},{5,1},{6,2},{7,3},{8,12},{9,13},{10,... | collective-permute-start | bytes 786440 | tf_op jit(solution)/shard_map/ppermute | solution.py:251
  33.5 6.4 %collective-permute-start.6 = (bf16[32,4096]{1,0:T(8,128)(2,1)S(1)}, bf16[32,4096]{1,0:T(8,128)(2,1)S(1)}, u32[]{:S(2)}, u32[]{:S(2)}) collective-permute-start(bf16[32,4096]{1,0:T(8,128)(2,1)S(1)} %collective-permute-done.5.refs_3_), channel_id=1, source_target_pairs={{0,2},{1,3},{2,0},{3,1},{4,6},{5,7},{6,4},{7,5},{8,10},{9,11},{10,... | collective-permute-start | bytes 786440 | tf_op jit(solution)/shard_map/ppermute | solution.py:251
  36.8 7.6 %copy-start = (bf16[1,32,4096]{2,1,0:T(8,128)(2,1)S(1)}, bf16[1,32,4096]{2,1,0:T(8,128)(2,1)}, u32[]{:S(2)}) copy-start(bf16[1,32,4096]{2,1,0:T(8,128)(2,1)} %param.4) | copy-start | bytes 786436
  39.9 1.9 %collective-permute-start.16 = (f32[128,1024]{1,0:T(8,128)S(1)}, f32[128,1024]{1,0:T(8,128)S(1)}, u32[]{:S(2)}, u32[]{:S(2)}) collective-permute-start(f32[128,1024]{1,0:T(8,128)S(1)} %get-tuple-element.24), channel_id=1, source_target_pairs={{0,1},{1,0},{2,3},{3,2},{4,5},{5,4},{6,7},{7,6},{8,9},{9,8},{10,11... | collective-permute-start | bytes 1572872 | tf_op jit(solution)/shard_map/ppermute | solution.py:251
  39.9 8.7 %collective-permute-start.2 = (bf16[32,4096]{1,0:T(8,128)(2,1)S(1)}, bf16[32,4096]{1,0:T(8,128)(2,1)S(1)}, u32[]{:S(2)}, u32[]{:S(2)}) collective-permute-start(bf16[32,4096]{1,0:T(8,128)(2,1)S(1)} %collective-permute-done.1.refs_1_), channel_id=1, source_target_pairs={{0,2},{1,3},{2,0},{3,1},{4,6},{5,7},{6,4},{7,5},{8,10},{9,11},{10,... | collective-permute-start | bytes 786440 | tf_op jit(solution)/shard_map/ppermute | solution.py:251
  42.8 8.5 %collective-permute-start.17 = (bf16[1040,128]{1,0:T(8,128)(2,1)S(1)}, bf16[1040,128]{1,0:T(8,128)(2,1)S(1)}, u32[]{:S(2)}, u32[]{:S(2)}) collective-permute-start(bf16[1040,128]{1,0:T(8,128)(2,1)S(1)} %shard_map.51), channel_id=1, source_target_pairs={{0,16},{1,17},{2,18},{3,19},{4,20},{5,21},{6,22},{7,23},{8,24},{9,... | collective-permute-start | bytes 798728 | tf_op jit(solution)/shard_map/ppermute | solution.py:251
  50.4 2.0 %collective-permute-start.7 = (f32[128,1024]{1,0:T(8,128)S(1)}, f32[128,1024]{1,0:T(8,128)S(1)}, u32[]{:S(2)}, u32[]{:S(2)}) collective-permute-start(f32[128,1024]{1,0:T(8,128)S(1)} %get-tuple-element.19), channel_id=1, source_target_pairs={{0,1},{1,0},{2,3},{3,2},{4,5},{5,4},{6,7},{7,6},{8,9},{9,8},{10,11... | collective-permute-start | bytes 1572872 | tf_op jit(solution)/shard_map/ppermute | solution.py:251

commit v8 on v6

--- a/solution.py
+++ b/solution.py
@@ -106,11 +106,17 @@
 
 
 def resident(gate_weights, up_weights, work):
+    parts = 4
+    step = gate_weights.shape[1] // parts
+
     def kernel(gate, up, gate_out, up_out, sems):
-        copies = [
-            pltpu.make_async_copy(gate, gate_out, sems.at[0]),
-            pltpu.make_async_copy(up, up_out, sems.at[1]),
-        ]
+        copies = []
+        for i, (source, target) in enumerate(((gate, gate_out), (up, up_out))):
+            for n in range(parts):
+                at = pl.ds(n * step, step)
+                copies.append(
+                    pltpu.make_async_copy(source.at[0, at, :], target.at[0, at, :], sems.at[i, n])
+                )
         for copy in copies:
             copy.start()
         for copy in copies:
@@ -122,7 +128,7 @@
         out_shape=[pltpu.VMEM(w.shape, w.dtype) for w in (gate_weights, up_weights)],
         in_specs=[pl.BlockSpec(memory_space=pltpu.HBM)] * 2,
         out_specs=[pl.BlockSpec(memory_space=pltpu.VMEM)] * 2,
-        scratch_shapes=[pltpu.SemaphoreType.DMA((2,))],
+        scratch_shapes=[pltpu.SemaphoreType.DMA((2, parts))],
         compiler_params=pltpu.CompilerParams(vmem_limit_bytes=48 * 2**20),
         cost_estimate=pl.CostEstimate(
             flops=work * size, bytes_accessed=4 * size, transcendentals=0

time: 53.4 us -> 53.4 us (level)
  no operation moved by 1% of the time
where the time goes in v8:
time: 53.4 us; the launch traced here: 53.2 us
  starting transfers between devices  29.6 us (55%)
  Pallas kernels  13.4 us (25%)
  waiting for transfers between devices  10.1 us (19%)
    ppermute x18, starting transfers between devices, swap(): return lax.ppermute(array, AXES, pairs)  29.6 us
    ppermute x18, waiting for transfers between devices, swap(): return lax.ppermute(array, AXES, pairs)  10.1 us
    pallas_call x4, Pallas kernels, products(): pl.pallas_call(kernel, out_shape=[jax.ShapeDtypeStruct((span, 2 * width),...  7.36 us
    pallas_call x1, Pallas kernels, resident(): pl.pallas_call(kernel, out_shape=[pltpu.VMEM(w.shape, w.dtype) for w in (...  3.47 us
  transfers between devices with their start and end apart: 18, of which 12 were waited for; matrix products, arithmetic and copies ran while one was open for 0% of the time, Pallas kernels for 24%

profile of v8, /device:TPU:0, one launch (start us, length us, event | category | flops | bytes accessed | tf_op | source)
XLA Modules:
  0.0 53.2 jit_solution(7951391984827095893)
XLA Ops:
  0.0 0.0 copy-start.1
  0.0 5.0 %collective-permute-start = (bf16[32,4096]{1,0:T(8,128)(2,1)}, bf16[32,4096]{1,0:T(8,128)(2,1)S(1)}, u32[]{:S(2)}, u32[]{:S(2)}) collective-permute-start(bf16[32,4096]{1,0:T(8,128)(2,1)} %bitcast.1), channel_id=1, source_target_pairs={{0,12},{1,13},{2,14},{3,15},{4,8},{5,9},{6,10},{7,11},{8,4},{9,5},... | collective-permute-start | bytes 786440 | tf_op jit(solution)/shard_map/ppermute | solution.py:257
  5.1 0.0 collective-permute-start.5
  5.1 1.5 %collective-permute-start.13 = (bf16[32,4096]{1,0:T(8,128)(2,1)}, bf16[32,4096]{1,0:T(8,128)(2,1)S(1)}, u32[]{:S(2)}, u32[]{:S(2)}) collective-permute-start(bf16[32,4096]{1,0:T(8,128)(2,1)} %bitcast.3), channel_id=1, source_target_pairs={{0,16},{1,17},{2,18},{3,19},{4,20},{5,21},{6,22},{7,23},{8,24},{9,... | collective-permute-start | bytes 786440 | tf_op jit(solution)/shard_map/ppermute | solution.py:257
  6.6 1.5 %collective-permute-start.4 = (bf16[32,4096]{1,0:T(8,128)(2,1)}, bf16[32,4096]{1,0:T(8,128)(2,1)S(1)}, u32[]{:S(2)}, u32[]{:S(2)}) collective-permute-start(bf16[32,4096]{1,0:T(8,128)(2,1)} %bitcast.4), channel_id=1, source_target_pairs={{0,2},{1,3},{2,0},{3,1},{4,6},{5,7},{6,4},{7,5},{8,10},{9,11},{10,... | collective-permute-start | bytes 786440 | tf_op jit(solution)/shard_map/ppermute | solution.py:257
  8.1 0.5 collective-permute-start.9
  8.5 3.5 %shard_map.46 = (bf16[1,4096,512]{2,1,0:T(8,128)(2,1)S(1)}, bf16[1,4096,512]{2,1,0:T(8,128)(2,1)S(1)}) custom-call(bf16[1,4096,512]{2,1,0:T(8,128)(2,1)} %gate.1, bf16[1,4096,512]{2,1,0:T(8,128)(2,1)} %up.1), custom_call_target="tpu_custom_call" | custom-call | flops 4194304 | bytes 16777216 | tf_op jit(solution)/shard_map/pallas_call | solution.py:126
  12.0 0.5 collective-permute-done.refs_3_
  12.5 4.4 %collective-permute-start.1 = (bf16[32,4096]{1,0:T(8,128)(2,1)S(1)}, bf16[32,4096]{1,0:T(8,128)(2,1)S(1)}, u32[]{:S(2)}, u32[]{:S(2)}) collective-permute-start(bf16[32,4096]{1,0:T(8,128)(2,1)S(1)} %collective-permute-done.refs_3_), channel_id=1, source_target_pairs={{0,4},{1,5},{2,6},{3,7},{4,0},{5,1},{6,2},{7,3},{8,12},{9,13},{10,... | collective-permute-start | bytes 786440 | tf_op jit(solution)/shard_map/ppermute | solution.py:257
  16.9 0.5 collective-permute-done.5.refs_3_
  17.4 0.0 collective-permute-done.13.refs_1_
  17.4 0.0 collective-permute-done.4.refs_2_
  17.4 1.5 %collective-permute-start.14 = (bf16[32,4096]{1,0:T(8,128)(2,1)S(1)}, bf16[32,4096]{1,0:T(8,128)(2,1)S(1)}, u32[]{:S(2)}, u32[]{:S(2)}) collective-permute-start(bf16[32,4096]{1,0:T(8,128)(2,1)S(1)} %collective-permute-done.5.refs_3_), channel_id=1, source_target_pairs={{0,16},{1,17},{2,18},{3,19},{4,20},{5,21},{6,22},{7,23},{8,24},{9,... | collective-permute-start | bytes 786440 | tf_op jit(solution)/shard_map/ppermute | solution.py:257
  18.9 0.9 %collective-permute-done.9.refs_2_ = bf16[32,4096]{1,0:T(8,128)(2,1)S(1)} collective-permute-done((bf16[32,4096]{1,0:T(8,128)(2,1)}, bf16[32,4096]{1,0:T(8,128)(2,1)S(1)}, u32[]{:S(2)}, u32[]{:S(2)}) %collective-permute-start.9) | collective-permute-done | bytes 262176 | tf_op jit(solution)/shard_map/ppermute | solution.py:257
  19.8 1.1 %collective-permute-start.10 = (bf16[32,4096]{1,0:T(8,128)(2,1)S(1)}, bf16[32,4096]{1,0:T(8,128)(2,1)S(1)}, u32[]{:S(2)}, u32[]{:S(2)}) collective-permute-start(bf16[32,4096]{1,0:T(8,128)(2,1)S(1)} %collective-permute-done.9.refs_2_), channel_id=1, source_target_pairs={{0,12},{1,13},{2,14},{3,15},{4,8},{5,9},{6,10},{7,11},{8,4},{9,5},... | collective-permute-start | bytes 786440 | tf_op jit(solution)/shard_map/ppermute | solution.py:257
  21.0 1.5 %collective-permute-start.3 = (bf16[32,4096]{1,0:T(8,128)(2,1)S(1)}, bf16[32,4096]{1,0:T(8,128)(2,1)S(1)}, u32[]{:S(2)}, u32[]{:S(2)}) collective-permute-start(bf16[32,4096]{1,0:T(8,128)(2,1)S(1)} %collective-permute-done.refs_3_), channel_id=1, source_target_pairs={{0,2},{1,3},{2,0},{3,1},{4,6},{5,7},{6,4},{7,5},{8,10},{9,11},{10,... | collective-permute-start | bytes 786440 | tf_op jit(solution)/shard_map/ppermute | solution.py:257
  22.5 1.2 %collective-permute-done.1.refs_1_ = bf16[32,4096]{1,0:T(8,128)(2,1)S(1)} collective-permute-done((bf16[32,4096]{1,0:T(8,128)(2,1)S(1)}, bf16[32,4096]{1,0:T(8,128)(2,1)S(1)}, u32[]{:S(2)}, u32[]{:S(2)}) %collective-permute-start.1) | collective-permute-done | bytes 262176 | tf_op jit(solution)/shard_map/ppermute | solution.py:257
  23.7 1.5 %collective-permute-start.8 = (bf16[32,4096]{1,0:T(8,128)(2,1)S(1)}, bf16[32,4096]{1,0:T(8,128)(2,1)S(1)}, u32[]{:S(2)}, u32[]{:S(2)}) collective-permute-start(bf16[32,4096]{1,0:T(8,128)(2,1)S(1)} %collective-permute-done.1.refs_1_), channel_id=1, source_target_pairs={{0,16},{1,17},{2,18},{3,19},{4,20},{5,21},{6,22},{7,23},{8,24},{9,... | collective-permute-start | bytes 786440 | tf_op jit(solution)/shard_map/ppermute | solution.py:257
  25.2 1.4 %collective-permute-done.14.refs_3_ = bf16[32,4096]{1,0:T(8,128)(2,1)S(1)} collective-permute-done((bf16[32,4096]{1,0:T(8,128)(2,1)S(1)}, bf16[32,4096]{1,0:T(8,128)(2,1)S(1)}, u32[]{:S(2)}, u32[]{:S(2)}) %collective-permute-start.14) | collective-permute-done | bytes 262176 | tf_op jit(solution)/shard_map/ppermute | solution.py:257
  26.6 1.5 %collective-permute-start.15 = (bf16[32,4096]{1,0:T(8,128)(2,1)S(1)}, bf16[32,4096]{1,0:T(8,128)(2,1)S(1)}, u32[]{:S(2)}, u32[]{:S(2)}) collective-permute-start(bf16[32,4096]{1,0:T(8,128)(2,1)S(1)} %collective-permute-done.14.refs_3_), channel_id=1, source_target_pairs={{0,2},{1,3},{2,0},{3,1},{4,6},{5,7},{6,4},{7,5},{8,10},{9,11},{10,... | collective-permute-start | bytes 786440 | tf_op jit(solution)/shard_map/ppermute | solution.py:257
  28.1 1.5 %collective-permute-start.12 = (bf16[32,4096]{1,0:T(8,128)(2,1)S(1)}, bf16[32,4096]{1,0:T(8,128)(2,1)S(1)}, u32[]{:S(2)}, u32[]{:S(2)}) collective-permute-start(bf16[32,4096]{1,0:T(8,128)(2,1)S(1)} %collective-permute-done.refs_3_), channel_id=1, source_target_pairs={{0,16},{1,17},{2,18},{3,19},{4,20},{5,21},{6,22},{7,23},{8,24},{9,... | collective-permute-start | bytes 786440 | tf_op jit(solution)/shard_map/ppermute | solution.py:257
  29.6 0.7 %collective-permute-done.10.refs_4_ = bf16[32,4096]{1,0:T(8,128)(2,1)S(1)} collective-permute-done((bf16[32,4096]{1,0:T(8,128)(2,1)S(1)}, bf16[32,4096]{1,0:T(8,128)(2,1)S(1)}, u32[]{:S(2)}, u32[]{:S(2)}) %collective-permute-start.10) | collective-permute-done | bytes 262176 | tf_op jit(solution)/shard_map/ppermute | solution.py:257
  30.2 3.2 %collective-permute-start.11 = (bf16[32,4096]{1,0:T(8,128)(2,1)S(1)}, bf16[32,4096]{1,0:T(8,128)(2,1)S(1)}, u32[]{:S(2)}, u32[]{:S(2)}) collective-permute-start(bf16[32,4096]{1,0:T(8,128)(2,1)S(1)} %collective-permute-done.10.refs_4_), channel_id=1, source_target_pairs={{0,4},{1,5},{2,6},{3,7},{4,0},{5,1},{6,2},{7,3},{8,12},{9,13},{10,... | collective-permute-start | bytes 786440 | tf_op jit(solution)/shard_map/ppermute | solution.py:257
  33.5 0.0 collective-permute-done.3.refs_4_
  33.5 1.5 %collective-permute-start.6 = (bf16[32,4096]{1,0:T(8,128)(2,1)S(1)}, bf16[32,4096]{1,0:T(8,128)(2,1)S(1)}, u32[]{:S(2)}, u32[]{:S(2)}) collective-permute-start(bf16[32,4096]{1,0:T(8,128)(2,1)S(1)} %collective-permute-done.5.refs_3_), channel_id=1, source_target_pairs={{0,2},{1,3},{2,0},{3,1},{4,6},{5,7},{6,4},{7,5},{8,10},{9,11},{10,... | collective-permute-start | bytes 786440 | tf_op jit(solution)/shard_map/ppermute | solution.py:257
  35.0 0.0 collective-permute-done.8.refs_1_
  35.0 0.0 collective-permute-done.15.refs_4_
  35.0 0.0 copy-done.1
  35.0 1.8 %shard_map.49.refs_7_ = f32[128,1024]{1,0:T(8,128)S(1)} custom-call(f32[2,2]{1,0:T(2,128)S(1)} %copy-done.1, bf16[32,4096]{1,0:T(8,128)(2,1)S(1)} %collective-permute-done.13.refs_1_, bf16[32,4096]{1,0:T(8,128)(2,1)S(1)} %collective-permute-done.9.refs_2_, bf16[32,4096]{1,0:T(8,128)(2,1)S(1)} %collective-permute-done.14.refs_3_, ...), custom_call_target="tpu_custom_call" | custom-call | flops 1073741824 | bytes 9437184 | tf_op jit(solution)/shard_map/pallas_call | solution.py:93
  36.8 0.0 copy-start
  36.8 0.0 collective-permute-done.12.refs_3_
  36.8 1.0 %collective-permute-done.11.refs_2_ = bf16[32,4096]{1,0:T(8,128)(2,1)S(1)} collective-permute-done((bf16[32,4096]{1,0:T(8,128)(2,1)S(1)}, bf16[32,4096]{1,0:T(8,128)(2,1)S(1)}, u32[]{:S(2)}, u32[]{:S(2)}) %collective-permute-start.11) | collective-permute-done | bytes 262176 | tf_op jit(solution)/shard_map/ppermute | solution.py:257
  37.8 1.9 %shard_map.50 = (f32[128,1024]{1,0:T(8,128)S(1)}, f32[128,1024]{1,0:T(8,128)S(1)}) custom-call(f32[2,2]{1,0:T(2,128)S(1)} %copy-done.1, bf16[32,4096]{1,0:T(8,128)(2,1)S(1)} %collective-permute-done.8.refs_1_, bf16[32,4096]{1,0:T(8,128)(2,1)S(1)} %collective-permute-done.11.refs_2_, bf16[32,4096]{1,0:T(8,128)(2,1)S(1)} %collective-permute-done.12.refs_3_, ...), custom_call_target="tpu_custom_call" | custom-call | flops 1073741824 | bytes 9437184 | tf_op jit(solution)/shard_map/pallas_call | solution.py:93
  39.7 0.1 collective-permute-done.6.refs_4_
  39.9 0.0 collective-permute-start.16
  39.9 1.5 %collective-permute-start.2 = (bf16[32,4096]{1,0:T(8,128)(2,1)S(1)}, bf16[32,4096]{1,0:T(8,128)(2,1)S(1)}, u32[]{:S(2)}, u32[]{:S(2)}) collective-permute-start(bf16[32,4096]{1,0:T(8,128)(2,1)S(1)} %collective-permute-done.1.refs_1_), channel_id=1, source_target_pairs={{0,2},{1,3},{2,0},{3,1},{4,6},{5,7},{6,4},{7,5},{8,10},{9,11},{10,... | collective-permute-start | bytes 786440 | tf_op jit(solution)/shard_map/ppermute | solution.py:257
  41.3 0.4 collective-permute-done.16.received_ref
  41.8 1.0 %shard_map.51 = bf16[1040,128]{1,0:T(8,128)(2,1)S(1)} custom-call(f32[128,1024]{1,0:T(8,128)S(1)} %get-tuple-element.20.kept_ref, f32[128,1024]{1,0:T(8,128)S(1)} %collective-permute-done.16.received_ref), custom_call_target="tpu_custom_call" | custom-call | tf_op jit(solution)/shard_map/pallas_call | solution.py:179
  42.8 1.7 %collective-permute-start.17 = (bf16[1040,128]{1,0:T(8,128)(2,1)S(1)}, bf16[1040,128]{1,0:T(8,128)(2,1)S(1)}, u32[]{:S(2)}, u32[]{:S(2)}) collective-permute-start(bf16[1040,128]{1,0:T(8,128)(2,1)S(1)} %shard_map.51), channel_id=1, source_target_pairs={{0,16},{1,17},{2,18},{3,19},{4,20},{5,21},{6,22},{7,23},{8,24},{9,... | collective-permute-start | bytes 798728 | tf_op jit(solution)/shard_map/ppermute | solution.py:257
  44.4 0.0 copy-done
  44.4 1.8 %shard_map.47.refs_7_ = f32[128,1024]{1,0:T(8,128)S(1)} custom-call(f32[2,2]{1,0:T(2,128)S(1)} %copy-done.1, bf16[32,4096]{1,0:T(8,128)(2,1)S(1)} %bitcast.6, bf16[32,4096]{1,0:T(8,128)(2,1)S(1)} %collective-permute-done.4.refs_2_, bf16[32,4096]{1,0:T(8,128)(2,1)S(1)} %collective-permute-done.5.refs_3_, bf16[32,4096]{1,0:T(8,128)(2,1)S(1)} %collective-permute-done.6.refs_4_, ...), custom_call_target="tpu_custom_call" | custom-call | flops 1073741824 | bytes 9437184 | tf_op jit(solution)/shard_map/pallas_call | solution.py:93
  46.3 2.3 %collective-permute-done.2.refs_2_ = bf16[32,4096]{1,0:T(8,128)(2,1)S(1)} collective-permute-done((bf16[32,4096]{1,0:T(8,128)(2,1)S(1)}, bf16[32,4096]{1,0:T(8,128)(2,1)S(1)}, u32[]{:S(2)}, u32[]{:S(2)}) %collective-permute-start.2) | collective-permute-done | bytes 262176 | tf_op jit(solution)/shard_map/ppermute | solution.py:257
  48.6 1.9 %shard_map.48 = (f32[128,1024]{1,0:T(8,128)S(1)}, f32[128,1024]{1,0:T(8,128)S(1)}) custom-call(f32[2,2]{1,0:T(2,128)S(1)} %copy-done.1, bf16[32,4096]{1,0:T(8,128)(2,1)S(1)} %collective-permute-done.1.refs_1_, bf16[32,4096]{1,0:T(8,128)(2,1)S(1)} %collective-permute-done.2.refs_2_, bf16[32,4096]{1,0:T(8,128)(2,1)S(1)} %collective-permute-done.refs_3_, ...), custom_call_target="tpu_custom_call" | custom-call | flops 1073741824 | bytes 9437184 | tf_op jit(solution)/shard_map/pallas_call | solution.py:93
  50.4 0.1 collective-permute-start.7
  50.5 0.7 %collective-permute-done.17.values_ref = bf16[1040,128]{1,0:T(8,128)(2,1)S(1)} collective-permute-done((bf16[1040,128]{1,0:T(8,128)(2,1)S(1)}, bf16[1040,128]{1,0:T(8,128)(2,1)S(1)}, u32[]{:S(2)}, u32[]{:S(2)}) %collective-permute-start.17) | collective-permute-done | bytes 266272 | tf_op jit(solution)/shard_map/ppermute | solution.py:257
  51.3 0.8 %shard_map.52.refs_2_ = f32[128,1024]{1,0:T(8,128)S(1)} custom-call(bf16[1040,128]{1,0:T(8,128)(2,1)S(1)} %collective-permute-done.17.values_ref), custom_call_target="tpu_custom_call" | custom-call | flops 11980800000 | bytes 266240 | tf_op jit(solution)/shard_map/pallas_call | solution.py:209
  52.1 0.3 collective-permute-done.7.refs_1_
  52.4 0.8 %shard_map.53 = bf16[1,128,512]{2,1,0:T(8,128)(2,1)} custom-call(f32[128,1024]{1,0:T(8,128)S(1)} %get-tuple-element.16.refs_0_, f32[128,1024]{1,0:T(8,128)S(1)} %collective-permute-done.7.refs_1_, f32[128,1024]{1,0:T(8,128)S(1)} %shard_map.52.refs_2_), custom_call_target="tpu_custom_call" | custom-call | tf_op jit(solution)/shard_map/pallas_call | solution.py:236
Async XLA Ops:
  0.0 35.0 %copy-start.1 = (f32[2,2]{1,0:T(2,128)S(1)}, f32[2,2]{1,0:T(2,128)}, u32[]{:S(2)}) copy-start(f32[2,2]{1,0:T(2,128)} %refs_0_.7) | copy-start | bytes 52
  0.0 12.5 %collective-permute-start = (bf16[32,4096]{1,0:T(8,128)(2,1)}, bf16[32,4096]{1,0:T(8,128)(2,1)S(1)}, u32[]{:S(2)}, u32[]{:S(2)}) collective-permute-start(bf16[32,4096]{1,0:T(8,128)(2,1)} %bitcast.1), channel_id=1, source_target_pairs={{0,12},{1,13},{2,14},{3,15},{4,8},{5,9},{6,10},{7,11},{8,4},{9,5},... | collective-permute-start | bytes 786440 | tf_op jit(solution)/shard_map/ppermute | solution.py:257
  5.1 12.3 %collective-permute-start.5 = (bf16[32,4096]{1,0:T(8,128)(2,1)}, bf16[32,4096]{1,0:T(8,128)(2,1)S(1)}, u32[]{:S(2)}, u32[]{:S(2)}) collective-permute-start(bf16[32,4096]{1,0:T(8,128)(2,1)} %bitcast.2), channel_id=1, source_target_pairs={{0,4},{1,5},{2,6},{3,7},{4,0},{5,1},{6,2},{7,3},{8,12},{9,13},{10,... | collective-permute-start | bytes 786440 | tf_op jit(solution)/shard_map/ppermute | solution.py:257
  5.1 12.3 %collective-permute-start.13 = (bf16[32,4096]{1,0:T(8,128)(2,1)}, bf16[32,4096]{1,0:T(8,128)(2,1)S(1)}, u32[]{:S(2)}, u32[]{:S(2)}) collective-permute-start(bf16[32,4096]{1,0:T(8,128)(2,1)} %bitcast.3), channel_id=1, source_target_pairs={{0,16},{1,17},{2,18},{3,19},{4,20},{5,21},{6,22},{7,23},{8,24},{9,... | collective-permute-start | bytes 786440 | tf_op jit(solution)/shard_map/ppermute | solution.py:257
  6.6 10.8 %collective-permute-start.4 = (bf16[32,4096]{1,0:T(8,128)(2,1)}, bf16[32,4096]{1,0:T(8,128)(2,1)S(1)}, u32[]{:S(2)}, u32[]{:S(2)}) collective-permute-start(bf16[32,4096]{1,0:T(8,128)(2,1)} %bitcast.4), channel_id=1, source_target_pairs={{0,2},{1,3},{2,0},{3,1},{4,6},{5,7},{6,4},{7,5},{8,10},{9,11},{10,... | collective-permute-start | bytes 786440 | tf_op jit(solution)/shard_map/ppermute | solution.py:257
  8.1 11.8 %collective-permute-start.9 = (bf16[32,4096]{1,0:T(8,128)(2,1)}, bf16[32,4096]{1,0:T(8,128)(2,1)S(1)}, u32[]{:S(2)}, u32[]{:S(2)}) collective-permute-start(bf16[32,4096]{1,0:T(8,128)(2,1)} %bitcast.5), channel_id=1, source_target_pairs={{0,18},{1,19},{2,16},{3,17},{4,22},{5,23},{6,20},{7,21},{8,26},{9,... | collective-permute-start | bytes 786440 | tf_op jit(solution)/shard_map/ppermute | solution.py:257
  12.5 11.2 %collective-permute-start.1 = (bf16[32,4096]{1,0:T(8,128)(2,1)S(1)}, bf16[32,4096]{1,0:T(8,128)(2,1)S(1)}, u32[]{:S(2)}, u32[]{:S(2)}) collective-permute-start(bf16[32,4096]{1,0:T(8,128)(2,1)S(1)} %collective-permute-done.refs_3_), channel_id=1, source_target_pairs={{0,4},{1,5},{2,6},{3,7},{4,0},{5,1},{6,2},{7,3},{8,12},{9,13},{10,... | collective-permute-start | bytes 786440 | tf_op jit(solution)/shard_map/ppermute | solution.py:257
  17.4 9.2 %collective-permute-start.14 = (bf16[32,4096]{1,0:T(8,128)(2,1)S(1)}, bf16[32,4096]{1,0:T(8,128)(2,1)S(1)}, u32[]{:S(2)}, u32[]{:S(2)}) collective-permute-start(bf16[32,4096]{1,0:T(8,128)(2,1)S(1)} %collective-permute-done.5.refs_3_), channel_id=1, source_target_pairs={{0,16},{1,17},{2,18},{3,19},{4,20},{5,21},{6,22},{7,23},{8,24},{9,... | collective-permute-start | bytes 786440 | tf_op jit(solution)/shard_map/ppermute | solution.py:257
  19.8 10.4 %collective-permute-start.10 = (bf16[32,4096]{1,0:T(8,128)(2,1)S(1)}, bf16[32,4096]{1,0:T(8,128)(2,1)S(1)}, u32[]{:S(2)}, u32[]{:S(2)}) collective-permute-start(bf16[32,4096]{1,0:T(8,128)(2,1)S(1)} %collective-permute-done.9.refs_2_), channel_id=1, source_target_pairs={{0,12},{1,13},{2,14},{3,15},{4,8},{5,9},{6,10},{7,11},{8,4},{9,5},... | collective-permute-start | bytes 786440 | tf_op jit(solution)/shard_map/ppermute | solution.py:257
  21.0 12.5 %collective-permute-start.3 = (bf16[32,4096]{1,0:T(8,128)(2,1)S(1)}, bf16[32,4096]{1,0:T(8,128)(2,1)S(1)}, u32[]{:S(2)}, u32[]{:S(2)}) collective-permute-start(bf16[32,4096]{1,0:T(8,128)(2,1)S(1)} %collective-permute-done.refs_3_), channel_id=1, source_target_pairs={{0,2},{1,3},{2,0},{3,1},{4,6},{5,7},{6,4},{7,5},{8,10},{9,11},{10,... | collective-permute-start | bytes 786440 | tf_op jit(solution)/shard_map/ppermute | solution.py:257
  23.7 11.3 %collective-permute-start.8 = (bf16[32,4096]{1,0:T(8,128)(2,1)S(1)}, bf16[32,4096]{1,0:T(8,128)(2,1)S(1)}, u32[]{:S(2)}, u32[]{:S(2)}) collective-permute-start(bf16[32,4096]{1,0:T(8,128)(2,1)S(1)} %collective-permute-done.1.refs_1_), channel_id=1, source_target_pairs={{0,16},{1,17},{2,18},{3,19},{4,20},{5,21},{6,22},{7,23},{8,24},{9,... | collective-permute-start | bytes 786440 | tf_op jit(solution)/shard_map/ppermute | solution.py:257
  26.6 8.4 %collective-permute-start.15 = (bf16[32,4096]{1,0:T(8,128)(2,1)S(1)}, bf16[32,4096]{1,0:T(8,128)(2,1)S(1)}, u32[]{:S(2)}, u32[]{:S(2)}) collective-permute-start(bf16[32,4096]{1,0:T(8,128)(2,1)S(1)} %collective-permute-done.14.refs_3_), channel_id=1, source_target_pairs={{0,2},{1,3},{2,0},{3,1},{4,6},{5,7},{6,4},{7,5},{8,10},{9,11},{10,... | collective-permute-start | bytes 786440 | tf_op jit(solution)/shard_map/ppermute | solution.py:257
  28.1 8.8 %collective-permute-start.12 = (bf16[32,4096]{1,0:T(8,128)(2,1)S(1)}, bf16[32,4096]{1,0:T(8,128)(2,1)S(1)}, u32[]{:S(2)}, u32[]{:S(2)}) collective-permute-start(bf16[32,4096]{1,0:T(8,128)(2,1)S(1)} %collective-permute-done.refs_3_), channel_id=1, source_target_pairs={{0,16},{1,17},{2,18},{3,19},{4,20},{5,21},{6,22},{7,23},{8,24},{9,... | collective-permute-start | bytes 786440 | tf_op jit(solution)/shard_map/ppermute | solution.py:257
  30.2 7.6 %collective-permute-start.11 = (bf16[32,4096]{1,0:T(8,128)(2,1)S(1)}, bf16[32,4096]{1,0:T(8,128)(2,1)S(1)}, u32[]{:S(2)}, u32[]{:S(2)}) collective-permute-start(bf16[32,4096]{1,0:T(8,128)(2,1)S(1)} %collective-permute-done.10.refs_4_), channel_id=1, source_target_pairs={{0,4},{1,5},{2,6},{3,7},{4,0},{5,1},{6,2},{7,3},{8,12},{9,13},{10,... | collective-permute-start | bytes 786440 | tf_op jit(solution)/shard_map/ppermute | solution.py:257
  33.5 6.4 %collective-permute-start.6 = (bf16[32,4096]{1,0:T(8,128)(2,1)S(1)}, bf16[32,4096]{1,0:T(8,128)(2,1)S(1)}, u32[]{:S(2)}, u32[]{:S(2)}) collective-permute-start(bf16[32,4096]{1,0:T(8,128)(2,1)S(1)} %collective-permute-done.5.refs_3_), channel_id=1, source_target_pairs={{0,2},{1,3},{2,0},{3,1},{4,6},{5,7},{6,4},{7,5},{8,10},{9,11},{10,... | collective-permute-start | bytes 786440 | tf_op jit(solution)/shard_map/ppermute | solution.py:257
  36.8 7.6 %copy-start = (bf16[1,32,4096]{2,1,0:T(8,128)(2,1)S(1)}, bf16[1,32,4096]{2,1,0:T(8,128)(2,1)}, u32[]{:S(2)}) copy-start(bf16[1,32,4096]{2,1,0:T(8,128)(2,1)} %param.4) | copy-start | bytes 786436
  39.9 1.9 %collective-permute-start.16 = (f32[128,1024]{1,0:T(8,128)S(1)}, f32[128,1024]{1,0:T(8,128)S(1)}, u32[]{:S(2)}, u32[]{:S(2)}) collective-permute-start(f32[128,1024]{1,0:T(8,128)S(1)} %get-tuple-element.22), channel_id=1, source_target_pairs={{0,1},{1,0},{2,3},{3,2},{4,5},{5,4},{6,7},{7,6},{8,9},{9,8},{10,11... | collective-permute-start | bytes 1572872 | tf_op jit(solution)/shard_map/ppermute | solution.py:257
  39.9 8.7 %collective-permute-start.2 = (bf16[32,4096]{1,0:T(8,128)(2,1)S(1)}, bf16[32,4096]{1,0:T(8,128)(2,1)S(1)}, u32[]{:S(2)}, u32[]{:S(2)}) collective-permute-start(bf16[32,4096]{1,0:T(8,128)(2,1)S(1)} %collective-permute-done.1.refs_1_), channel_id=1, source_target_pairs={{0,2},{1,3},{2,0},{3,1},{4,6},{5,7},{6,4},{7,5},{8,10},{9,11},{10,... | collective-permute-start | bytes 786440 | tf_op jit(solution)/shard_map/ppermute | solution.py:257
  42.8 8.5 %collective-permute-start.17 = (bf16[1040,128]{1,0:T(8,128)(2,1)S(1)}, bf16[1040,128]{1,0:T(8,128)(2,1)S(1)}, u32[]{:S(2)}, u32[]{:S(2)}) collective-permute-start(bf16[1040,128]{1,0:T(8,128)(2,1)S(1)} %shard_map.51), channel_id=1, source_target_pairs={{0,16},{1,17},{2,18},{3,19},{4,20},{5,21},{6,22},{7,23},{8,24},{9,... | collective-permute-start | bytes 798728 | tf_op jit(solution)/shard_map/ppermute | solution.py:257
  50.4 2.0 %collective-permute-start.7 = (f32[128,1024]{1,0:T(8,128)S(1)}, f32[128,1024]{1,0:T(8,128)S(1)}, u32[]{:S(2)}, u32[]{:S(2)}) collective-permute-start(f32[128,1024]{1,0:T(8,128)S(1)} %get-tuple-element.17), channel_id=1, source_target_pairs={{0,1},{1,0},{2,3},{3,2},{4,5},{5,4},{6,7},{7,6},{8,9},{9,8},{10,11... | collective-permute-start | bytes 1572872 | tf_op jit(solution)/shard_map/ppermute | solution.py:257
